TPU v7x, 32 devices: a whole 2x2x4 slice. The times are simulated.
32 devices in a mesh: row: 16 (over z, y, core), chan: 2 (over x).
Axes of the slice: x: 2, y: 2, z: 4, core: 2. Of those that a mesh axis runs over, the one named last changes fastest.
Arguments:
- pair: float32 [128, 32, 32], P('chan', 'row'), may hold values from -6 to 6
- in_gain: float32 [128], replicated, may hold values from 0.1 to 1.9
- output_gain: float32 [128], P('chan'), may hold values from 0.1 to 1.9
- w_edges: float32 [4, 128, 128], P(None, None, 'chan'), may hold values from -0.5 to 0.5
- w_gate: float32 [128, 128], P(None, 'chan'), may hold values from -0.5 to 0.5
- w_out: float32 [128, 128], P('chan'), may hold values from -0.5 to 0.5
- cotangent: float32 [128, 32, 32], P('chan', 'row'), may hold values from -6 to 6
Outputs:
- update: float32 [128, 32, 32], P('chan', 'row')
- d_pair: float32 [128, 32, 32], P('chan', 'row')
- d_in_gain: float32 [128], P('chan')
- d_out_gain: float32 [128], P('chan')
- d_edges: float32 [4, 128, 128], P(None, None, 'chan')
- d_gate: float32 [128, 128], P(None, 'chan')
- d_out: float32 [128, 128], P('chan')
All inputs are finite; a program needn't handle non-finite values.
Results may differ from a plain program's by a relative error of at most 0.00019.
Values sent between devices are 32-bit elements; how exact they have to be, the bound alone decides.
No kernel may reach another device: no remote copies, remote signals or barrier semaphores. Data moves between devices by JAX's collectives and lax.ppermute only.
A program may use at most 64 MiB of HBM per device.

v0:
```python
import jax
import jax.numpy as jnp
from jax import lax
from jax.sharding import PartitionSpec as P

HIDDEN_WIDTH = 128


def shards(pair, in_gain, output_gain, w_edges, w_gate, w_out, cotangent):
    hp = lax.Precision.HIGHEST
    shard_c = pair.shape[0]
    whole = lax.all_gather(pair, "chan", axis=0, tiled=True)
    centred = whole - jnp.mean(whole, 0)
    pair_rstd = lax.rsqrt(jnp.mean(centred * centred, 0) + 1e-05)
    zhat = centred * pair_rstd
    normed = zhat * in_gain[:, None, None]
    proj = jnp.einsum("ech,crn->ehrn", w_edges, normed, precision=hp)
    left_sig = jax.nn.sigmoid(proj[1])
    left = left_sig * proj[0]
    right_sig = jax.nn.sigmoid(proj[3])
    right = right_sig * proj[2]
    gate = jax.nn.sigmoid(jnp.einsum("dc,drn->crn", w_gate, normed, precision=hp))
    right_all = lax.all_gather(right, "row", axis=1, tiled=True)
    triangle_product = jnp.einsum("hrk,hjk->hrj", left, right_all, precision=hp)
    first, second = lax.psum(
        (jnp.sum(triangle_product, 0), jnp.sum(triangle_product * triangle_product, 0)), "chan"
    )
    hidden_average = first / HIDDEN_WIDTH
    hidden_inverse_deviation = lax.rsqrt(
        second / HIDDEN_WIDTH - hidden_average * hidden_average + 1e-05
    )
    normalized_hidden = (triangle_product - hidden_average) * hidden_inverse_deviation
    hidden_state = normalized_hidden * output_gain[:, None, None]
    mixed = lax.psum_scatter(
        jnp.einsum("hc,hrn->crn", w_out, hidden_state, precision=hp),
        "chan",
        scatter_dimension=0,
        tiled=True,
    )
    update = gate * mixed
    d_mixed = cotangent * gate
    d_gate_pre = cotangent * mixed * gate * (1.0 - gate)
    d_mixed_all = lax.all_gather(d_mixed, "chan", axis=0, tiled=True)
    hidden_gradient = jnp.einsum("hc,crn->hrn", w_out, d_mixed_all, precision=hp)
    g_out = jnp.einsum("hrn,crn->hc", hidden_state, d_mixed_all, precision=hp)
    output_gain_gradient = jnp.sum(normalized_hidden * hidden_gradient, (1, 2))
    normalized_gradient = hidden_gradient * output_gain[:, None, None]
    first_average_term, second_average_term = lax.psum(
        (jnp.sum(normalized_gradient, 0), jnp.sum(normalized_gradient * normalized_hidden, 0)),
        "chan",
    )
    triangle_gradient = hidden_inverse_deviation * (
        normalized_gradient
        - first_average_term / HIDDEN_WIDTH
        - normalized_hidden * (second_average_term / HIDDEN_WIDTH)
    )
    d_tri_cols = lax.all_to_all(triangle_gradient, "row", split_axis=2, concat_axis=1, tiled=True)
    d_left = jnp.einsum("hrj,hjk->hrk", triangle_gradient, right_all, precision=hp)
    d_right = jnp.einsum(
        "hij,hik->hjk", d_tri_cols, lax.all_gather(left, "row", axis=1, tiled=True), precision=hp
    )
    d_proj = jnp.stack(
        [
            d_left * left_sig,
            d_left * proj[0] * left_sig * (1.0 - left_sig),
            d_right * right_sig,
            d_right * proj[2] * right_sig * (1.0 - right_sig),
        ]
    )
    g_edges = jnp.einsum("crn,ehrn->ech", normed, d_proj, precision=hp)
    g_gate = jnp.einsum("drn,crn->dc", normed, d_gate_pre, precision=hp)
    offset = lax.axis_index("chan") * shard_c
    first_part = jnp.einsum("ech,ehrn->crn", w_edges, d_proj, precision=hp)
    d_normed = lax.psum(
        first_part + jnp.einsum("dc,crn->drn", w_gate, d_gate_pre, precision=hp), "chan"
    )
    d_zhat = d_normed * in_gain[:, None, None]
    first_mean = jnp.mean(d_zhat, 0)
    second_mean = jnp.mean(d_zhat * zhat, 0)
    d_full = pair_rstd * (d_zhat - first_mean - zhat * second_mean)
    d_pair = lax.dynamic_slice_in_dim(d_full, offset, shard_c, 0)
    g_in_gain = lax.dynamic_slice_in_dim(jnp.sum(zhat * d_normed, (1, 2)), offset, shard_c, 0)
    totals = lax.psum((g_in_gain, output_gain_gradient, g_edges, g_gate, g_out), "row")
    return (update, d_pair, totals[0], totals[1], totals[2], totals[3], totals[4])


def solution(mesh):
    placed = (
        P("chan", "row", None),
        P(),
        P("chan"),
        P(None, None, "chan"),
        P(None, "chan"),
        P("chan", None),
        P("chan", "row", None),
    )
    return jax.shard_map(
        shards,
        mesh=mesh,
        in_specs=placed,
        out_specs=(
            P("chan", "row", None),
            P("chan", "row", None),
            P("chan"),
            P("chan"),
            P(None, None, "chan"),
            P(None, "chan"),
            P("chan", None),
        ),
        check_vma=False,
    )
```

profile of v0, /device:TPU:0, one launch (start us, length us, event | category | flops | bytes accessed | tf_op | source)
XLA Modules:
  0.0 283.8 jit_solution(18326567018283969467)
XLA Ops:
  8.1 0.9 copy.44
  8.9 5.8 %all_gather.12 = f32[128,2,32]{2,1,0:T(2,128)S(1)} all-gather(f32[64,2,32]{2,1,0:T(2,128)S(1)} %copy.44), channel_id=1, replica_groups=mesh['row'=16,'chan'=2] {'chan'}, dimensions={0}, use_global_device_ids=true | all-gather | bytes 49152 | tf_op jit(solution)/shard_map/all_gather | solution.py:12
  15.3 0.7 copy-done.1
  16.3 4.9 %all_gather.14 = f32[128,2,32]{2,1,0:T(2,128)S(1)} all-gather(f32[64,2,32]{2,1,0:T(2,128)S(1)} %copy.50), channel_id=1, replica_groups=mesh['row'=16,'chan'=2] {'chan'}, dimensions={0}, use_global_device_ids=true | all-gather | bytes 49152 | tf_op jit(solution)/shard_map/all_gather | solution.py:43
  21.3 0.7 copy-done.2
  22.9 23.8 %all_gather.13 = f32[64,32,32]{0,2,1:T(8,128)S(1)} all-gather(f32[64,2,32]{0,2,1:T(8,128)S(1)} %get-tuple-element.30), channel_id=1, replica_groups=mesh['row'=16,'chan'=2] {'row'}, dimensions={1}, use_global_device_ids=true | all-gather | bytes 278528 | tf_op jit(solution)/shard_map/all_gather | solution.py:23
  46.7 0.9 copy.48
  47.6 1.8 fusion.39
  49.4 4.9 %all-reduce.2 = (f32[2,32]{1,0:T(2,128)S(1)}, f32[2,32]{1,0:T(2,128)S(1)}) all-reduce(f32[2,32]{1,0:T(2,128)S(1)} %get-tuple-element.11, f32[2,32]{1,0:T(2,128)S(1)} %get-tuple-element.10), channel_id=1, replica_groups=mesh['row'=16,'chan'=2] {'chan'}, use_global_device_ids=true, to_apply=%region_5.0 | all-reduce | flops 128 | bytes 1024 | tf_op jit(solution)/shard_map/psum | solution.py:25
  54.4 0.7 copy-done.7
  55.0 1.1 fusion.7
  56.1 4.9 %all-reduce.1 = (f32[2,32]{1,0:T(2,128)S(1)}, f32[2,32]{1,0:T(2,128)S(1)}) all-reduce(f32[2,32]{1,0:T(2,128)S(1)} %get-tuple-element.8, f32[2,32]{1,0:T(2,128)S(1)} %get-tuple-element.9), channel_id=1, replica_groups=mesh['row'=16,'chan'=2] {'chan'}, use_global_device_ids=true, to_apply=%region_10.0 | all-reduce | flops 128 | bytes 1024 | tf_op jit(solution)/shard_map/psum | solution.py:48
  61.4 0.7 copy.70
  62.2 0.7 reshape.56
  62.9 3.5 %all-to-all-start = ((f32[16,1,256]{2,1,0:T(1,128)}), f32[16,1,256]{2,1,0:T(1,128)S(1)}, u32[]{:S(2)}, u32[]{:S(2)}) async-start(f32[16,1,256]{2,1,0:T(1,128)} %reshape.56), calls=%async_computation | async-start | bytes 32768 | tf_op jit(solution)/shard_map/all_to_all | solution.py:57
  66.5 0.9 fusion.41
  67.5 23.2 %all_gather.15 = f32[64,32,32]{0,2,1:T(8,128)S(1)} all-gather(f32[64,2,32]{0,2,1:T(8,128)S(1)} %get-tuple-element.31), channel_id=1, replica_groups=mesh['row'=16,'chan'=2] {'row'}, dimensions={1}, use_global_device_ids=true | all-gather | bytes 278528 | tf_op jit(solution)/shard_map/all_gather | solution.py:60
  90.7 0.9 convolution_bitcast_fusion.2
  91.6 0.9 copy.60
  93.1 0.7 reduce
  94.0 1.0 fusion.42
  95.4 1.0 convolution_bitcast_fusion
  96.5 0.8 copy.71
  97.5 8.4 %psum.74 = f32[128,2,32]{0,2,1:T(8,128)S(1)} all-reduce(f32[128,2,32]{0,2,1:T(8,128)S(1)} %fusion), channel_id=1, replica_groups=mesh['row'=16,'chan'=2] {'chan'}, use_global_device_ids=true, to_apply=%region_11.0 | all-reduce | flops 8192 | bytes 65536 | tf_op jit(solution)/shard_map/psum | solution.py:74
  106.7 0.9 convolution_bitcast_fusion.3
  107.5 0.7 fusion.10
  108.3 0.6 mul.154
  108.9 71.6 %all-reduce.6.cloned.1.call-done = f32[4,128,64]{1,2,0:T(8,128)} async-done(((f32[4,128,64]{1,2,0:T(8,128)}), f32[4,128,64]{1,2,0:T(8,128)}) %all-reduce.6.cloned.1.call-update) | async-done | bytes 131088 | tf_op jit(solution)/shard_map/psum | solution.py:83
  180.5 91.1 %all-reduce.8.cloned.1.call-done = (f32[64]{0:T(128)}, f32[64]{0:T(128)}, f32[128,64]{0,1:T(8,128)}, f32[64,128]{1,0:T(8,128)}) async-done(((f32[64]{0:T(128)}, f32[64]{0:T(128)}, f32[128,64]{0,1:T(8,128)}, f32[64,128]{1,0:T(8,128)}), (f32[64]{0:T(128)}, f32[64]{0:T(128)}, f32[128,64]{0,1:T(8,128)}, f32[64,128]{1,0:T(8,128)})) %all-reduce.8.cloned.1.call-update) | async-done | bytes 66064 | tf_op jit(solution)/shard_map/psum | solution.py:83
  271.6 0.7 copy-done.9
  273.4 1.6 copy.79
  274.9 0.6 copy.80
  (61 shorter events, 6.5 us)
Async XLA Ops:
  8.0 14.3 %copy-start = (f32[4,128,64]{1,2,0:T(8,128)S(1)}, f32[4,128,64]{1,2,0:T(8,128)}, u32[]{:S(2)}) copy-start(f32[4,128,64]{1,2,0:T(8,128)} %param.10) | copy-start | bytes 393220
  8.0 88.5 %reduce-scatter.4.cloned.1.call-start = ((), (), s32[]{:S(2)}) async-start(), calls=%async_computation.3 | async-start | bytes 98304
  15.2 0.8 copy-start.1
  15.2 0.8 copy-start.3
  15.2 0.8 copy-start.6
  21.2 0.8 copy-start.2
  54.4 0.7 copy-start.7
  62.9 29.6 %all-to-all-start = ((f32[16,1,256]{2,1,0:T(1,128)}), f32[16,1,256]{2,1,0:T(1,128)S(1)}, u32[]{:S(2)}, u32[]{:S(2)}) async-start(f32[16,1,256]{2,1,0:T(1,128)} %reshape.56), calls=%async_computation | async-start | bytes 32768 | tf_op jit(solution)/shard_map/all_to_all | solution.py:57
  66.5 114.0 %all-reduce.6.cloned.1.call-start = ((), (), s32[]{:S(2)}) async-start(), calls=%async_computation.2 | async-start | bytes 262144 | tf_op jit(solution)/shard_map/psum | solution.py:83
  96.4 175.1 %all-reduce.8.cloned.1.call-start = ((), (), s32[]{:S(2)}) async-start(), calls=%async_computation.4 | async-start | bytes 133120 | tf_op jit(solution)/shard_map/psum | solution.py:83
  271.6 0.7 copy-start.9
  272.2 0.6 copy-start.8
  273.4 1.6 copy-start.5
  274.9 0.8 copy-start.4
Sparse Core Ops, SparseCore 0:
  62.3 7.1 reduce-scatter.3
Sparse Core Ops, SparseCore 1:
  96.5 83.9 all-reduce.5
  184.8 86.7 all-reduce.7
where the time goes:
time: 285 us; the launch traced here: 284 us
  waiting for transfers between devices  163 us (57%)
  blocking collectives  76 us (27%)
  between operations  15.7 us (6%)
  local copies, waits for them, and re-layouts  13.8 us (5%)
  matrix products  7.94 us (3%)
  other arithmetic  3.91 us (1%)
  starting transfers between devices  3.62 us (1%)
    psum x2, waiting for transfers between devices, shards(): lax.psum((g_in_gain, output_gain_gradient, g_edges, g_gate, g_out), 'row')  163 us
    all_gather x1, blocking collectives, shards(): right_all = lax.all_gather(right, 'row', axis=1, tiled=True)  23.8 us
    all_gather x1, blocking collectives, shards(): lax.all_gather(left, 'row', axis=1, tiled=True)  23.2 us
    unnamed x30, local copies, waits for them, and re-layouts  10 us
    psum x1, blocking collectives, shards(): lax.psum(first_part + jnp.einsum('dc,crn->drn', w_gate, d_gate_pre, preci...  8.37 us
    all_gather x1, blocking collectives, shards(): whole = lax.all_gather(pair, 'chan', axis=0, tiled=True)  5.84 us
  transfers between devices with their start and end apart: 4, of which 2 were waited for; matrix products, arithmetic and copies ran while one was open for 4% of the time, Pallas kernels for 0%

commit v1 on v0

--- a/solution.py
+++ b/solution.py
@@ -1,12 +1,20 @@
+import functools
+
 import jax
 import jax.numpy as jnp
 from jax import lax
+from jax.experimental import pallas as pl
+from jax.experimental.pallas import tpu as pltpu
 from jax.sharding import PartitionSpec as P
 
 HIDDEN_WIDTH = 128
-
-
-def shards(pair, in_gain, output_gain, w_edges, w_gate, w_out, cotangent):
+EPS = 1e-05
+F32 = jnp.float32
+BF16 = jnp.bfloat16
+LANES = 128
+
+
+def spread(pair, in_gain, output_gain, w_edges, w_gate, w_out, cotangent):
     hp = lax.Precision.HIGHEST
     shard_c = pair.shape[0]
     whole = lax.all_gather(pair, "chan", axis=0, tiled=True)
@@ -84,7 +92,258 @@
     return (update, d_pair, totals[0], totals[1], totals[2], totals[3], totals[4])
 
 
+def split(x):
+    hi = x.astype(BF16)
+    return hi, (x - hi.astype(F32)).astype(BF16)
+
+
+def dot3(a, b, dims=((1,), (0,))):
+    (ah, al), (bh, bl) = a, b
+    dot = functools.partial(lax.dot_general, dimension_numbers=(dims, ((), ())), preferred_element_type=F32)
+    return dot(ah, bh) + (dot(ah, bl) + dot(al, bh))
+
+
+def mean_lanes(x):
+    return jnp.mean(x, axis=-1, keepdims=True)
+
+
+def norm_lanes(x):
+    centred = x - mean_lanes(x)
+    rstd = lax.rsqrt(mean_lanes(centred * centred) + EPS)
+    return centred * rstd, rstd
+
+
+def prepare_kernel(gain_ref, we, wg, wo, oe, og, oo, wnh, wnl, wth, wtl, woh, wol, wqh, wql):
+    s, c = wg.shape
+    chan = lax.axis_index("chan")
+    gain = gain_ref[...]
+
+    def put(k, both):
+        at = slice(k * c, (k + 1) * c)
+        wnh[at, :], wnl[at, :] = split(both)
+        wth[:, at], wtl[:, at] = split(both.T)
+
+    for e in range(4):
+        put(e, jnp.concatenate([we[e], oe[e * s : (e + 1) * s, :]], axis=0) * gain)
+    own, other = wg[...] * gain, og[...] * gain
+    put(4, jnp.concatenate([jnp.where(chan == 0, own, other), jnp.where(chan == 0, other, own)], axis=0))
+    both = jnp.concatenate([wo[...], oo[...]], axis=0)
+    woh[...], wol[...] = split(both)
+    wqh[...], wql[...] = split(both.T)
+
+
+def prepare(gain, w_e, w_g, w_o, other):
+    s, c = w_g.shape
+    vm = pl.BlockSpec(memory_space=pltpu.VMEM)
+    shapes = [(5 * c, c)] * 2 + [(c, 5 * c)] * 2 + [(c, c)] * 4
+    return pl.pallas_call(
+        prepare_kernel,
+        out_shape=[jax.ShapeDtypeStruct(x, BF16) for x in shapes],
+        in_specs=[vm] * 7,
+        out_specs=[vm] * 8,
+        compiler_params=pltpu.CompilerParams(vmem_limit_bytes=8 << 20),
+        name="prepare",
+    )(gain, w_e, w_g, w_o, *other)
+
+
+def products(n, rows, x_row, y_ref):
+    acc = [jnp.zeros((n // 8, 8, LANES), F32) for _ in range(rows)]
+    for m in range(n):
+        y = y_ref[m * n : (m + 1) * n, :].reshape(n // 8, 8, LANES)
+        for a in range(rows):
+            acc[a] = acc[a] + x_row(a, m)[None] * y
+    return jnp.concatenate([part.reshape(n, LANES) for part in acc], axis=0)
+
+
+def update_kernel(
+    n, x_ref, y_ref, gain_ref, out_gain_ref, we, wg, oe, og, wnh, wnl, wth, wtl, woh, wol, wqh, wql,
+    up_ref, dp_ref, dig_ref, dog_ref, de_ref, dg_ref, do_ref,
+    ct, zh, zl, left, s1, right, s3, right_t, gate, upd, xh, xl, mh, ml, dtri, dgp, dh, dl, zown, rown, grads,
+):
+    c, s = LANES, LANES // 2
+    blk = up_ref.shape[0]
+    q = blk // n
+    upper = x_ref.shape[0] // (4 * blk)
+    row, chan = lax.axis_index("row"), lax.axis_index("chan")
+    zy, core = row // 2, row % 2
+    rows = 4
+    cells = rows * n
+    low = lax.broadcasted_iota(jnp.int32, (blk, c), 1) < s
+
+    def project(t, carry):
+        zpos, ypos = t % upper, t // upper
+        base = (zpos + upper * 2 * ypos) * blk
+        first_at = pl.multiple_of(base + upper * blk * chan, blk)
+        second_at = pl.multiple_of(base + upper * blk * (1 - chan), blk)
+        target = zy ^ (zpos * 2 + ypos)
+        pair, places = [], []
+        for k, ref in enumerate((x_ref, y_ref)):
+            first, second = ref[pl.ds(first_at, blk), :], ref[pl.ds(second_at, blk), :]
+            pair.append(jnp.where(low, first, pltpu.roll(second, s, 1)))
+            at = pl.multiple_of((target * 2 + (core ^ k)) * blk, blk)
+            places.append(at)
+            ct[pl.ds(at, blk), :] = jnp.where(low, pltpu.roll(first, s, 1), second)
+        zhat, rstd = norm_lanes(jnp.concatenate(pair, axis=0))
+        z = split(zhat)
+
+        @pl.when(t == 0)
+        def _():
+            zown[...] = zhat[:blk]
+            rown[...] = jnp.broadcast_to(rstd[:blk], (blk, c))
+
+        proj = dot3(z, (wth[...], wtl[...]))
+        sl = jax.nn.sigmoid(proj[:, c : 2 * c])
+        le = sl * proj[:, :c]
+        sr = jax.nn.sigmoid(proj[:, 3 * c : 4 * c])
+        ri = sr * proj[:, 2 * c : 3 * c]
+        ga = jax.nn.sigmoid(proj[:, 4 * c :])
+        for k in range(2):
+            here, part = pl.ds(places[k], blk), slice(k * blk, (k + 1) * blk)
+            zh[here, :], zl[here, :] = z[0][part], z[1][part]
+            left[here, :], s1[here, :] = le[part], sl[part]
+            right[here, :], s3[here, :] = ri[part], sr[part]
+            gate[here, :] = ga[part]
+            for r in range(q):
+                at = k * blk + r * n
+                right_t[pl.ds(places[k] // n + r, n, stride=n), :] = ri[at : at + n]
+        return carry
+
+    lax.fori_loop(0, 2 * upper, project, 0)
+
+    def row_of(ref, at):
+        return ref[pl.ds(at, 8, stride=0), :]
+
+    def triangle(b, total):
+        r0 = pl.multiple_of(b * cells, cells)
+        here = pl.ds(r0, cells)
+        tri = products(n, rows, lambda a, m: row_of(left, r0 + a * n + m), right_t)
+        xhat, rstd = norm_lanes(tri)
+        x = split(xhat * out_gain_ref[...])
+        xh[here, :], xl[here, :] = x
+        mixed = dot3(x, (woh[...], wol[...]))
+        ga = gate[here, :]
+        upd[here, :] = ga * mixed
+        dm = ct[here, :] * ga
+        m = split(dm)
+        mh[here, :], ml[here, :] = m
+        dgp[here, :] = dm * mixed * (1.0 - ga)
+        hidden = dot3(m, (wqh[...], wql[...]))
+        ng = hidden * out_gain_ref[...]
+        dtri[here, :] = rstd * (ng - mean_lanes(ng) - xhat * mean_lanes(ng * xhat))
+        return total + jnp.sum(xhat * hidden, axis=0, keepdims=True)
+
+    total = lax.fori_loop(0, n // rows, triangle, jnp.zeros((1, c), F32))
+    dog_ref[...] = total[:, :s]
+
+    def gradients(b, carry):
+        r0 = pl.multiple_of(b * cells, cells)
+        here = pl.ds(r0, cells)
+        dle = products(n, rows, lambda a, m: row_of(dtri, r0 + a * n + m), right)
+        a = s1[here, :]
+        dh[here, :c], dl[here, :c] = split(dle * a)
+        dh[here, c : 2 * c], dl[here, c : 2 * c] = split(dle * left[here, :] * (1.0 - a))
+        dri = products(n, rows, lambda a, m: row_of(dtri, m * n + b * rows + a), left)
+        a = s3[here, :]
+        dh[here, 2 * c : 3 * c], dl[here, 2 * c : 3 * c] = split(dri * a)
+        dh[here, 3 * c : 4 * c], dl[here, 3 * c : 4 * c] = split(dri * right[here, :] * (1.0 - a))
+        dh[here, 4 * c :], dl[here, 4 * c :] = split(dgp[here, :])
+        return carry
+
+    lax.fori_loop(0, n // rows, gradients, 0)
+
+    down = ((0,), (0,))
+    grads[...] = dot3((dh[...], dl[...]), (zh[...], zl[...]), down)
+    do_ref[...] = dot3((xh[:, :s], xl[:, :s]), (mh[...], ml[...]), down)
+
+    gain = gain_ref[...]
+    mine = pl.ds(pl.multiple_of(4 * c + s * chan, s), s)
+    others = pl.ds(pl.multiple_of(4 * c + s * (1 - chan), s), s)
+    dg_ref[...] = grads[mine, :] * gain
+    weighted = wg[...] * grads[mine, :] + og[...] * grads[others, :]
+    for e in range(4):
+        mine, others = grads[e * c : e * c + s, :], grads[e * c + s : (e + 1) * c, :]
+        de_ref[e] = mine * gain
+        weighted = weighted + we[e] * mine + oe[e * s : (e + 1) * s, :] * others
+    d_gain = jnp.sum(weighted, axis=0, keepdims=True)
+
+    def half(x):
+        return jnp.where(chan == 0, x[:, :s], pltpu.roll(x, s, 1)[:, :s])
+
+    dig_ref[...] = half(jnp.broadcast_to(d_gain, (8, c)))[:1]
+    here = pl.ds(pl.multiple_of(row * blk, blk), blk)
+    up_ref[...] = half(upd[here, :])
+    dz = dot3((dh[here, :], dl[here, :]), (wnh[...], wnl[...]))
+    zhat = zown[...]
+    dp_ref[...] = half(rown[...] * (dz - mean_lanes(dz) - zhat * mean_lanes(dz * zhat)))
+
+
+def whole_update(n, blk, x, y, gain, out_gain, w_e, w_g, other, ready):
+    c, s = LANES, LANES // 2
+    vm = pl.BlockSpec(memory_space=pltpu.VMEM)
+    cells = n * n
+    out = [(blk, s), (blk, s), (1, s), (1, s), (4, s, c), (s, c), (s, c)]
+    full, half = pltpu.VMEM((cells, c), F32), pltpu.VMEM((cells, c), BF16)
+    scratch = (
+        [full, half, half] + [full] * 7 + [half] * 4 + [full] * 2
+        + [pltpu.VMEM((cells, 5 * c), BF16)] * 2 + [pltpu.VMEM((blk, c), F32)] * 2 + [pltpu.VMEM((5 * c, c), F32)]
+    )
+    return pl.pallas_call(
+        functools.partial(update_kernel, n),
+        out_shape=[jax.ShapeDtypeStruct(shape, F32) for shape in out],
+        in_specs=[vm] * 16,
+        out_specs=[vm] * 7,
+        scratch_shapes=scratch,
+        compiler_params=pltpu.CompilerParams(vmem_limit_bytes=32 << 20),
+        name="whole_update",
+    )(x, y, gain, out_gain, w_e, w_g, *other, *ready)
+
+
+def gathered(devices, pair, in_gain, output_gain, w_edges, w_gate, w_out, cotangent):
+    s, q, n = pair.shape
+    c = 2 * s
+    blk = q * n
+
+    def swap(x, bits):
+        return lax.ppermute(x, ("row", "chan"), [(i, i ^ bits) for i in range(devices)])
+
+    def cells_of(x):
+        return jnp.transpose(x, (1, 2, 0)).reshape(blk, s)
+
+    w_e = jnp.transpose(w_edges, (0, 2, 1))
+    w_g = jnp.transpose(w_gate)
+    held = jnp.concatenate([cells_of(pair), cells_of(cotangent)], axis=1)
+    mine = jnp.concatenate([w_e.reshape(4 * s, c), w_g, w_out, jnp.pad(output_gain[None], ((0, 7), (0, s)))])
+    bits = 8
+    while bits < devices:
+        held = jnp.concatenate([held, swap(held, bits)])
+        bits *= 2
+    theirs = swap(mine, 1)
+    held = jnp.concatenate([held, swap(held, 1), swap(held, 4), swap(held, 5)])
+    beside = swap(held, 2)
+    o_e, o_g, o_o = theirs[: 4 * s], theirs[4 * s : 5 * s], theirs[5 * s : 6 * s]
+    gain = in_gain[None]
+    out_gain = jnp.concatenate([output_gain[None], theirs[6 * s : 6 * s + 1, :s]], axis=1)
+    ready = prepare(gain, w_e, w_g, w_out, (o_e, o_g, o_o))
+    up, dp, dig, dog, de, dg, do = whole_update(n, blk, held, beside, gain, out_gain, w_e, w_g, (o_e, o_g), ready)
+
+    def pair_of(x):
+        return jnp.transpose(x.reshape(q, n, s), (2, 0, 1))
+
+    return (pair_of(up), pair_of(dp), dig[0], dog[0], jnp.transpose(de, (0, 2, 1)), jnp.transpose(dg), do)
+
+
 def solution(mesh):
+    devices, chans = mesh.size, mesh.shape["chan"]
+
+    def shards(pair, in_gain, output_gain, w_edges, *rest):
+        n, c = pair.shape[2], w_edges.shape[1]
+        fits = (
+            chans == 2 and devices >= 8 and devices & (devices - 1) == 0 and n <= 32 and n % 8 == 0
+            and c == LANES and w_edges.shape[2] * chans == LANES and (pair.shape[1] * n) % 16 == 0
+        )
+        step = functools.partial(gathered, devices) if fits else spread
+        return step(pair, in_gain, output_gain, w_edges, *rest)
+
     placed = (
         P("chan", "row", None),
         P(),
@@ -98,14 +357,6 @@
         shards,
         mesh=mesh,
         in_specs=placed,
-        out_specs=(
-            P("chan", "row", None),
-            P("chan", "row", None),
-            P("chan"),
-            P("chan"),
-            P(None, None, "chan"),
-            P(None, "chan"),
-            P("chan", None),
-        ),
+        out_specs=(placed[0], placed[0], P("chan"), P("chan"), placed[3], placed[4], placed[5]),
         check_vma=False,
     )

time: 285 us -> 40.7 us (0.14)
  waiting for transfers between devices: 163 us -> 9.59 us
  blocking collectives: 76 us -> 0 us
  Pallas kernels: 0 us -> 16.4 us
  between operations: 15.7 us -> 0.75 us
  local copies, waits for them, and re-layouts: 13.8 us -> 1.38 us
  matrix products: 7.94 us -> 0 us
  starting transfers between devices: 3.62 us -> 11.3 us
    psum x2 -> x0, waiting for transfers between devices: 163 us -> none  [shards(): lax.psum((g_in_gain, output_gain_gradient, g_edges, g_gate, g_out), 'row')]
    all_gather x4 -> x0, blocking collectives: 57.8 us -> none  [the longest x1 23.8 us: shards(): right_all = lax.all_gather(right, 'row', axis=1, tiled=True)]
    psum x3 -> x0, blocking collectives: 18.2 us -> none  [the longest x1 8.37 us: shards(): lax.psum(first_part + jnp.einsum('dc,crn->drn', w_gate, d_gate_pre, preci...]
    pallas_call x0 -> x2, Pallas kernels: none -> 16.4 us  [the longest x1 16.2 us: whole_update(): pl.pallas_call(functools.partial(update_kernel, n), out_shape=[jax.ShapeD...]
    ppermute x0 -> x7, starting transfers between devices: none -> 11.3 us  [swap(): lax.ppermute(x, ('row', 'chan'), [(i, i ^ bits) for i in range(devices)])]
    ppermute x0 -> x7, waiting for transfers between devices: none -> 9.59 us  [swap(): lax.ppermute(x, ('row', 'chan'), [(i, i ^ bits) for i in range(devices)])]
    unnamed x30 -> x18, local copies, waits for them, and re-layouts: 10 us -> 1.35 us
    dot_general x12 -> x0, matrix products: 7.94 us -> none  [the longest x1 1.77 us: shards(): triangle_product = jnp.einsum('hrk,hjk->hrj', left, right_all, precision=hp)]
  transfers between devices with their start and end apart: 4 -> 7, of which waited for: 2 -> 5; matrix products, arithmetic and copies ran while one was open for 4% -> 1% of each run, Pallas kernels for 0% -> 0%
where the time goes in v1:
time: 40.7 us; the launch traced here: 40.5 us
  Pallas kernels  16.4 us (40%)
  starting transfers between devices  11.3 us (28%)
  waiting for transfers between devices  9.59 us (24%)
  local copies, waits for them, and re-layouts  1.38 us (3%)
  other arithmetic  1.14 us (3%)
  between operations  0.75 us (2%)
    pallas_call x1, Pallas kernels, whole_update(): pl.pallas_call(functools.partial(update_kernel, n), out_shape=[jax.ShapeD...  16.2 us
    ppermute x7, starting transfers between devices, swap(): lax.ppermute(x, ('row', 'chan'), [(i, i ^ bits) for i in range(devices)])  11.3 us
    ppermute x7, waiting for transfers between devices, swap(): lax.ppermute(x, ('row', 'chan'), [(i, i ^ bits) for i in range(devices)])  9.59 us
    unnamed x18, local copies, waits for them, and re-layouts  1.35 us
    unnamed x1, other arithmetic  0.89 us
  transfers between devices with their start and end apart: 7, of which 5 were waited for; matrix products, arithmetic and copies ran while one was open for 1% of the time, Pallas kernels for 0%

profile of v1, /device:TPU:0, one launch (start us, length us, event | category | flops | bytes accessed | tf_op | source)
XLA Modules:
  0.0 40.5 jit_solution(14538630451671534758)
XLA Ops:
  0.6 0.0 copy-start.4
  0.6 0.0 copy-start.5
  0.7 0.0 copy-start
  0.7 0.9 %constant_dynamic-update-slice_fusion.5 = (f32[1024,128]{1,0:T(8,128)S(1)}, f32[64,128]{1,0:T(8,128)S(1)}) fusion(f32[64,64]{1,0:T(8,128)} %bitcast.30, f32[64,64]{1,0:T(8,128)} %bitcast.33), kind=kLoop, calls=%fused_computation.10 | loop fusion | flops 8191 | bytes 98304
  1.6 0.0 copy-start.2
  1.6 3.1 %collective-permute-start = (f32[64,128]{1,0:T(8,128)S(1)}, f32[64,128]{1,0:T(8,128)S(1)}, u32[]{:S(2)}, u32[]{:S(2)}) collective-permute-start(f32[64,128]{1,0:T(8,128)S(1)} %get-tuple-element.38), channel_id=1, source_target_pairs={{0,8},{1,9},{2,10},{3,11},{4,12},{5,13},{6,14},{7,15},{8,0},{9,1},... | collective-permute-start | bytes 98312 | tf_op jit(solution)/shard_map/ppermute | solution.py:307
  4.7 1.9 %collective-permute-done = f32[64,128]{1,0:T(8,128)S(1)} collective-permute-done((f32[64,128]{1,0:T(8,128)S(1)}, f32[64,128]{1,0:T(8,128)S(1)}, u32[]{:S(2)}, u32[]{:S(2)}) %collective-permute-start) | collective-permute-done | bytes 32800 | tf_op jit(solution)/shard_map/ppermute | solution.py:307
  6.6 0.0 copy-done.4
  6.6 0.0 copy-done.5
  6.6 0.1 pad_maximum_fusion.1
  6.6 3.0 %collective-permute-start.1 = (f32[128,128]{1,0:T(8,128)S(1)}, f32[128,128]{1,0:T(8,128)S(1)}, u32[]{:S(2)}, u32[]{:S(2)}) collective-permute-start(f32[128,128]{1,0:T(8,128)S(1)} %pad_maximum_fusion.1), channel_id=1, source_target_pairs={{0,16},{1,17},{2,18},{3,19},{4,20},{5,21},{6,22},{7,23},{8,24},{9,... | collective-permute-start | bytes 196616 | tf_op jit(solution)/shard_map/ppermute | solution.py:307
  9.7 0.0 copy-done
  9.7 0.0 copy-done.1
  9.7 0.0 copy-done.2
  9.7 0.6 %copy-done.6 = f32[64]{0:T(128)S(1)} copy-done((f32[64]{0:T(128)S(1)}, f32[64]{0:T(128)}, u32[]{:S(2)}) %copy-start.6) | copy-done | bytes 280
  10.4 1.6 %collective-permute-start.6 = (f32[392,128]{1,0:T(8,128)S(1)}, f32[392,128]{1,0:T(8,128)S(1)}, u32[]{:S(2)}, u32[]{:S(2)}) collective-permute-start(f32[392,128]{1,0:T(8,128)S(1)} %select_maximum_fusion), channel_id=1, source_target_pairs={{0,1},{1,0},{2,3},{3,2},{4,5},{5,4},{6,7},{7,6},{8,9},{9,8},{10,11... | collective-permute-start | bytes 602120 | tf_op jit(solution)/shard_map/ppermute | solution.py:307
  11.9 0.0 collective-permute-done.1
  11.9 0.1 pad_maximum_fusion
  12.0 1.8 %collective-permute-start.2 = (f32[256,128]{1,0:T(8,128)S(1)}, f32[256,128]{1,0:T(8,128)S(1)}, u32[]{:S(2)}, u32[]{:S(2)}) collective-permute-start(f32[256,128]{1,0:T(8,128)S(1)} %pad_maximum_fusion), channel_id=1, source_target_pairs={{0,1},{1,0},{2,3},{3,2},{4,5},{5,4},{6,7},{7,6},{8,9},{9,8},{10,11... | collective-permute-start | bytes 393224 | tf_op jit(solution)/shard_map/ppermute | solution.py:307
  13.8 1.5 %collective-permute-start.4 = (f32[256,128]{1,0:T(8,128)S(1)}, f32[256,128]{1,0:T(8,128)S(1)}, u32[]{:S(2)}, u32[]{:S(2)}) collective-permute-start(f32[256,128]{1,0:T(8,128)S(1)} %pad_maximum_fusion), channel_id=1, source_target_pairs={{0,5},{1,4},{2,7},{3,6},{4,1},{5,0},{6,3},{7,2},{8,13},{9,12},{10,... | collective-permute-start | bytes 393224 | tf_op jit(solution)/shard_map/ppermute | solution.py:307
  15.3 0.2 collective-permute-start.3
  15.5 4.4 %collective-permute-done.2 = f32[256,128]{1,0:T(8,128)S(1)} collective-permute-done((f32[256,128]{1,0:T(8,128)S(1)}, f32[256,128]{1,0:T(8,128)S(1)}, u32[]{:S(2)}, u32[]{:S(2)}) %collective-permute-start.2) | collective-permute-done | bytes 131104 | tf_op jit(solution)/shard_map/ppermute | solution.py:307
  19.9 0.7 %collective-permute-done.3 = f32[256,128]{1,0:T(8,128)S(1)} collective-permute-done((f32[256,128]{1,0:T(8,128)S(1)}, f32[256,128]{1,0:T(8,128)S(1)}, u32[]{:S(2)}, u32[]{:S(2)}) %collective-permute-start.3) | collective-permute-done | bytes 131104 | tf_op jit(solution)/shard_map/ppermute | solution.py:307
  20.7 1.6 %collective-permute-done.4 = f32[256,128]{1,0:T(8,128)S(1)} collective-permute-done((f32[256,128]{1,0:T(8,128)S(1)}, f32[256,128]{1,0:T(8,128)S(1)}, u32[]{:S(2)}, u32[]{:S(2)}) %collective-permute-start.4) | collective-permute-done | bytes 131104 | tf_op jit(solution)/shard_map/ppermute | solution.py:307
  22.3 0.1 collective-permute-start.5
  22.4 0.0 collective-permute-done.6
  22.4 0.0 copy-start.3
  22.4 0.6 %copy-done.3 = f32[128]{0:T(128)S(1)} copy-done((f32[128]{0:T(128)S(1)}, f32[128]{0:T(128)}, u32[]{:S(2)}) %copy-start.3) | copy-done | bytes 536
  23.1 0.2 prepare.1
  23.3 0.1 pad_maximum_fusion.3.out_gain_ref
  23.4 0.9 %collective-permute-done.5.y_ref = f32[1024,128]{1,0:T(8,128)S(1)} collective-permute-done((f32[1024,128]{1,0:T(8,128)S(1)}, f32[1024,128]{1,0:T(8,128)S(1)}, u32[]{:S(2)}, u32[]{:S(2)}) %collective-permute-start.5) | collective-permute-done | bytes 524320 | tf_op jit(solution)/shard_map/ppermute | solution.py:307
  24.3 16.2 %whole_update.1 = (f32[64,64]{1,0:T(8,128)}, f32[64,64]{1,0:T(8,128)}, f32[1,64]{1,0:T(1,128)}, f32[1,64]{1,0:T(1,128)}, f32[4,64,128]{2,1,0:T(8,128)}, /*index=5*/f32[64,128]{1,0:T(8,128)}, f32[64,128]{1,0:T(8,128)}) custom-call(f32[1024,128]{1,0:T(8,128)S(1)} %constant_dynamic-update-slice_fusion.x_ref, f32[1024,128]{1,0:T(8,128)S(1)} %collective-permute-done.5.y_ref, ...), custom_call_target="tpu_custom_call" | custom-call | tf_op jit(solution)/shard_map/whole_update/pallas_call | solution.py:290
  (11 shorter events, 0.1 us)
Async XLA Ops:
  0.6 5.9 %copy-start.4 = (f32[64,2,32]{0,2,1:T(8,128)S(1)}, f32[64,2,32]{0,2,1:T(8,128)}, u32[]{:S(2)}) copy-start(f32[64,2,32]{0,2,1:T(8,128)} %param.13) | copy-start | bytes 49156
  0.6 5.9 %copy-start.5 = (f32[64,2,32]{0,2,1:T(8,128)S(1)}, f32[64,2,32]{0,2,1:T(8,128)}, u32[]{:S(2)}) copy-start(f32[64,2,32]{0,2,1:T(8,128)} %param.7) | copy-start | bytes 49156
  0.7 9.0 %copy-start = (f32[4,128,64]{1,2,0:T(8,128)S(1)}, f32[4,128,64]{1,2,0:T(8,128)}, u32[]{:S(2)}) copy-start(f32[4,128,64]{1,2,0:T(8,128)} %param.10) | copy-start | bytes 393220
  1.6 8.1 %copy-start.1 = (f32[128,64]{0,1:T(8,128)S(1)}, f32[128,64]{0,1:T(8,128)}, u32[]{:S(2)}) copy-start(f32[128,64]{0,1:T(8,128)} %param.11) | copy-start | bytes 98308
  1.6 8.1 %copy-start.2 = (f32[64,128]{1,0:T(8,128)S(1)}, f32[64,128]{1,0:T(8,128)}, u32[]{:S(2)}) copy-start(f32[64,128]{1,0:T(8,128)} %wo.1) | copy-start | bytes 98308
  1.6 5.0 %collective-permute-start = (f32[64,128]{1,0:T(8,128)S(1)}, f32[64,128]{1,0:T(8,128)S(1)}, u32[]{:S(2)}, u32[]{:S(2)}) collective-permute-start(f32[64,128]{1,0:T(8,128)S(1)} %get-tuple-element.38), channel_id=1, source_target_pairs={{0,8},{1,9},{2,10},{3,11},{4,12},{5,13},{6,14},{7,15},{8,0},{9,1},... | collective-permute-start | bytes 98312 | tf_op jit(solution)/shard_map/ppermute | solution.py:307
  6.6 5.3 %collective-permute-start.1 = (f32[128,128]{1,0:T(8,128)S(1)}, f32[128,128]{1,0:T(8,128)S(1)}, u32[]{:S(2)}, u32[]{:S(2)}) collective-permute-start(f32[128,128]{1,0:T(8,128)S(1)} %pad_maximum_fusion.1), channel_id=1, source_target_pairs={{0,16},{1,17},{2,18},{3,19},{4,20},{5,21},{6,22},{7,23},{8,24},{9,... | collective-permute-start | bytes 196616 | tf_op jit(solution)/shard_map/ppermute | solution.py:307
  9.7 0.7 %copy-start.6 = (f32[64]{0:T(128)S(1)}, f32[64]{0:T(128)}, u32[]{:S(2)}) copy-start(f32[64]{0:T(128)} %param.9) | copy-start | bytes 772
  10.4 12.0 %collective-permute-start.6 = (f32[392,128]{1,0:T(8,128)S(1)}, f32[392,128]{1,0:T(8,128)S(1)}, u32[]{:S(2)}, u32[]{:S(2)}) collective-permute-start(f32[392,128]{1,0:T(8,128)S(1)} %select_maximum_fusion), channel_id=1, source_target_pairs={{0,1},{1,0},{2,3},{3,2},{4,5},{5,4},{6,7},{7,6},{8,9},{9,8},{10,11... | collective-permute-start | bytes 602120 | tf_op jit(solution)/shard_map/ppermute | solution.py:307
  12.0 7.9 %collective-permute-start.2 = (f32[256,128]{1,0:T(8,128)S(1)}, f32[256,128]{1,0:T(8,128)S(1)}, u32[]{:S(2)}, u32[]{:S(2)}) collective-permute-start(f32[256,128]{1,0:T(8,128)S(1)} %pad_maximum_fusion), channel_id=1, source_target_pairs={{0,1},{1,0},{2,3},{3,2},{4,5},{5,4},{6,7},{7,6},{8,9},{9,8},{10,11... | collective-permute-start | bytes 393224 | tf_op jit(solution)/shard_map/ppermute | solution.py:307
  13.8 8.5 %collective-permute-start.4 = (f32[256,128]{1,0:T(8,128)S(1)}, f32[256,128]{1,0:T(8,128)S(1)}, u32[]{:S(2)}, u32[]{:S(2)}) collective-permute-start(f32[256,128]{1,0:T(8,128)S(1)} %pad_maximum_fusion), channel_id=1, source_target_pairs={{0,5},{1,4},{2,7},{3,6},{4,1},{5,0},{6,3},{7,2},{8,13},{9,12},{10,... | collective-permute-start | bytes 393224 | tf_op jit(solution)/shard_map/ppermute | solution.py:307
  15.3 5.4 %collective-permute-start.3 = (f32[256,128]{1,0:T(8,128)S(1)}, f32[256,128]{1,0:T(8,128)S(1)}, u32[]{:S(2)}, u32[]{:S(2)}) collective-permute-start(f32[256,128]{1,0:T(8,128)S(1)} %pad_maximum_fusion), channel_id=1, source_target_pairs={{0,4},{1,5},{2,6},{3,7},{4,0},{5,1},{6,2},{7,3},{8,12},{9,13},{10,... | collective-permute-start | bytes 393224 | tf_op jit(solution)/shard_map/ppermute | solution.py:307
  22.3 2.0 %collective-permute-start.5 = (f32[1024,128]{1,0:T(8,128)S(1)}, f32[1024,128]{1,0:T(8,128)S(1)}, u32[]{:S(2)}, u32[]{:S(2)}) collective-permute-start(f32[1024,128]{1,0:T(8,128)S(1)} %constant_dynamic-update-slice_fusion.x_ref), channel_id=1, source_target_pairs={{0,2},{1,3},{2,0},{3,1},{4,6},{5,7},{6,4},{7,5},{8,10},{9,11},{10,... | collective-permute-start | bytes 1572872 | tf_op jit(solution)/shard_map/ppermute | solution.py:307
  22.4 0.7 %copy-start.3 = (f32[128]{0:T(128)S(1)}, f32[128]{0:T(128)}, u32[]{:S(2)}) copy-start(f32[128]{0:T(128)} %param.8) | copy-start | bytes 1540

commit v2 on v1

--- a/solution.py
+++ b/solution.py
@@ -12,6 +12,7 @@
 F32 = jnp.float32
 BF16 = jnp.bfloat16
 LANES = 128
+ROWS = 8
 
 
 def spread(pair, in_gain, output_gain, w_edges, w_gate, w_out, cotangent):
@@ -97,10 +98,8 @@
     return hi, (x - hi.astype(F32)).astype(BF16)
 
 
-def dot3(a, b, dims=((1,), (0,))):
-    (ah, al), (bh, bl) = a, b
-    dot = functools.partial(lax.dot_general, dimension_numbers=(dims, ((), ())), preferred_element_type=F32)
-    return dot(ah, bh) + (dot(ah, bl) + dot(al, bh))
+def dot(a, b):
+    return jnp.dot(a, b, preferred_element_type=F32)
 
 
 def mean_lanes(x):
@@ -113,7 +112,7 @@
     return centred * rstd, rstd
 
 
-def prepare_kernel(gain_ref, we, wg, wo, oe, og, oo, wnh, wnl, wth, wtl, woh, wol, wqh, wql):
+def prepare_kernel(gain_ref, we, wg, wo, oe, og, oo, wnh, wnl, wdh, wtl, woh, wol, wqh, wql):
     s, c = wg.shape
     chan = lax.axis_index("chan")
     gain = gain_ref[...]
@@ -121,21 +120,27 @@
     def put(k, both):
         at = slice(k * c, (k + 1) * c)
         wnh[at, :], wnl[at, :] = split(both)
-        wth[:, at], wtl[:, at] = split(both.T)
+        high, wtl[:, at] = split(both.T)
+        wdh[:c, at] = high
+        wdh[c:, at] = high
 
     for e in range(4):
         put(e, jnp.concatenate([we[e], oe[e * s : (e + 1) * s, :]], axis=0) * gain)
     own, other = wg[...] * gain, og[...] * gain
     put(4, jnp.concatenate([jnp.where(chan == 0, own, other), jnp.where(chan == 0, other, own)], axis=0))
     both = jnp.concatenate([wo[...], oo[...]], axis=0)
-    woh[...], wol[...] = split(both)
-    wqh[...], wql[...] = split(both.T)
+    high, wol[...] = split(both)
+    woh[:c, :] = high
+    woh[c:, :] = high
+    high, wql[...] = split(both.T)
+    wqh[:c, :] = high
+    wqh[c:, :] = high
 
 
 def prepare(gain, w_e, w_g, w_o, other):
     s, c = w_g.shape
     vm = pl.BlockSpec(memory_space=pltpu.VMEM)
-    shapes = [(5 * c, c)] * 2 + [(c, 5 * c)] * 2 + [(c, c)] * 4
+    shapes = [(5 * c, c), (5 * c, c), (2 * c, 5 * c), (c, 5 * c), (2 * c, c), (c, c), (2 * c, c), (c, c)]
     return pl.pallas_call(
         prepare_kernel,
         out_shape=[jax.ShapeDtypeStruct(x, BF16) for x in shapes],
@@ -156,9 +161,10 @@
 
 
 def update_kernel(
-    n, x_ref, y_ref, gain_ref, out_gain_ref, we, wg, oe, og, wnh, wnl, wth, wtl, woh, wol, wqh, wql,
+    n, x_ref, y_ref, gain_ref, out_gain_ref, we, wg, oe, og, wnh, wnl, wdh, wtl, woh, wol, wqh, wql,
     up_ref, dp_ref, dig_ref, dog_ref, de_ref, dg_ref, do_ref,
-    ct, zh, zl, left, s1, right, s3, right_t, gate, upd, xh, xl, mh, ml, dtri, dgp, dh, dl, zown, rown, grads,
+    ct, z, proj, left, s1, right, s3, right_t, gate, upd, xhat, xs, rstds, ms, mid, dtri, dgp, dh, dl, zown, rown,
+    grads,
 ):
     c, s = LANES, LANES // 2
     blk = up_ref.shape[0]
@@ -166,94 +172,95 @@
     upper = x_ref.shape[0] // (4 * blk)
     row, chan = lax.axis_index("row"), lax.axis_index("chan")
     zy, core = row // 2, row % 2
-    rows = 4
-    cells = rows * n
     low = lax.broadcasted_iota(jnp.int32, (blk, c), 1) < s
 
-    def project(t, carry):
-        zpos, ypos = t % upper, t // upper
-        base = (zpos + upper * 2 * ypos) * blk
+    def place(t, k):
+        target = zy ^ (t % upper * 2 + t // upper)
+        return pl.multiple_of((target * 2 + (core ^ k)) * blk, blk)
+
+    for t in range(2 * upper):
+        base = (t % upper + upper * 2 * (t // upper)) * blk
         first_at = pl.multiple_of(base + upper * blk * chan, blk)
         second_at = pl.multiple_of(base + upper * blk * (1 - chan), blk)
-        target = zy ^ (zpos * 2 + ypos)
-        pair, places = [], []
+        pair = []
         for k, ref in enumerate((x_ref, y_ref)):
             first, second = ref[pl.ds(first_at, blk), :], ref[pl.ds(second_at, blk), :]
             pair.append(jnp.where(low, first, pltpu.roll(second, s, 1)))
-            at = pl.multiple_of((target * 2 + (core ^ k)) * blk, blk)
-            places.append(at)
-            ct[pl.ds(at, blk), :] = jnp.where(low, pltpu.roll(first, s, 1), second)
+            ct[pl.ds(place(t, k), blk), :] = jnp.where(low, pltpu.roll(first, s, 1), second)
         zhat, rstd = norm_lanes(jnp.concatenate(pair, axis=0))
-        z = split(zhat)
-
-        @pl.when(t == 0)
-        def _():
+        hi, lo = split(zhat)
+        for k in range(2):
+            here, part = pl.ds(place(t, k), blk), slice(k * blk, (k + 1) * blk)
+            z[here, :c], z[here, c:] = hi[part], lo[part]
+        if t == 0:
             zown[...] = zhat[:blk]
             rown[...] = jnp.broadcast_to(rstd[:blk], (blk, c))
 
-        proj = dot3(z, (wth[...], wtl[...]))
-        sl = jax.nn.sigmoid(proj[:, c : 2 * c])
-        le = sl * proj[:, :c]
-        sr = jax.nn.sigmoid(proj[:, 3 * c : 4 * c])
-        ri = sr * proj[:, 2 * c : 3 * c]
-        ga = jax.nn.sigmoid(proj[:, 4 * c :])
-        for k in range(2):
-            here, part = pl.ds(places[k], blk), slice(k * blk, (k + 1) * blk)
-            zh[here, :], zl[here, :] = z[0][part], z[1][part]
-            left[here, :], s1[here, :] = le[part], sl[part]
-            right[here, :], s3[here, :] = ri[part], sr[part]
-            gate[here, :] = ga[part]
-            for r in range(q):
-                at = k * blk + r * n
-                right_t[pl.ds(places[k] // n + r, n, stride=n), :] = ri[at : at + n]
-        return carry
-
-    lax.fori_loop(0, 2 * upper, project, 0)
+    def matmul(a, high, low):
+        return dot(a[...], high[...]) + dot(a[:, :c], low[...])
+
+    proj[...] = matmul(z, wdh, wtl)
+    a = jax.nn.sigmoid(proj[:, c : 2 * c])
+    left[...], s1[...] = a * proj[:, :c], a
+    a = jax.nn.sigmoid(proj[:, 3 * c : 4 * c])
+    found = a * proj[:, 2 * c : 3 * c]
+    right[...], s3[...] = found, a
+    for r in range(n):
+        right_t[pl.ds(r, n, stride=n), :] = found[r * n : (r + 1) * n]
+    gate[...] = jax.nn.sigmoid(proj[:, 4 * c :])
 
     def row_of(ref, at):
         return ref[pl.ds(at, 8, stride=0), :]
 
-    def triangle(b, total):
+    rows = ROWS
+    cells = rows * n
+
+    def triangle(b, carry):
         r0 = pl.multiple_of(b * cells, cells)
-        here = pl.ds(r0, cells)
-        tri = products(n, rows, lambda a, m: row_of(left, r0 + a * n + m), right_t)
-        xhat, rstd = norm_lanes(tri)
-        x = split(xhat * out_gain_ref[...])
-        xh[here, :], xl[here, :] = x
-        mixed = dot3(x, (woh[...], wol[...]))
-        ga = gate[here, :]
-        upd[here, :] = ga * mixed
-        dm = ct[here, :] * ga
-        m = split(dm)
-        mh[here, :], ml[here, :] = m
-        dgp[here, :] = dm * mixed * (1.0 - ga)
-        hidden = dot3(m, (wqh[...], wql[...]))
-        ng = hidden * out_gain_ref[...]
-        dtri[here, :] = rstd * (ng - mean_lanes(ng) - xhat * mean_lanes(ng * xhat))
-        return total + jnp.sum(xhat * hidden, axis=0, keepdims=True)
-
-    total = lax.fori_loop(0, n // rows, triangle, jnp.zeros((1, c), F32))
-    dog_ref[...] = total[:, :s]
-
-    def gradients(b, carry):
+        mid[pl.ds(r0, cells), :] = products(n, rows, lambda a, m: row_of(left, r0 + a * n + m), right_t)
+        return carry
+
+    lax.fori_loop(0, n // rows, triangle, 0)
+    found, rstd = norm_lanes(mid[...])
+    xhat[...] = found
+    rstds[...] = jnp.broadcast_to(rstd, found.shape)
+    xs[:, :c], xs[:, c:] = split(found * out_gain_ref[...])
+    mixed, a = matmul(xs, woh, wol), gate[...]
+    upd[...] = a * mixed
+    dm = ct[...] * a
+    ms[:, :c], ms[:, c:] = split(dm)
+    dh[:, 4 * c :], dl[:, 4 * c :] = split(dm * mixed * (1.0 - a))
+    hidden, found = matmul(ms, wqh, wql), xhat[...]
+    ng = hidden * out_gain_ref[...]
+    dtri[...] = rstds[...] * (ng - mean_lanes(ng) - found * mean_lanes(ng * found))
+    dog_ref[...] = jnp.sum(found * hidden, axis=0, keepdims=True)[:, :s]
+
+    def left_gradient(b, carry):
         r0 = pl.multiple_of(b * cells, cells)
-        here = pl.ds(r0, cells)
-        dle = products(n, rows, lambda a, m: row_of(dtri, r0 + a * n + m), right)
-        a = s1[here, :]
-        dh[here, :c], dl[here, :c] = split(dle * a)
-        dh[here, c : 2 * c], dl[here, c : 2 * c] = split(dle * left[here, :] * (1.0 - a))
-        dri = products(n, rows, lambda a, m: row_of(dtri, m * n + b * rows + a), left)
-        a = s3[here, :]
-        dh[here, 2 * c : 3 * c], dl[here, 2 * c : 3 * c] = split(dri * a)
-        dh[here, 3 * c : 4 * c], dl[here, 3 * c : 4 * c] = split(dri * right[here, :] * (1.0 - a))
-        dh[here, 4 * c :], dl[here, 4 * c :] = split(dgp[here, :])
+        mid[pl.ds(r0, cells), :] = products(n, rows, lambda a, m: row_of(dtri, r0 + a * n + m), right)
         return carry
 
-    lax.fori_loop(0, n // rows, gradients, 0)
-
-    down = ((0,), (0,))
-    grads[...] = dot3((dh[...], dl[...]), (zh[...], zl[...]), down)
-    do_ref[...] = dot3((xh[:, :s], xl[:, :s]), (mh[...], ml[...]), down)
+    def right_gradient(b, carry):
+        r0 = pl.multiple_of(b * cells, cells)
+        xhat[pl.ds(r0, cells), :] = products(n, rows, lambda a, m: row_of(dtri, m * n + b * rows + a), left)
+        return carry
+
+    lax.fori_loop(0, n // rows, left_gradient, 0)
+    lax.fori_loop(0, n // rows, right_gradient, 0)
+    dle, a = mid[...], s1[...]
+    dh[:, :c], dl[:, :c] = split(dle * a)
+    dh[:, c : 2 * c], dl[:, c : 2 * c] = split(dle * left[...] * (1.0 - a))
+    dri, a = xhat[...], s3[...]
+    dh[:, 2 * c : 3 * c], dl[:, 2 * c : 3 * c] = split(dri * a)
+    dh[:, 3 * c : 4 * c], dl[:, 3 * c : 4 * c] = split(dri * right[...] * (1.0 - a))
+
+    def down(a, b):
+        return lax.dot_general(a, b, (((0,), (0,)), ((), ())), preferred_element_type=F32)
+
+    wide = down(dh[...], z[...])
+    grads[...] = wide[:, :c] + (wide[:, c:] + down(dl[...], z[:, :c]))
+    wide = down(xs[:, :s], ms[...])
+    do_ref[...] = wide[:, :c] + (wide[:, c:] + down(xs[:, c : c + s], ms[:, :c]))
 
     gain = gain_ref[...]
     mine = pl.ds(pl.multiple_of(4 * c + s * chan, s), s)
@@ -272,7 +279,7 @@
     dig_ref[...] = half(jnp.broadcast_to(d_gain, (8, c)))[:1]
     here = pl.ds(pl.multiple_of(row * blk, blk), blk)
     up_ref[...] = half(upd[here, :])
-    dz = dot3((dh[here, :], dl[here, :]), (wnh[...], wnl[...]))
+    dz = dot(dh[here, :], wnh[...]) + (dot(dh[here, :], wnl[...]) + dot(dl[here, :], wnh[...]))
     zhat = zown[...]
     dp_ref[...] = half(rown[...] * (dz - mean_lanes(dz) - zhat * mean_lanes(dz * zhat)))
 
@@ -282,10 +289,14 @@
     vm = pl.BlockSpec(memory_space=pltpu.VMEM)
     cells = n * n
     out = [(blk, s), (blk, s), (1, s), (1, s), (4, s, c), (s, c), (s, c)]
-    full, half = pltpu.VMEM((cells, c), F32), pltpu.VMEM((cells, c), BF16)
+
+    def vmem(rows, width, dtype=F32):
+        return pltpu.VMEM((rows, width), dtype)
+
+    full, both = vmem(cells, c), vmem(cells, 2 * c, BF16)
     scratch = (
-        [full, half, half] + [full] * 7 + [half] * 4 + [full] * 2
-        + [pltpu.VMEM((cells, 5 * c), BF16)] * 2 + [pltpu.VMEM((blk, c), F32)] * 2 + [pltpu.VMEM((5 * c, c), F32)]
+        [full, both, vmem(cells, 5 * c)] + [full] * 8 + [both, full, both] + [full] * 3
+        + [vmem(cells, 5 * c, BF16)] * 2 + [vmem(blk, c)] * 2 + [vmem(5 * c, c)]
     )
     return pl.pallas_call(
         functools.partial(update_kernel, n),

time: 40.7 us -> 33.1 us (0.81)
  Pallas kernels: 16.4 us -> 8.79 us
    pallas_call x1, Pallas kernels: 16.2 us -> 8.61 us  [whole_update(): pl.pallas_call(functools.partial(update_kernel, n), out_shape=[jax.ShapeD...]
  transfers between devices with their start and end apart: 7 -> 7, of which waited for: 5 -> 5; matrix products, arithmetic and copies ran while one was open for 1% -> 1% of each run, Pallas kernels for 0% -> 1%
where the time goes in v2:
time: 33.1 us; the launch traced here: 32.9 us
  starting transfers between devices  11.3 us (34%)
  waiting for transfers between devices  9.59 us (29%)
  Pallas kernels  8.79 us (27%)
  local copies, waits for them, and re-layouts  1.38 us (4%)
  other arithmetic  1.14 us (3%)
  between operations  0.75 us (2%)
    ppermute x7, starting transfers between devices, swap(): lax.ppermute(x, ('row', 'chan'), [(i, i ^ bits) for i in range(devices)])  11.3 us
    ppermute x7, waiting for transfers between devices, swap(): lax.ppermute(x, ('row', 'chan'), [(i, i ^ bits) for i in range(devices)])  9.59 us
    pallas_call x1, Pallas kernels, whole_update(): pl.pallas_call(functools.partial(update_kernel, n), out_shape=[jax.ShapeD...  8.61 us
    unnamed x18, local copies, waits for them, and re-layouts  1.35 us
    unnamed x1, other arithmetic  0.89 us
  transfers between devices with their start and end apart: 7, of which 5 were waited for; matrix products, arithmetic and copies ran while one was open for 1% of the time, Pallas kernels for 1%

profile of v2, /device:TPU:0, one launch (start us, length us, event | category | flops | bytes accessed | tf_op | source)
XLA Modules:
  0.0 32.9 jit_solution(2817512347717064405)
XLA Ops:
  0.6 0.0 copy-start.4
  0.6 0.0 copy-start.5
  0.7 0.0 copy-start
  0.7 0.9 %constant_dynamic-update-slice_fusion.5 = (f32[1024,128]{1,0:T(8,128)S(1)}, f32[64,128]{1,0:T(8,128)S(1)}) fusion(f32[64,64]{1,0:T(8,128)} %bitcast.30, f32[64,64]{1,0:T(8,128)} %bitcast.33), kind=kLoop, calls=%fused_computation.10 | loop fusion | flops 8191 | bytes 98304
  1.6 0.0 copy-start.2
  1.6 3.1 %collective-permute-start = (f32[64,128]{1,0:T(8,128)S(1)}, f32[64,128]{1,0:T(8,128)S(1)}, u32[]{:S(2)}, u32[]{:S(2)}) collective-permute-start(f32[64,128]{1,0:T(8,128)S(1)} %get-tuple-element.38), channel_id=1, source_target_pairs={{0,8},{1,9},{2,10},{3,11},{4,12},{5,13},{6,14},{7,15},{8,0},{9,1},... | collective-permute-start | bytes 98312 | tf_op jit(solution)/shard_map/ppermute | solution.py:318
  4.7 1.9 %collective-permute-done = f32[64,128]{1,0:T(8,128)S(1)} collective-permute-done((f32[64,128]{1,0:T(8,128)S(1)}, f32[64,128]{1,0:T(8,128)S(1)}, u32[]{:S(2)}, u32[]{:S(2)}) %collective-permute-start) | collective-permute-done | bytes 32800 | tf_op jit(solution)/shard_map/ppermute | solution.py:318
  6.6 0.0 copy-done.4
  6.6 0.0 copy-done.5
  6.6 0.1 pad_maximum_fusion.1
  6.6 3.0 %collective-permute-start.1 = (f32[128,128]{1,0:T(8,128)S(1)}, f32[128,128]{1,0:T(8,128)S(1)}, u32[]{:S(2)}, u32[]{:S(2)}) collective-permute-start(f32[128,128]{1,0:T(8,128)S(1)} %pad_maximum_fusion.1), channel_id=1, source_target_pairs={{0,16},{1,17},{2,18},{3,19},{4,20},{5,21},{6,22},{7,23},{8,24},{9,... | collective-permute-start | bytes 196616 | tf_op jit(solution)/shard_map/ppermute | solution.py:318
  9.7 0.0 copy-done
  9.7 0.0 copy-done.1
  9.7 0.0 copy-done.2
  9.7 0.6 %copy-done.6 = f32[64]{0:T(128)S(1)} copy-done((f32[64]{0:T(128)S(1)}, f32[64]{0:T(128)}, u32[]{:S(2)}) %copy-start.6) | copy-done | bytes 280
  10.4 1.6 %collective-permute-start.6 = (f32[392,128]{1,0:T(8,128)S(1)}, f32[392,128]{1,0:T(8,128)S(1)}, u32[]{:S(2)}, u32[]{:S(2)}) collective-permute-start(f32[392,128]{1,0:T(8,128)S(1)} %select_maximum_fusion), channel_id=1, source_target_pairs={{0,1},{1,0},{2,3},{3,2},{4,5},{5,4},{6,7},{7,6},{8,9},{9,8},{10,11... | collective-permute-start | bytes 602120 | tf_op jit(solution)/shard_map/ppermute | solution.py:318
  11.9 0.0 collective-permute-done.1
  11.9 0.1 pad_maximum_fusion
  12.0 1.8 %collective-permute-start.2 = (f32[256,128]{1,0:T(8,128)S(1)}, f32[256,128]{1,0:T(8,128)S(1)}, u32[]{:S(2)}, u32[]{:S(2)}) collective-permute-start(f32[256,128]{1,0:T(8,128)S(1)} %pad_maximum_fusion), channel_id=1, source_target_pairs={{0,1},{1,0},{2,3},{3,2},{4,5},{5,4},{6,7},{7,6},{8,9},{9,8},{10,11... | collective-permute-start | bytes 393224 | tf_op jit(solution)/shard_map/ppermute | solution.py:318
  13.8 1.5 %collective-permute-start.4 = (f32[256,128]{1,0:T(8,128)S(1)}, f32[256,128]{1,0:T(8,128)S(1)}, u32[]{:S(2)}, u32[]{:S(2)}) collective-permute-start(f32[256,128]{1,0:T(8,128)S(1)} %pad_maximum_fusion), channel_id=1, source_target_pairs={{0,5},{1,4},{2,7},{3,6},{4,1},{5,0},{6,3},{7,2},{8,13},{9,12},{10,... | collective-permute-start | bytes 393224 | tf_op jit(solution)/shard_map/ppermute | solution.py:318
  15.3 0.2 collective-permute-start.3
  15.5 4.4 %collective-permute-done.2 = f32[256,128]{1,0:T(8,128)S(1)} collective-permute-done((f32[256,128]{1,0:T(8,128)S(1)}, f32[256,128]{1,0:T(8,128)S(1)}, u32[]{:S(2)}, u32[]{:S(2)}) %collective-permute-start.2) | collective-permute-done | bytes 131104 | tf_op jit(solution)/shard_map/ppermute | solution.py:318
  19.9 0.7 %collective-permute-done.3 = f32[256,128]{1,0:T(8,128)S(1)} collective-permute-done((f32[256,128]{1,0:T(8,128)S(1)}, f32[256,128]{1,0:T(8,128)S(1)}, u32[]{:S(2)}, u32[]{:S(2)}) %collective-permute-start.3) | collective-permute-done | bytes 131104 | tf_op jit(solution)/shard_map/ppermute | solution.py:318
  20.7 1.6 %collective-permute-done.4 = f32[256,128]{1,0:T(8,128)S(1)} collective-permute-done((f32[256,128]{1,0:T(8,128)S(1)}, f32[256,128]{1,0:T(8,128)S(1)}, u32[]{:S(2)}, u32[]{:S(2)}) %collective-permute-start.4) | collective-permute-done | bytes 131104 | tf_op jit(solution)/shard_map/ppermute | solution.py:318
  22.3 0.1 collective-permute-start.5
  22.4 0.0 collective-permute-done.6
  22.4 0.0 copy-start.3
  22.4 0.6 %copy-done.3 = f32[128]{0:T(128)S(1)} copy-done((f32[128]{0:T(128)S(1)}, f32[128]{0:T(128)}, u32[]{:S(2)}) %copy-start.3) | copy-done | bytes 536
  23.1 0.2 prepare.1
  23.3 0.1 pad_maximum_fusion.3.out_gain_ref
  23.4 0.9 %collective-permute-done.5.y_ref = f32[1024,128]{1,0:T(8,128)S(1)} collective-permute-done((f32[1024,128]{1,0:T(8,128)S(1)}, f32[1024,128]{1,0:T(8,128)S(1)}, u32[]{:S(2)}, u32[]{:S(2)}) %collective-permute-start.5) | collective-permute-done | bytes 524320 | tf_op jit(solution)/shard_map/ppermute | solution.py:318
  24.3 8.6 %whole_update.1 = (f32[64,64]{1,0:T(8,128)}, f32[64,64]{1,0:T(8,128)}, f32[1,64]{1,0:T(1,128)}, f32[1,64]{1,0:T(1,128)}, f32[4,64,128]{2,1,0:T(8,128)}, /*index=5*/f32[64,128]{1,0:T(8,128)}, f32[64,128]{1,0:T(8,128)}) custom-call(f32[1024,128]{1,0:T(8,128)S(1)} %constant_dynamic-update-slice_fusion.x_ref, f32[1024,128]{1,0:T(8,128)S(1)} %collective-permute-done.5.y_ref, ...), custom_call_target="tpu_custom_call" | custom-call | tf_op jit(solution)/shard_map/whole_update/pallas_call | solution.py:301
  (11 shorter events, 0.1 us)
Async XLA Ops:
  0.6 5.9 %copy-start.4 = (f32[64,2,32]{0,2,1:T(8,128)S(1)}, f32[64,2,32]{0,2,1:T(8,128)}, u32[]{:S(2)}) copy-start(f32[64,2,32]{0,2,1:T(8,128)} %param.13) | copy-start | bytes 49156
  0.6 5.9 %copy-start.5 = (f32[64,2,32]{0,2,1:T(8,128)S(1)}, f32[64,2,32]{0,2,1:T(8,128)}, u32[]{:S(2)}) copy-start(f32[64,2,32]{0,2,1:T(8,128)} %param.7) | copy-start | bytes 49156
  0.7 9.0 %copy-start = (f32[4,128,64]{1,2,0:T(8,128)S(1)}, f32[4,128,64]{1,2,0:T(8,128)}, u32[]{:S(2)}) copy-start(f32[4,128,64]{1,2,0:T(8,128)} %param.10) | copy-start | bytes 393220
  1.6 8.1 %copy-start.1 = (f32[128,64]{0,1:T(8,128)S(1)}, f32[128,64]{0,1:T(8,128)}, u32[]{:S(2)}) copy-start(f32[128,64]{0,1:T(8,128)} %param.11) | copy-start | bytes 98308
  1.6 8.1 %copy-start.2 = (f32[64,128]{1,0:T(8,128)S(1)}, f32[64,128]{1,0:T(8,128)}, u32[]{:S(2)}) copy-start(f32[64,128]{1,0:T(8,128)} %wo.1) | copy-start | bytes 98308
  1.6 5.0 %collective-permute-start = (f32[64,128]{1,0:T(8,128)S(1)}, f32[64,128]{1,0:T(8,128)S(1)}, u32[]{:S(2)}, u32[]{:S(2)}) collective-permute-start(f32[64,128]{1,0:T(8,128)S(1)} %get-tuple-element.38), channel_id=1, source_target_pairs={{0,8},{1,9},{2,10},{3,11},{4,12},{5,13},{6,14},{7,15},{8,0},{9,1},... | collective-permute-start | bytes 98312 | tf_op jit(solution)/shard_map/ppermute | solution.py:318
  6.6 5.3 %collective-permute-start.1 = (f32[128,128]{1,0:T(8,128)S(1)}, f32[128,128]{1,0:T(8,128)S(1)}, u32[]{:S(2)}, u32[]{:S(2)}) collective-permute-start(f32[128,128]{1,0:T(8,128)S(1)} %pad_maximum_fusion.1), channel_id=1, source_target_pairs={{0,16},{1,17},{2,18},{3,19},{4,20},{5,21},{6,22},{7,23},{8,24},{9,... | collective-permute-start | bytes 196616 | tf_op jit(solution)/shard_map/ppermute | solution.py:318
  9.7 0.7 %copy-start.6 = (f32[64]{0:T(128)S(1)}, f32[64]{0:T(128)}, u32[]{:S(2)}) copy-start(f32[64]{0:T(128)} %param.9) | copy-start | bytes 772
  10.4 12.0 %collective-permute-start.6 = (f32[392,128]{1,0:T(8,128)S(1)}, f32[392,128]{1,0:T(8,128)S(1)}, u32[]{:S(2)}, u32[]{:S(2)}) collective-permute-start(f32[392,128]{1,0:T(8,128)S(1)} %select_maximum_fusion), channel_id=1, source_target_pairs={{0,1},{1,0},{2,3},{3,2},{4,5},{5,4},{6,7},{7,6},{8,9},{9,8},{10,11... | collective-permute-start | bytes 602120 | tf_op jit(solution)/shard_map/ppermute | solution.py:318
  12.0 7.9 %collective-permute-start.2 = (f32[256,128]{1,0:T(8,128)S(1)}, f32[256,128]{1,0:T(8,128)S(1)}, u32[]{:S(2)}, u32[]{:S(2)}) collective-permute-start(f32[256,128]{1,0:T(8,128)S(1)} %pad_maximum_fusion), channel_id=1, source_target_pairs={{0,1},{1,0},{2,3},{3,2},{4,5},{5,4},{6,7},{7,6},{8,9},{9,8},{10,11... | collective-permute-start | bytes 393224 | tf_op jit(solution)/shard_map/ppermute | solution.py:318
  13.8 8.5 %collective-permute-start.4 = (f32[256,128]{1,0:T(8,128)S(1)}, f32[256,128]{1,0:T(8,128)S(1)}, u32[]{:S(2)}, u32[]{:S(2)}) collective-permute-start(f32[256,128]{1,0:T(8,128)S(1)} %pad_maximum_fusion), channel_id=1, source_target_pairs={{0,5},{1,4},{2,7},{3,6},{4,1},{5,0},{6,3},{7,2},{8,13},{9,12},{10,... | collective-permute-start | bytes 393224 | tf_op jit(solution)/shard_map/ppermute | solution.py:318
  15.3 5.4 %collective-permute-start.3 = (f32[256,128]{1,0:T(8,128)S(1)}, f32[256,128]{1,0:T(8,128)S(1)}, u32[]{:S(2)}, u32[]{:S(2)}) collective-permute-start(f32[256,128]{1,0:T(8,128)S(1)} %pad_maximum_fusion), channel_id=1, source_target_pairs={{0,4},{1,5},{2,6},{3,7},{4,0},{5,1},{6,2},{7,3},{8,12},{9,13},{10,... | collective-permute-start | bytes 393224 | tf_op jit(solution)/shard_map/ppermute | solution.py:318
  22.3 2.0 %collective-permute-start.5 = (f32[1024,128]{1,0:T(8,128)S(1)}, f32[1024,128]{1,0:T(8,128)S(1)}, u32[]{:S(2)}, u32[]{:S(2)}) collective-permute-start(f32[1024,128]{1,0:T(8,128)S(1)} %constant_dynamic-update-slice_fusion.x_ref), channel_id=1, source_target_pairs={{0,2},{1,3},{2,0},{3,1},{4,6},{5,7},{6,4},{7,5},{8,10},{9,11},{10,... | collective-permute-start | bytes 1572872 | tf_op jit(solution)/shard_map/ppermute | solution.py:318
  22.4 0.7 %copy-start.3 = (f32[128]{0:T(128)S(1)}, f32[128]{0:T(128)}, u32[]{:S(2)}) copy-start(f32[128]{0:T(128)} %param.8) | copy-start | bytes 1540

commit v3 on v0

--- a/solution.py
+++ b/solution.py
@@ -1,12 +1,23 @@
+import functools
+
 import jax
 import jax.numpy as jnp
 from jax import lax
+from jax.experimental import pallas as pl
+from jax.experimental.pallas import tpu as pltpu
 from jax.sharding import PartitionSpec as P
 
 HIDDEN_WIDTH = 128
-
-
-def shards(pair, in_gain, output_gain, w_edges, w_gate, w_out, cotangent):
+EPS = 1e-05
+F32 = jnp.float32
+BF16 = jnp.bfloat16
+LANES = 128
+ROWS = 8
+CHUNK = 64
+DEEP = 256
+
+
+def spread(pair, in_gain, output_gain, w_edges, w_gate, w_out, cotangent):
     hp = lax.Precision.HIGHEST
     shard_c = pair.shape[0]
     whole = lax.all_gather(pair, "chan", axis=0, tiled=True)
@@ -84,7 +95,368 @@
     return (update, d_pair, totals[0], totals[1], totals[2], totals[3], totals[4])
 
 
+def split(x):
+    hi = x.astype(BF16)
+    return hi, (x - hi.astype(F32)).astype(BF16)
+
+
+def dot(a, b):
+    return jnp.dot(a, b, preferred_element_type=F32)
+
+
+def matmul(a, twice_high, low):
+    return dot(a, twice_high) + dot(a[:, :LANES], low)
+
+
+def down(a, b):
+    return lax.dot_general(a, b, (((0,), (0,)), ((), ())), preferred_element_type=F32)
+
+
+def chunks(cells, step=CHUNK):
+    return [slice(at, at + step) for at in range(0, cells, step)]
+
+
+def mean_lanes(x):
+    return jnp.mean(x, axis=-1, keepdims=True)
+
+
+def norm_lanes(x):
+    centred = x - mean_lanes(x)
+    rstd = lax.rsqrt(mean_lanes(centred * centred) + EPS)
+    return centred * rstd, rstd
+
+
+def cells_from(ref, blk, upper, chan):
+    half = blk // 2
+    low = lax.broadcasted_iota(jnp.int32, (half, LANES), 1) < LANES // 2
+    for t in range(2 * upper):
+        own, other = ((0, 3), (2, 1))[t // upper]
+
+        def block(side):
+            at = (t % upper + upper * (own + (other - own) * side)) * half
+            return ref[pl.ds(pl.multiple_of(at, half), half), :]
+
+        first, second = block(chan), block(1 - chan)
+        yield jnp.where(low, first, pltpu.roll(second, LANES // 2, 1))
+        yield jnp.where(low, pltpu.roll(first, LANES // 2, 1), second)
+
+
+def true_row(p, q, upper, rows):
+    row = lax.axis_index("row")
+    far, t = p // (rows // 2), p % (rows // 2) // q
+    return (((row // 2) ^ (t % upper * 2 + t // upper)) * 2 + ((row % 2) ^ far)) * q + p % q
+
+
+def held_row(j, q, upper, rows):
+    row = lax.axis_index("row")
+    apart = (row // 2) ^ (j // q // 2)
+    t = apart % 2 * upper + apart // 2
+    return ((row % 2) ^ (j // q % 2)) * (rows // 2) + t * q + j % q
+
+
+def pack_kernel(we, wg, wo, gain, mine):
+    s = wg.shape[0]
+    for e in range(4):
+        mine[e * s : (e + 1) * s, :] = we[e]
+    mine[4 * s : 5 * s, :] = wg[...]
+    mine[5 * s : 6 * s, :] = wo[...]
+    mine[6 * s :, :] = gain[...]
+
+
+def prepare_kernel(gain_ref, mine, other, wnh, wnl, wdh, wtl, woh, wol, wqh, wql, gain_out):
+    c = LANES
+    s = c // 2
+    chan = lax.axis_index("chan")
+    gain = gain_ref[...]
+
+    def both(k):
+        at = slice(k * s, (k + 1) * s)
+        return mine[at, :], other[at, :]
+
+    def put(k, whole):
+        at = slice(k * c, (k + 1) * c)
+        wnh[at, :], wnl[at, :] = split(whole)
+        high, wtl[:, at] = split(whole.T)
+        wdh[:c, at] = high
+        wdh[c:, at] = high
+
+    for e in range(4):
+        put(e, jnp.concatenate(both(e), axis=0) * gain)
+    a, b = both(4)
+    put(4, jnp.concatenate([jnp.where(chan == 0, a, b), jnp.where(chan == 0, b, a)], axis=0) * gain)
+    whole = jnp.concatenate(both(5), axis=0)
+    high, wol[...] = split(whole)
+    woh[:c, :] = high
+    woh[c:, :] = high
+    high, wql[...] = split(whole.T)
+    wqh[:c, :] = high
+    wqh[c:, :] = high
+    gain_out[:, :s] = mine[6 * s : 6 * s + 1, :s]
+    gain_out[:, s:] = other[6 * s : 6 * s + 1, :s]
+
+
+def project_kernel(blk, x_ref, wdh, wtl, z, left, s1, right, s3, gate, zown, rown, proj):
+    c = LANES
+    upper = x_ref.shape[0] // (2 * blk)
+    chan = lax.axis_index("chan")
+    half = blk // 2
+    for k, cells in enumerate(cells_from(x_ref, blk, upper, chan)):
+        at = slice(k * half, (k + 1) * half)
+        zhat, rstd = norm_lanes(cells)
+        z[at, :c], z[at, c:] = split(zhat)
+        if k < 2 and zown is not None:
+            zown[at, :] = zhat
+            rown[at, :] = jnp.broadcast_to(rstd, zhat.shape)
+    for at in chunks(z.shape[0], DEEP):
+        proj[at, :] = matmul(z[at, :], wdh[...], wtl[...])
+    for at in chunks(z.shape[0]):
+        a = jax.nn.sigmoid(proj[at, c : 2 * c])
+        left[at, :], s1[at, :] = a * proj[at, :c], a
+        a = jax.nn.sigmoid(proj[at, 3 * c : 4 * c])
+        right[at, :], s3[at, :] = a * proj[at, 2 * c : 3 * c], a
+        gate[at, :] = jax.nn.sigmoid(proj[at, 4 * c :])
+
+
+def products(n, x_row, y_of):
+    acc = [jnp.zeros((n // 8, 8, LANES), F32) for _ in range(ROWS)]
+    for m in range(n):
+        y = y_of(m).reshape(n // 8, 8, LANES)
+        for a in range(ROWS):
+            acc[a] = acc[a] + x_row(a, m)[None] * y
+    return jnp.concatenate([part.reshape(n, LANES) for part in acc], axis=0)
+
+
+def row_of(ref, at):
+    return ref[pl.ds(at, 8, stride=0), :]
+
+
+def over_rows(n, out, body):
+    def some(b, carry):
+        out[pl.ds(pl.multiple_of(b * ROWS * n, ROWS * n), ROWS * n), :] = body(b * ROWS)
+        return carry
+
+    lax.fori_loop(0, n // ROWS, some, 0)
+
+
+def triangle_kernel(n, q, upper, left, right, gain_ref, woh, wol, xhat, rstds, xs, mixed, right_t, tri):
+    c = LANES
+    for p in range(n):
+        right_t[pl.ds(true_row(p, q, upper, n), n, stride=n), :] = right[p * n : (p + 1) * n, :]
+
+    def body(first):
+        return products(
+            n, lambda a, m: row_of(left, (first + a) * n + m), lambda m: right_t[m * n : (m + 1) * n, :]
+        )
+
+    over_rows(n, tri, body)
+    for at in chunks(n * n):
+        found, rstd = norm_lanes(tri[at, :])
+        xhat[at, :] = found
+        rstds[at, :] = jnp.broadcast_to(rstd, found.shape)
+        xs[at, :c], xs[at, c:] = split(found * gain_ref[...])
+    for at in chunks(n * n, DEEP):
+        mixed[at, :] = matmul(xs[at, :], woh[...], wol[...])
+
+
+def gradient_kernel(
+    n, x_ref, y_ref, left, right, z_n, s1_n, s3_n, gate_n, z_f, s1_f, s3_f, gate_f, zown, rown,
+    xhat, rstds, xs, mixed, gain_ref, out_gain_ref, own, other, wnh, wnl, wqh, wql,
+    up_ref, dp_ref, dig_ref, dog_ref, de_ref, dg_ref, do_ref, ms, dh, dl, upd, hidden, dtri, d_left, d_right, grads,
+):
+    c, s = LANES, LANES // 2
+    blk = up_ref.shape[0]
+    q = blk // n
+    upper = x_ref.shape[0] // (2 * blk)
+    chan = lax.axis_index("chan")
+    half = blk // 2
+    part = n * n // 2
+    sides = ((x_ref, gate_n), (y_ref, gate_f))
+
+    for k, (ref, gate) in enumerate(sides):
+        for b, ct in enumerate(cells_from(ref, blk, upper, chan)):
+            here, there = slice(b * half, (b + 1) * half), slice(k * part + b * half, k * part + (b + 1) * half)
+            a, mix = gate[here, :], mixed[there, :]
+            dm = ct * a
+            ms[there, :c], ms[there, c:] = split(dm)
+            dh[there, 4 * c :], dl[there, 4 * c :] = split(dm * mix * (1.0 - a))
+            if k == 0 and b < 2:
+                upd[here, :] = a * mix
+    for at in chunks(n * n, DEEP):
+        hidden[at, :] = matmul(ms[at, :], wqh[...], wql[...])
+    total = jnp.zeros((8, c), F32)
+    for at in chunks(n * n):
+        found, ng = xhat[at, :], hidden[at, :] * out_gain_ref[...]
+        dtri[at, :] = rstds[at, :] * (ng - mean_lanes(ng) - found * mean_lanes(ng * found))
+        total = total + jnp.sum((found * hidden[at, :]).reshape(-1, 8, c), axis=0)
+    dog_ref[...] = jnp.sum(total, axis=0, keepdims=True)[:, :s]
+
+    held = [pl.multiple_of(held_row(m, q, upper, n) * n, n) for m in range(n)]
+
+    def of_left(first):
+        return products(n, lambda a, m: row_of(dtri, (first + a) * n + m), lambda m: right[pl.ds(held[m], n), :])
+
+    def of_right(first):
+        mine = [true_row(first + a, q, upper, n) for a in range(ROWS)]
+        return products(n, lambda a, m: row_of(dtri, m * n + mine[a]), lambda m: left[m * n : (m + 1) * n, :])
+
+    over_rows(n, d_left, of_left)
+    over_rows(n, d_right, of_right)
+    for k, (s1, s3) in enumerate(((s1_n, s3_n), (s1_f, s3_f))):
+        for here in chunks(part):
+            at = slice(k * part + here.start, k * part + here.stop)
+            d, a = d_left[at, :], s1[here, :]
+            dh[at, :c], dl[at, :c] = split(d * a)
+            dh[at, c : 2 * c], dl[at, c : 2 * c] = split(d * left[at, :] * (1.0 - a))
+            d, a = d_right[at, :], s3[here, :]
+            dh[at, 2 * c : 3 * c], dl[at, 2 * c : 3 * c] = split(d * a)
+            dh[at, 3 * c : 4 * c], dl[at, 3 * c : 4 * c] = split(d * right[at, :] * (1.0 - a))
+
+    def turned(at, z):
+        zt = z[...].T
+        wide = dot(zt, dh[at, :])
+        return wide[:c] + (wide[c:] + dot(zt[:c], dl[at, :]))
+
+    def joined(high, low, b):
+        wide = down(high, b)
+        return wide[:, :c] + (wide[:, c:] + down(low, b[:, :c]))
+
+    grads[...] = (turned(slice(0, part), z_n) + turned(slice(part, 2 * part), z_f)).T
+    do_ref[...] = joined(xs[:, :s], xs[:, c : c + s], ms[...])
+
+    gain = gain_ref[...]
+    mine = pl.ds(pl.multiple_of(4 * c + s * chan, s), s)
+    others = pl.ds(pl.multiple_of(4 * c + s * (1 - chan), s), s)
+    dg_ref[...] = grads[mine, :] * gain
+    weighted = own[4 * s : 5 * s, :] * grads[mine, :] + other[4 * s : 5 * s, :] * grads[others, :]
+    for e in range(4):
+        mine, others = grads[e * c : e * c + s, :], grads[e * c + s : (e + 1) * c, :]
+        de_ref[e] = mine * gain
+        at = slice(e * s, (e + 1) * s)
+        weighted = weighted + own[at, :] * mine + other[at, :] * others
+    d_gain = jnp.sum(weighted, axis=0, keepdims=True)
+
+    def own_half(x):
+        return jnp.where(chan == 0, x[:, :s], pltpu.roll(x, s, 1)[:, :s])
+
+    dig_ref[...] = own_half(jnp.broadcast_to(d_gain, (8, c)))[:1]
+    up_ref[...] = own_half(upd[...])
+    dz = dot(dh[:blk, :], wnh[...]) + (dot(dh[:blk, :], wnl[...]) + dot(dl[:blk, :], wnh[...]))
+    zhat = zown[...]
+    dp_ref[...] = own_half(rown[...] * (dz - mean_lanes(dz) - zhat * mean_lanes(dz * zhat)))
+
+
+def rest_kernel(
+    n, blk, x_ref, y_ref, pair_ref, z_n, left_n, s1_n, right_n, s3_n, gate_n, zown, rown, gain_ref, out_gain_ref, own,
+    other, wnh, wnl, wdh, wtl, woh, wol, wqh, wql, up_ref, dp_ref, dig_ref, dog_ref, de_ref, dg_ref, do_ref,
+    left, right, z_f, s1_f, s3_f, gate_f, xhat, rstds, xs, mixed, right_t, tri, proj, *scratch,
+):
+    q, upper, part = blk // n, x_ref.shape[0] // (2 * blk), n * n // 2
+    left[:part, :], right[:part, :] = left_n[...], right_n[...]
+    left_f, right_f = left.at[pl.ds(part, part)], right.at[pl.ds(part, part)]
+    project_kernel(blk, pair_ref, wdh, wtl, z_f, left_f, s1_f, right_f, s3_f, gate_f, None, None, proj)
+    triangle_kernel(n, q, upper, left, right, out_gain_ref, woh, wol, xhat, rstds, xs, mixed, right_t, tri)
+    gradient_kernel(
+        n, x_ref, y_ref, left, right, z_n, s1_n, s3_n, gate_n, z_f, s1_f, s3_f, gate_f, zown, rown,
+        xhat, rstds, xs, mixed, gain_ref, out_gain_ref, own, other, wnh, wnl, wqh, wql,
+        up_ref, dp_ref, dig_ref, dog_ref, de_ref, dg_ref, do_ref, *scratch,
+    )
+
+
+def call(kernel, name, out, scratch, limit, flops, *args):
+    vm = pl.BlockSpec(memory_space=pltpu.VMEM)
+    return pl.pallas_call(
+        kernel,
+        out_shape=[jax.ShapeDtypeStruct(shape, dtype) for shape, dtype in out],
+        in_specs=[vm] * len(args),
+        out_specs=[vm] * len(out),
+        scratch_shapes=[pltpu.VMEM(shape, dtype) for shape, dtype in scratch],
+        compiler_params=pltpu.CompilerParams(vmem_limit_bytes=limit << 20),
+        cost_estimate=pl.CostEstimate(flops=flops, bytes_accessed=1 << 10, transcendentals=0),
+        name=name,
+    )(*args)
+
+
+def gathered(devices, pair, in_gain, output_gain, w_edges, w_gate, w_out, cotangent):
+    s, q, n = pair.shape
+    c = 2 * s
+    blk = q * n
+    cells = n * n
+    upper = devices // 8
+
+    def swap(x, bits):
+        return lax.ppermute(x, ("row", "chan"), [(i, i ^ bits) for i in range(devices)])
+
+    def packed(x):
+        x = jnp.transpose(x, (1, 2, 0)).reshape(2, blk // 2, s)
+        return jnp.concatenate([x[0], x[1]], axis=1)[None]
+
+    w_e = jnp.transpose(w_edges, (0, 2, 1))
+    w_g = jnp.transpose(w_gate)
+    held = jnp.concatenate([packed(pair), packed(cotangent)])
+    gain_row = jnp.pad(output_gain[None], ((0, 7), (0, s)))
+    held, gain_row = lax.optimization_barrier((held, gain_row))
+    (mine,) = call(pack_kernel, "pack", [((6 * s + 8, c), F32)], [], 8, 1 << 20, w_e, w_g, w_out, gain_row)
+    held = jnp.concatenate([held, swap(held, 8)], axis=1)
+    other = swap(mine, 1)
+    held, mine = lax.optimization_barrier((held, mine))
+    bits = 16
+    while bits < devices:
+        held = jnp.concatenate([held, swap(held, bits)], axis=1)
+        bits *= 2
+    parts = [swap(held, bits) for bits in (1, 4, 5)]
+
+    gain = in_gain[None]
+    wnh, wnl, wdh, wtl, woh, wol, wqh, wql, out_gain = call(
+        prepare_kernel,
+        "prepare",
+        [(x, BF16) for x in [(5 * c, c), (5 * c, c), (2 * c, 5 * c), (c, 5 * c), (2 * c, c), (c, c), (2 * c, c), (c, c)]]
+        + [((1, c), F32)],
+        [],
+        8,
+        1 << 20,
+        gain, mine, other,
+    )
+    parts, wdh = lax.optimization_barrier((parts, wdh))
+    held = jnp.concatenate([held, *parts[::-1]], axis=1)
+    pairs, cots = held[0], held[1]
+    pairs_far = swap(pairs, 2)
+    cots_far = swap(cots, 2)
+
+    full, both, wide = ((cells, c), F32), ((cells, 2 * c), BF16), ((cells, 5 * c), BF16)
+    part, own = ((cells // 2, c), F32), ((blk, c), F32)
+    half, many = [((cells // 2, 2 * c), BF16)] + [part] * 5, ((cells // 2, 5 * c), F32)
+    near = call(
+        functools.partial(project_kernel, blk), "project", half + [own] * 2, [many], 16, 1 << 30, pairs, wdh, wtl
+    )
+    up, dp, dig, dog, de, dg, do = call(
+        functools.partial(rest_kernel, n, blk),
+        "rest",
+        [(x, F32) for x in [(blk, s), (blk, s), (1, s), (1, s), (4, s, c), (s, c), (s, c)]],
+        [full, full] + half[:1] + [part] * 3 + [full, full, both, full, full, full, many]
+        + [both, wide, wide, own] + [full] * 4 + [((5 * c, c), F32)],
+        32,
+        1 << 33,
+        cots, cots_far, pairs_far, *near, gain, out_gain, mine, other, wnh, wnl, wdh, wtl, woh, wol, wqh, wql,
+    )
+
+    def pair_of(x):
+        return jnp.transpose(x.reshape(q, n, s), (2, 0, 1))
+
+    return (pair_of(up), pair_of(dp), dig[0], dog[0], jnp.transpose(de, (0, 2, 1)), jnp.transpose(dg), do)
+
+
 def solution(mesh):
+    devices, chans = mesh.size, mesh.shape["chan"]
+
+    def shards(pair, in_gain, output_gain, w_edges, *rest):
+        n, c = pair.shape[2], w_edges.shape[1]
+        fits = (
+            chans == 2 and devices >= 8 and devices & (devices - 1) == 0 and n <= 32 and n % 16 == 0
+            and c == LANES and w_edges.shape[2] * chans == LANES and (pair.shape[1] * n) % 32 == 0
+        )
+        step = functools.partial(gathered, devices) if fits else spread
+        return step(pair, in_gain, output_gain, w_edges, *rest)
+
     placed = (
         P("chan", "row", None),
         P(),
@@ -98,14 +470,6 @@
         shards,
         mesh=mesh,
         in_specs=placed,
-        out_specs=(
-            P("chan", "row", None),
-            P("chan", "row", None),
-            P("chan"),
-            P("chan"),
-            P(None, None, "chan"),
-            P(None, "chan"),
-            P("chan", None),
-        ),
+        out_specs=(placed[0], placed[0], P("chan"), P("chan"), placed[3], placed[4], placed[5]),
         check_vma=False,
     )

time: 285 us -> 31 us (0.11)
  waiting for transfers between devices: 163 us -> 7.51 us
  blocking collectives: 76 us -> 0 us
  between operations: 15.7 us -> 0.75 us
  local copies, waits for them, and re-layouts: 13.8 us -> 0.87 us
  Pallas kernels: 0 us -> 9.77 us
  starting transfers between devices: 3.62 us -> 11.8 us
  matrix products: 7.94 us -> 0 us
  other arithmetic: 3.91 us -> 0.09 us
    psum x2 -> x0, waiting for transfers between devices: 163 us -> none  [shards(): lax.psum((g_in_gain, output_gain_gradient, g_edges, g_gate, g_out), 'row')]
    all_gather x4 -> x0, blocking collectives: 57.8 us -> none  [the longest x1 23.8 us: shards(): right_all = lax.all_gather(right, 'row', axis=1, tiled=True)]
    psum x3 -> x0, blocking collectives: 18.2 us -> none  [the longest x1 8.37 us: shards(): lax.psum(first_part + jnp.einsum('dc,crn->drn', w_gate, d_gate_pre, preci...]
    ppermute x0 -> x8, starting transfers between devices: none -> 11.8 us  [swap(): lax.ppermute(x, ('row', 'chan'), [(i, i ^ bits) for i in range(devices)])]
    unnamed x30 -> x15, local copies, waits for them, and re-layouts: 10 us -> 0.06 us
    pallas_call x0 -> x4, Pallas kernels: none -> 9.77 us  [call(): pl.pallas_call(kernel, out_shape=[jax.ShapeDtypeStruct(shape, dtype) for...]
    dot_general x12 -> x0, matrix products: 7.94 us -> none  [the longest x1 1.77 us: shards(): triangle_product = jnp.einsum('hrk,hjk->hrj', left, right_all, precision=hp)]
    ppermute x0 -> x8, waiting for transfers between devices: none -> 7.51 us  [swap(): lax.ppermute(x, ('row', 'chan'), [(i, i ^ bits) for i in range(devices)])]
  transfers between devices with their start and end apart: 4 -> 8, of which waited for: 2 -> 6; matrix products, arithmetic and copies ran while one was open for 4% -> 0% of each run, Pallas kernels for 0% -> 4%
where the time goes in v3:
time: 31 us; the launch traced here: 30.8 us
  starting transfers between devices  11.8 us (38%)
  Pallas kernels  9.77 us (32%)
  waiting for transfers between devices  7.51 us (24%)
  local copies, waits for them, and re-layouts  0.87 us (3%)
  between operations  0.75 us (2%)
    ppermute x8, starting transfers between devices, swap(): lax.ppermute(x, ('row', 'chan'), [(i, i ^ bits) for i in range(devices)])  11.8 us
    pallas_call x4, Pallas kernels, call(): pl.pallas_call(kernel, out_shape=[jax.ShapeDtypeStruct(shape, dtype) for...  9.77 us
    ppermute x8, waiting for transfers between devices, swap(): lax.ppermute(x, ('row', 'chan'), [(i, i ^ bits) for i in range(devices)])  7.51 us
    squeeze x2, local copies, waits for them, and re-layouts, packed(): return jnp.concatenate([x[0], x[1]], axis=1)[None]  0.75 us
  transfers between devices with their start and end apart: 8, of which 6 were waited for; matrix products, arithmetic and copies ran while one was open for 0% of the time, Pallas kernels for 4%

profile of v3, /device:TPU:0, one launch (start us, length us, event | category | flops | bytes accessed | tf_op | source)
XLA Modules:
  0.0 30.8 jit_solution(12162130955469095201)
XLA Ops:
  0.6 0.0 copy-start.4
  0.6 0.0 copy-start.5
  0.7 0.7 %slice_bitcast_fusion.5 = (f32[32,64]{1,0:T(8,128)S(1)}, f32[32,64]{1,0:T(8,128)S(1)}) fusion(f32[2,32,64]{2,1,0:T(8,128)} %bitcast.36), kind=kLoop, calls=%fused_computation.7 | loop fusion | bytes 32768 | tf_op jit(solution)/shard_map/squeeze | solution.py:391
  1.4 0.0 copy-start
  1.4 0.0 copy-done.4
  1.4 0.0 copy-done.5
  1.4 0.1 maximum_bitcast_fusion
  1.5 0.0 copy-start.1
  1.5 3.1 %collective-permute-start = (f32[2,32,128]{2,1,0:T(8,128)S(1)}, f32[2,32,128]{2,1,0:T(8,128)S(1)}, u32[]{:S(2)}, u32[]{:S(2)}) collective-permute-start(f32[2,32,128]{2,1,0:T(8,128)S(1)} %pad_maximum_fusion.1), channel_id=1, source_target_pairs={{0,8},{1,9},{2,10},{3,11},{4,12},{5,13},{6,14},{7,15},{8,0},{9,1},... | collective-permute-start | bytes 98312 | tf_op jit(solution)/shard_map/ppermute | solution.py:387
  4.6 0.0 copy-done
  4.6 0.0 copy-done.1
  4.6 0.0 copy-done.2
  4.7 1.6 %collective-permute-start.5 = (f32[392,128]{1,0:T(8,128)S(1)}, f32[392,128]{1,0:T(8,128)S(1)}, u32[]{:S(2)}, u32[]{:S(2)}) collective-permute-start(f32[392,128]{1,0:T(8,128)S(1)} %pack.1.mine.own), channel_id=1, source_target_pairs={{0,1},{1,0},{2,3},{3,2},{4,5},{5,4},{6,7},{7,6},{8,9},{9,8},{10,11... | collective-permute-start | bytes 602120 | tf_op jit(solution)/shard_map/ppermute | solution.py:387
  6.2 0.3 %collective-permute-done = f32[2,32,128]{2,1,0:T(8,128)S(1)} collective-permute-done((f32[2,32,128]{2,1,0:T(8,128)S(1)}, f32[2,32,128]{2,1,0:T(8,128)S(1)}, u32[]{:S(2)}, u32[]{:S(2)}) %collective-permute-start) | collective-permute-done | bytes 32800 | tf_op jit(solution)/shard_map/ppermute | solution.py:387
  6.5 3.0 %collective-permute-start.1 = (f32[2,64,128]{2,1,0:T(8,128)S(1)}, f32[2,64,128]{2,1,0:T(8,128)S(1)}, u32[]{:S(2)}, u32[]{:S(2)}) collective-permute-start(f32[2,64,128]{2,1,0:T(8,128)S(1)} %pad_maximum_fusion), channel_id=1, source_target_pairs={{0,16},{1,17},{2,18},{3,19},{4,20},{5,21},{6,22},{7,23},{8,24},{9,... | collective-permute-start | bytes 196616 | tf_op jit(solution)/shard_map/ppermute | solution.py:387
  9.6 2.2 %collective-permute-done.1 = f32[2,64,128]{2,1,0:T(8,128)S(1)} collective-permute-done((f32[2,64,128]{2,1,0:T(8,128)S(1)}, f32[2,64,128]{2,1,0:T(8,128)S(1)}, u32[]{:S(2)}, u32[]{:S(2)}) %collective-permute-start.1) | collective-permute-done | bytes 65568 | tf_op jit(solution)/shard_map/ppermute | solution.py:387
  11.8 0.0 copy-start.3
  11.8 2.8 %collective-permute-start.4 = (f32[2,128,128]{2,1,0:T(8,128)S(1)}, f32[2,128,128]{2,1,0:T(8,128)S(1)}, u32[]{:S(2)}, u32[]{:S(2)}) collective-permute-start(f32[2,128,128]{2,1,0:T(8,128)S(1)} %get-tuple-element.73), channel_id=1, source_target_pairs={{0,5},{1,4},{2,7},{3,6},{4,1},{5,0},{6,3},{7,2},{8,13},{9,12},{10,... | collective-permute-start | bytes 393224 | tf_op jit(solution)/shard_map/ppermute | solution.py:387
  14.7 0.5 %collective-permute-start.3 = (f32[2,128,128]{2,1,0:T(8,128)S(1)}, f32[2,128,128]{2,1,0:T(8,128)S(1)}, u32[]{:S(2)}, u32[]{:S(2)}) collective-permute-start(f32[2,128,128]{2,1,0:T(8,128)S(1)} %get-tuple-element.73), channel_id=1, source_target_pairs={{0,4},{1,5},{2,6},{3,7},{4,0},{5,1},{6,2},{7,3},{8,12},{9,13},{10,... | collective-permute-start | bytes 393224 | tf_op jit(solution)/shard_map/ppermute | solution.py:387
  15.2 0.2 collective-permute-start.2
  15.4 0.0 collective-permute-done.5.other
  15.4 0.0 copy-done.3
  15.4 0.2 prepare.1
  15.6 3.0 %collective-permute-done.4 = f32[2,128,128]{2,1,0:T(8,128)S(1)} collective-permute-done((f32[2,128,128]{2,1,0:T(8,128)S(1)}, f32[2,128,128]{2,1,0:T(8,128)S(1)}, u32[]{:S(2)}, u32[]{:S(2)}) %collective-permute-start.4) | collective-permute-done | bytes 131104 | tf_op jit(solution)/shard_map/ppermute | solution.py:387
  18.5 1.4 %collective-permute-done.3 = f32[2,128,128]{2,1,0:T(8,128)S(1)} collective-permute-done((f32[2,128,128]{2,1,0:T(8,128)S(1)}, f32[2,128,128]{2,1,0:T(8,128)S(1)}, u32[]{:S(2)}, u32[]{:S(2)}) %collective-permute-start.3) | collective-permute-done | bytes 131104 | tf_op jit(solution)/shard_map/ppermute | solution.py:387
  19.9 0.2 collective-permute-done.2
  20.2 0.1 collective-permute-start.7
  20.3 0.5 %collective-permute-start.6 = (f32[512,128]{1,0:T(8,128)S(1)}, f32[512,128]{1,0:T(8,128)S(1)}, u32[]{:S(2)}, u32[]{:S(2)}) collective-permute-start(f32[512,128]{1,0:T(8,128)S(1)} %get-tuple-element.72.x_ref), channel_id=1, source_target_pairs={{0,2},{1,3},{2,0},{3,1},{4,6},{5,7},{6,4},{7,5},{8,10},{9,11},{10,... | collective-permute-start | bytes 786440 | tf_op jit(solution)/shard_map/ppermute | solution.py:387
  20.8 1.0 %project.1 = (bf16[512,256]{1,0:T(8,128)(2,1)S(1)}, f32[512,128]{1,0:T(8,128)S(1)}, f32[512,128]{1,0:T(8,128)S(1)}, f32[512,128]{1,0:T(8,128)S(1)}, f32[512,128]...) custom-call(f32[512,128]{1,0:T(8,128)S(1)} %get-tuple-element.71.x_ref, ...), custom_call_target="tpu_custom_call" | custom-call | flops 1073741824 | bytes 1024 | tf_op jit(solution)/shard_map/project/pallas_call | solution.py:367
  21.8 0.0 collective-permute-done.7.pair_ref
  21.8 0.4 %collective-permute-done.6.y_ref = f32[512,128]{1,0:T(8,128)S(1)} collective-permute-done((f32[512,128]{1,0:T(8,128)S(1)}, f32[512,128]{1,0:T(8,128)S(1)}, u32[]{:S(2)}, u32[]{:S(2)}) %collective-permute-start.6) | collective-permute-done | bytes 262176 | tf_op jit(solution)/shard_map/ppermute | solution.py:387
  22.2 8.6 %rest.1 = (f32[64,64]{1,0:T(8,128)}, f32[64,64]{1,0:T(8,128)}, f32[1,64]{1,0:T(1,128)}, f32[1,64]{1,0:T(1,128)}, f32[4,64,128]{2,1,0:T(8,128)}, /*index=5*/f32[64,128]{1,0:T(8,128)}, f32[64,128]{1,0:T(8,128)}) custom-call(f32[512,128]{1,0:T(8,128)S(1)} %get-tuple-element.72.x_ref, f32[512,128]{1,0:T(8,128)S(1)} %collective-permute-done.6.y_ref, ...), custom_call_target="tpu_custom_call" | custom-call | flops 8589934592 | bytes 1024 | tf_op jit(solution)/shard_map/rest/pallas_call | solution.py:367
  (12 shorter events, 0.1 us)
Async XLA Ops:
  0.6 0.8 %copy-start.4 = (f32[64,2,32]{0,2,1:T(8,128)S(1)}, f32[64,2,32]{0,2,1:T(8,128)}, u32[]{:S(2)}) copy-start(f32[64,2,32]{0,2,1:T(8,128)} %param.13) | copy-start | bytes 49156
  0.6 0.8 %copy-start.5 = (f32[64]{0:T(128)S(1)}, f32[64]{0:T(128)}, u32[]{:S(2)}) copy-start(f32[64]{0:T(128)} %param.9) | copy-start | bytes 772
  1.4 3.2 %copy-start = (f32[4,128,64]{1,2,0:T(8,128)S(1)}, f32[4,128,64]{1,2,0:T(8,128)}, u32[]{:S(2)}) copy-start(f32[4,128,64]{1,2,0:T(8,128)} %param.10) | copy-start | bytes 393220
  1.5 3.1 %copy-start.1 = (f32[128,64]{0,1:T(8,128)S(1)}, f32[128,64]{0,1:T(8,128)}, u32[]{:S(2)}) copy-start(f32[128,64]{0,1:T(8,128)} %param.11) | copy-start | bytes 98308
  1.5 3.1 %copy-start.2 = (f32[64,128]{1,0:T(8,128)S(1)}, f32[64,128]{1,0:T(8,128)}, u32[]{:S(2)}) copy-start(f32[64,128]{1,0:T(8,128)} %wo.1) | copy-start | bytes 98308
  1.5 5.0 %collective-permute-start = (f32[2,32,128]{2,1,0:T(8,128)S(1)}, f32[2,32,128]{2,1,0:T(8,128)S(1)}, u32[]{:S(2)}, u32[]{:S(2)}) collective-permute-start(f32[2,32,128]{2,1,0:T(8,128)S(1)} %pad_maximum_fusion.1), channel_id=1, source_target_pairs={{0,8},{1,9},{2,10},{3,11},{4,12},{5,13},{6,14},{7,15},{8,0},{9,1},... | collective-permute-start | bytes 98312 | tf_op jit(solution)/shard_map/ppermute | solution.py:387
  4.7 10.7 %collective-permute-start.5 = (f32[392,128]{1,0:T(8,128)S(1)}, f32[392,128]{1,0:T(8,128)S(1)}, u32[]{:S(2)}, u32[]{:S(2)}) collective-permute-start(f32[392,128]{1,0:T(8,128)S(1)} %pack.1.mine.own), channel_id=1, source_target_pairs={{0,1},{1,0},{2,3},{3,2},{4,5},{5,4},{6,7},{7,6},{8,9},{9,8},{10,11... | collective-permute-start | bytes 602120 | tf_op jit(solution)/shard_map/ppermute | solution.py:387
  6.5 5.3 %collective-permute-start.1 = (f32[2,64,128]{2,1,0:T(8,128)S(1)}, f32[2,64,128]{2,1,0:T(8,128)S(1)}, u32[]{:S(2)}, u32[]{:S(2)}) collective-permute-start(f32[2,64,128]{2,1,0:T(8,128)S(1)} %pad_maximum_fusion), channel_id=1, source_target_pairs={{0,16},{1,17},{2,18},{3,19},{4,20},{5,21},{6,22},{7,23},{8,24},{9,... | collective-permute-start | bytes 196616 | tf_op jit(solution)/shard_map/ppermute | solution.py:387
  11.8 3.6 %copy-start.3 = (f32[128]{0:T(128)S(1)}, f32[128]{0:T(128)}, u32[]{:S(2)}) copy-start(f32[128]{0:T(128)} %param.8) | copy-start | bytes 1540
  11.8 6.7 %collective-permute-start.4 = (f32[2,128,128]{2,1,0:T(8,128)S(1)}, f32[2,128,128]{2,1,0:T(8,128)S(1)}, u32[]{:S(2)}, u32[]{:S(2)}) collective-permute-start(f32[2,128,128]{2,1,0:T(8,128)S(1)} %get-tuple-element.73), channel_id=1, source_target_pairs={{0,5},{1,4},{2,7},{3,6},{4,1},{5,0},{6,3},{7,2},{8,13},{9,12},{10,... | collective-permute-start | bytes 393224 | tf_op jit(solution)/shard_map/ppermute | solution.py:387
  14.7 5.2 %collective-permute-start.3 = (f32[2,128,128]{2,1,0:T(8,128)S(1)}, f32[2,128,128]{2,1,0:T(8,128)S(1)}, u32[]{:S(2)}, u32[]{:S(2)}) collective-permute-start(f32[2,128,128]{2,1,0:T(8,128)S(1)} %get-tuple-element.73), channel_id=1, source_target_pairs={{0,4},{1,5},{2,6},{3,7},{4,0},{5,1},{6,2},{7,3},{8,12},{9,13},{10,... | collective-permute-start | bytes 393224 | tf_op jit(solution)/shard_map/ppermute | solution.py:387
  15.2 5.0 %collective-permute-start.2 = (f32[2,128,128]{2,1,0:T(8,128)S(1)}, f32[2,128,128]{2,1,0:T(8,128)S(1)}, u32[]{:S(2)}, u32[]{:S(2)}) collective-permute-start(f32[2,128,128]{2,1,0:T(8,128)S(1)} %get-tuple-element.73), channel_id=1, source_target_pairs={{0,1},{1,0},{2,3},{3,2},{4,5},{5,4},{6,7},{7,6},{8,9},{9,8},{10,11... | collective-permute-start | bytes 393224 | tf_op jit(solution)/shard_map/ppermute | solution.py:387
  20.2 1.6 %collective-permute-start.7 = (f32[512,128]{1,0:T(8,128)S(1)}, f32[512,128]{1,0:T(8,128)S(1)}, u32[]{:S(2)}, u32[]{:S(2)}) collective-permute-start(f32[512,128]{1,0:T(8,128)S(1)} %get-tuple-element.71.x_ref), channel_id=1, source_target_pairs={{0,2},{1,3},{2,0},{3,1},{4,6},{5,7},{6,4},{7,5},{8,10},{9,11},{10,... | collective-permute-start | bytes 786440 | tf_op jit(solution)/shard_map/ppermute | solution.py:387
  20.3 1.9 %collective-permute-start.6 = (f32[512,128]{1,0:T(8,128)S(1)}, f32[512,128]{1,0:T(8,128)S(1)}, u32[]{:S(2)}, u32[]{:S(2)}) collective-permute-start(f32[512,128]{1,0:T(8,128)S(1)} %get-tuple-element.72.x_ref), channel_id=1, source_target_pairs={{0,2},{1,3},{2,0},{3,1},{4,6},{5,7},{6,4},{7,5},{8,10},{9,11},{10,... | collective-permute-start | bytes 786440 | tf_op jit(solution)/shard_map/ppermute | solution.py:387

commit v4 on v3

--- a/solution.py
+++ b/solution.py
@@ -12,7 +12,7 @@
 F32 = jnp.float32
 BF16 = jnp.bfloat16
 LANES = 128
-ROWS = 8
+ROWS = 16
 CHUNK = 64
 DEEP = 256
 
@@ -137,8 +137,8 @@
             return ref[pl.ds(pl.multiple_of(at, half), half), :]
 
         first, second = block(chan), block(1 - chan)
-        yield jnp.where(low, first, pltpu.roll(second, LANES // 2, 1))
-        yield jnp.where(low, pltpu.roll(first, LANES // 2, 1), second)
+        yield jnp.where(low, first, second)
+        yield pltpu.roll(jnp.where(low, second, first), LANES // 2, 1)
 
 
 def true_row(p, q, upper, rows):
@@ -394,15 +394,12 @@
     w_g = jnp.transpose(w_gate)
     held = jnp.concatenate([packed(pair), packed(cotangent)])
     gain_row = jnp.pad(output_gain[None], ((0, 7), (0, s)))
-    held, gain_row = lax.optimization_barrier((held, gain_row))
+    held = lax.optimization_barrier(held)
+    held = jnp.where(lax.axis_index("chan") == 0, held, jnp.concatenate([held[..., s:], held[..., :s]], axis=-1))
     (mine,) = call(pack_kernel, "pack", [((6 * s + 8, c), F32)], [], 8, 1 << 20, w_e, w_g, w_out, gain_row)
-    held = jnp.concatenate([held, swap(held, 8)], axis=1)
+    held = jnp.concatenate([held] + [swap(held, 8 * apart) for apart in range(1, upper)], axis=1)
     other = swap(mine, 1)
     held, mine = lax.optimization_barrier((held, mine))
-    bits = 16
-    while bits < devices:
-        held = jnp.concatenate([held, swap(held, bits)], axis=1)
-        bits *= 2
     parts = [swap(held, bits) for bits in (1, 4, 5)]
 
     gain = in_gain[None]

time: 31 us -> 30.3 us (0.977)
  waiting for transfers between devices: 7.51 us -> 6.76 us
  local copies, waits for them, and re-layouts: 0.87 us -> 1.57 us
  Pallas kernels: 9.77 us -> 9.19 us
    ppermute x8 -> x9, waiting for transfers between devices: 7.51 us -> 6.76 us  [swap(): lax.ppermute(x, ('row', 'chan'), [(i, i ^ bits) for i in range(devices)])]
    unnamed x15, local copies, waits for them, and re-layouts: 0.06 us -> 0.7 us
    pallas_call x4, Pallas kernels: 9.77 us -> 9.19 us  [call(): pl.pallas_call(kernel, out_shape=[jax.ShapeDtypeStruct(shape, dtype) for...]
    ppermute x8 -> x9, starting transfers between devices: 11.8 us -> 11.6 us  [swap(): lax.ppermute(x, ('row', 'chan'), [(i, i ^ bits) for i in range(devices)])]
  transfers between devices with their start and end apart: 8 -> 9, of which waited for: 6 -> 5; matrix products, arithmetic and copies ran while one was open for 0% -> 0% of each run, Pallas kernels for 4% -> 4%
where the time goes in v4:
time: 30.3 us; the launch traced here: 30 us
  starting transfers between devices  11.6 us (38%)
  Pallas kernels  9.19 us (30%)
  waiting for transfers between devices  6.76 us (22%)
  local copies, waits for them, and re-layouts  1.57 us (5%)
  between operations  0.76 us (3%)
    ppermute x9, starting transfers between devices, swap(): lax.ppermute(x, ('row', 'chan'), [(i, i ^ bits) for i in range(devices)])  11.6 us
    pallas_call x4, Pallas kernels, call(): pl.pallas_call(kernel, out_shape=[jax.ShapeDtypeStruct(shape, dtype) for...  9.19 us
    ppermute x9, waiting for transfers between devices, swap(): lax.ppermute(x, ('row', 'chan'), [(i, i ^ bits) for i in range(devices)])  6.76 us
    squeeze x2, local copies, waits for them, and re-layouts, packed(): return jnp.concatenate([x[0], x[1]], axis=1)[None]  0.75 us
    unnamed x15, local copies, waits for them, and re-layouts  0.7 us
  transfers between devices with their start and end apart: 9, of which 5 were waited for; matrix products, arithmetic and copies ran while one was open for 0% of the time, Pallas kernels for 4%

profile of v4, /device:TPU:0, one launch (start us, length us, event | category | flops | bytes accessed | tf_op | source)
XLA Modules:
  0.0 30.0 jit_solution(14616425611035893495)
XLA Ops:
  0.6 0.0 copy-start.4
  0.6 0.7 %slice_bitcast_fusion.5 = (f32[32,64]{1,0:T(8,128)S(1)}, f32[32,64]{1,0:T(8,128)S(1)}) fusion(f32[2,32,64]{2,1,0:T(8,128)} %bitcast.36), kind=kLoop, calls=%fused_computation.8 | loop fusion | bytes 32768 | tf_op jit(solution)/shard_map/squeeze | solution.py:391
  1.4 0.0 copy-done.4
  1.4 0.1 maximum_bitcast_fusion
  1.5 0.0 copy-start
  1.5 0.1 fusion
  1.6 0.1 maximum_select_fusion
  1.7 5.1 %collective-permute-start.2 = (f32[2,32,128]{2,1,0:T(8,128)S(1)}, f32[2,32,128]{2,1,0:T(8,128)S(1)}, u32[]{:S(2)}, u32[]{:S(2)}) collective-permute-start(f32[2,32,128]{2,1,0:T(8,128)S(1)} %maximum_select_fusion), channel_id=1, source_target_pairs={{0,24},{1,25},{2,26},{3,27},{4,28},{5,29},{6,30},{7,31},{8,16},{9,... | collective-permute-start | bytes 98312 | tf_op jit(solution)/shard_map/ppermute | solution.py:387
  6.8 0.0 collective-permute-start.1
  6.8 0.6 %collective-permute-start = (f32[2,32,128]{2,1,0:T(8,128)S(1)}, f32[2,32,128]{2,1,0:T(8,128)S(1)}, u32[]{:S(2)}, u32[]{:S(2)}) collective-permute-start(f32[2,32,128]{2,1,0:T(8,128)S(1)} %maximum_select_fusion), channel_id=1, source_target_pairs={{0,8},{1,9},{2,10},{3,11},{4,12},{5,13},{6,14},{7,15},{8,0},{9,1},... | collective-permute-start | bytes 98312 | tf_op jit(solution)/shard_map/ppermute | solution.py:387
  7.4 0.0 copy-done.5
  7.4 0.0 copy-done
  7.5 1.7 %collective-permute-start.6 = (f32[392,128]{1,0:T(8,128)S(1)}, f32[392,128]{1,0:T(8,128)S(1)}, u32[]{:S(2)}, u32[]{:S(2)}) collective-permute-start(f32[392,128]{1,0:T(8,128)S(1)} %pack.1.mine.own), channel_id=1, source_target_pairs={{0,1},{1,0},{2,3},{3,2},{4,5},{5,4},{6,7},{7,6},{8,9},{9,8},{10,11... | collective-permute-start | bytes 602120 | tf_op jit(solution)/shard_map/ppermute | solution.py:387
  9.2 0.0 collective-permute-done.2
  9.2 2.4 %collective-permute-done.1 = f32[2,32,128]{2,1,0:T(8,128)S(1)} collective-permute-done((f32[2,32,128]{2,1,0:T(8,128)S(1)}, f32[2,32,128]{2,1,0:T(8,128)S(1)}, u32[]{:S(2)}, u32[]{:S(2)}) %collective-permute-start.1) | collective-permute-done | bytes 32800 | tf_op jit(solution)/shard_map/ppermute | solution.py:387
  11.6 0.0 collective-permute-done
  11.6 2.5 %collective-permute-start.5 = (f32[2,128,128]{2,1,0:T(8,128)S(1)}, f32[2,128,128]{2,1,0:T(8,128)S(1)}, u32[]{:S(2)}, u32[]{:S(2)}) collective-permute-start(f32[2,128,128]{2,1,0:T(8,128)S(1)} %pad_maximum_fusion), channel_id=1, source_target_pairs={{0,5},{1,4},{2,7},{3,6},{4,1},{5,0},{6,3},{7,2},{8,13},{9,12},{10,... | collective-permute-start | bytes 393224 | tf_op jit(solution)/shard_map/ppermute | solution.py:387
  14.1 0.5 %collective-permute-start.4 = (f32[2,128,128]{2,1,0:T(8,128)S(1)}, f32[2,128,128]{2,1,0:T(8,128)S(1)}, u32[]{:S(2)}, u32[]{:S(2)}) collective-permute-start(f32[2,128,128]{2,1,0:T(8,128)S(1)} %pad_maximum_fusion), channel_id=1, source_target_pairs={{0,4},{1,5},{2,6},{3,7},{4,0},{5,1},{6,2},{7,3},{8,12},{9,13},{10,... | collective-permute-start | bytes 393224 | tf_op jit(solution)/shard_map/ppermute | solution.py:387
  14.6 0.5 %collective-permute-start.3 = (f32[2,128,128]{2,1,0:T(8,128)S(1)}, f32[2,128,128]{2,1,0:T(8,128)S(1)}, u32[]{:S(2)}, u32[]{:S(2)}) collective-permute-start(f32[2,128,128]{2,1,0:T(8,128)S(1)} %pad_maximum_fusion), channel_id=1, source_target_pairs={{0,1},{1,0},{2,3},{3,2},{4,5},{5,4},{6,7},{7,6},{8,9},{9,8},{10,11... | collective-permute-start | bytes 393224 | tf_op jit(solution)/shard_map/ppermute | solution.py:387
  15.2 0.0 copy-start.3
  15.2 0.0 collective-permute-done.6.other
  15.2 0.6 %copy-done.3 = f32[128]{0:T(128)S(1)} copy-done((f32[128]{0:T(128)S(1)}, f32[128]{0:T(128)}, u32[]{:S(2)}) %copy-start.3) | copy-done | bytes 536
  15.8 0.2 prepare.1
  16.0 2.9 %collective-permute-done.5 = f32[2,128,128]{2,1,0:T(8,128)S(1)} collective-permute-done((f32[2,128,128]{2,1,0:T(8,128)S(1)}, f32[2,128,128]{2,1,0:T(8,128)S(1)}, u32[]{:S(2)}, u32[]{:S(2)}) %collective-permute-start.5) | collective-permute-done | bytes 131104 | tf_op jit(solution)/shard_map/ppermute | solution.py:387
  18.9 1.0 %collective-permute-done.4 = f32[2,128,128]{2,1,0:T(8,128)S(1)} collective-permute-done((f32[2,128,128]{2,1,0:T(8,128)S(1)}, f32[2,128,128]{2,1,0:T(8,128)S(1)}, u32[]{:S(2)}, u32[]{:S(2)}) %collective-permute-start.4) | collective-permute-done | bytes 131104 | tf_op jit(solution)/shard_map/ppermute | solution.py:387
  19.8 0.0 collective-permute-done.3
  19.9 0.1 collective-permute-start.8
  20.0 0.5 %collective-permute-start.7 = (f32[512,128]{1,0:T(8,128)S(1)}, f32[512,128]{1,0:T(8,128)S(1)}, u32[]{:S(2)}, u32[]{:S(2)}) collective-permute-start(f32[512,128]{1,0:T(8,128)S(1)} %get-tuple-element.68.x_ref), channel_id=1, source_target_pairs={{0,2},{1,3},{2,0},{3,1},{4,6},{5,7},{6,4},{7,5},{8,10},{9,11},{10,... | collective-permute-start | bytes 786440 | tf_op jit(solution)/shard_map/ppermute | solution.py:387
  20.5 0.9 %project.1 = (bf16[512,256]{1,0:T(8,128)(2,1)S(1)}, f32[512,128]{1,0:T(8,128)S(1)}, f32[512,128]{1,0:T(8,128)S(1)}, f32[512,128]{1,0:T(8,128)S(1)}, f32[512,128]...) custom-call(f32[512,128]{1,0:T(8,128)S(1)} %get-tuple-element.67.x_ref, ...), custom_call_target="tpu_custom_call" | custom-call | flops 1073741824 | bytes 1024 | tf_op jit(solution)/shard_map/project/pallas_call | solution.py:367
  21.4 0.1 collective-permute-done.8.pair_ref
  21.5 0.4 %collective-permute-done.7.y_ref = f32[512,128]{1,0:T(8,128)S(1)} collective-permute-done((f32[512,128]{1,0:T(8,128)S(1)}, f32[512,128]{1,0:T(8,128)S(1)}, u32[]{:S(2)}, u32[]{:S(2)}) %collective-permute-start.7) | collective-permute-done | bytes 262176 | tf_op jit(solution)/shard_map/ppermute | solution.py:387
  21.9 8.1 %rest.1 = (f32[64,64]{1,0:T(8,128)}, f32[64,64]{1,0:T(8,128)}, f32[1,64]{1,0:T(1,128)}, f32[1,64]{1,0:T(1,128)}, f32[4,64,128]{2,1,0:T(8,128)}, /*index=5*/f32[64,128]{1,0:T(8,128)}, f32[64,128]{1,0:T(8,128)}) custom-call(f32[512,128]{1,0:T(8,128)S(1)} %get-tuple-element.68.x_ref, f32[512,128]{1,0:T(8,128)S(1)} %collective-permute-done.7.y_ref, ...), custom_call_target="tpu_custom_call" | custom-call | flops 8589934592 | bytes 1024 | tf_op jit(solution)/shard_map/rest/pallas_call | solution.py:367
  (15 shorter events, 0.1 us)
Async XLA Ops:
  0.6 0.8 %copy-start.4 = (f32[64,2,32]{0,2,1:T(8,128)S(1)}, f32[64,2,32]{0,2,1:T(8,128)}, u32[]{:S(2)}) copy-start(f32[64,2,32]{0,2,1:T(8,128)} %param.13) | copy-start | bytes 49156
  1.5 5.9 %copy-start = (f32[4,128,64]{1,2,0:T(8,128)S(1)}, f32[4,128,64]{1,2,0:T(8,128)}, u32[]{:S(2)}) copy-start(f32[4,128,64]{1,2,0:T(8,128)} %param.10) | copy-start | bytes 393220
  1.6 5.8 %copy-start.1 = (f32[128,64]{0,1:T(8,128)S(1)}, f32[128,64]{0,1:T(8,128)}, u32[]{:S(2)}) copy-start(f32[128,64]{0,1:T(8,128)} %param.11) | copy-start | bytes 98308
  1.6 5.9 %copy-start.2 = (f32[64,128]{1,0:T(8,128)S(1)}, f32[64,128]{1,0:T(8,128)}, u32[]{:S(2)}) copy-start(f32[64,128]{1,0:T(8,128)} %wo.1) | copy-start | bytes 98308
  1.7 5.8 %copy-start.5 = (f32[64]{0:T(128)S(1)}, f32[64]{0:T(128)}, u32[]{:S(2)}) copy-start(f32[64]{0:T(128)} %param.9) | copy-start | bytes 772
  1.7 7.5 %collective-permute-start.2 = (f32[2,32,128]{2,1,0:T(8,128)S(1)}, f32[2,32,128]{2,1,0:T(8,128)S(1)}, u32[]{:S(2)}, u32[]{:S(2)}) collective-permute-start(f32[2,32,128]{2,1,0:T(8,128)S(1)} %maximum_select_fusion), channel_id=1, source_target_pairs={{0,24},{1,25},{2,26},{3,27},{4,28},{5,29},{6,30},{7,31},{8,16},{9,... | collective-permute-start | bytes 98312 | tf_op jit(solution)/shard_map/ppermute | solution.py:387
  6.8 4.8 %collective-permute-start.1 = (f32[2,32,128]{2,1,0:T(8,128)S(1)}, f32[2,32,128]{2,1,0:T(8,128)S(1)}, u32[]{:S(2)}, u32[]{:S(2)}) collective-permute-start(f32[2,32,128]{2,1,0:T(8,128)S(1)} %maximum_select_fusion), channel_id=1, source_target_pairs={{0,16},{1,17},{2,18},{3,19},{4,20},{5,21},{6,22},{7,23},{8,24},{9,... | collective-permute-start | bytes 98312 | tf_op jit(solution)/shard_map/ppermute | solution.py:387
  6.8 4.8 %collective-permute-start = (f32[2,32,128]{2,1,0:T(8,128)S(1)}, f32[2,32,128]{2,1,0:T(8,128)S(1)}, u32[]{:S(2)}, u32[]{:S(2)}) collective-permute-start(f32[2,32,128]{2,1,0:T(8,128)S(1)} %maximum_select_fusion), channel_id=1, source_target_pairs={{0,8},{1,9},{2,10},{3,11},{4,12},{5,13},{6,14},{7,15},{8,0},{9,1},... | collective-permute-start | bytes 98312 | tf_op jit(solution)/shard_map/ppermute | solution.py:387
  7.5 7.7 %collective-permute-start.6 = (f32[392,128]{1,0:T(8,128)S(1)}, f32[392,128]{1,0:T(8,128)S(1)}, u32[]{:S(2)}, u32[]{:S(2)}) collective-permute-start(f32[392,128]{1,0:T(8,128)S(1)} %pack.1.mine.own), channel_id=1, source_target_pairs={{0,1},{1,0},{2,3},{3,2},{4,5},{5,4},{6,7},{7,6},{8,9},{9,8},{10,11... | collective-permute-start | bytes 602120 | tf_op jit(solution)/shard_map/ppermute | solution.py:387
  11.6 7.3 %collective-permute-start.5 = (f32[2,128,128]{2,1,0:T(8,128)S(1)}, f32[2,128,128]{2,1,0:T(8,128)S(1)}, u32[]{:S(2)}, u32[]{:S(2)}) collective-permute-start(f32[2,128,128]{2,1,0:T(8,128)S(1)} %pad_maximum_fusion), channel_id=1, source_target_pairs={{0,5},{1,4},{2,7},{3,6},{4,1},{5,0},{6,3},{7,2},{8,13},{9,12},{10,... | collective-permute-start | bytes 393224 | tf_op jit(solution)/shard_map/ppermute | solution.py:387
  14.1 5.7 %collective-permute-start.4 = (f32[2,128,128]{2,1,0:T(8,128)S(1)}, f32[2,128,128]{2,1,0:T(8,128)S(1)}, u32[]{:S(2)}, u32[]{:S(2)}) collective-permute-start(f32[2,128,128]{2,1,0:T(8,128)S(1)} %pad_maximum_fusion), channel_id=1, source_target_pairs={{0,4},{1,5},{2,6},{3,7},{4,0},{5,1},{6,2},{7,3},{8,12},{9,13},{10,... | collective-permute-start | bytes 393224 | tf_op jit(solution)/shard_map/ppermute | solution.py:387
  14.6 5.2 %collective-permute-start.3 = (f32[2,128,128]{2,1,0:T(8,128)S(1)}, f32[2,128,128]{2,1,0:T(8,128)S(1)}, u32[]{:S(2)}, u32[]{:S(2)}) collective-permute-start(f32[2,128,128]{2,1,0:T(8,128)S(1)} %pad_maximum_fusion), channel_id=1, source_target_pairs={{0,1},{1,0},{2,3},{3,2},{4,5},{5,4},{6,7},{7,6},{8,9},{9,8},{10,11... | collective-permute-start | bytes 393224 | tf_op jit(solution)/shard_map/ppermute | solution.py:387
  15.2 0.7 %copy-start.3 = (f32[128]{0:T(128)S(1)}, f32[128]{0:T(128)}, u32[]{:S(2)}) copy-start(f32[128]{0:T(128)} %param.8) | copy-start | bytes 1540
  19.9 1.6 %collective-permute-start.8 = (f32[512,128]{1,0:T(8,128)S(1)}, f32[512,128]{1,0:T(8,128)S(1)}, u32[]{:S(2)}, u32[]{:S(2)}) collective-permute-start(f32[512,128]{1,0:T(8,128)S(1)} %get-tuple-element.67.x_ref), channel_id=1, source_target_pairs={{0,2},{1,3},{2,0},{3,1},{4,6},{5,7},{6,4},{7,5},{8,10},{9,11},{10,... | collective-permute-start | bytes 786440 | tf_op jit(solution)/shard_map/ppermute | solution.py:387
  20.0 1.9 %collective-permute-start.7 = (f32[512,128]{1,0:T(8,128)S(1)}, f32[512,128]{1,0:T(8,128)S(1)}, u32[]{:S(2)}, u32[]{:S(2)}) collective-permute-start(f32[512,128]{1,0:T(8,128)S(1)} %get-tuple-element.68.x_ref), channel_id=1, source_target_pairs={{0,2},{1,3},{2,0},{3,1},{4,6},{5,7},{6,4},{7,5},{8,10},{9,11},{10,... | collective-permute-start | bytes 786440 | tf_op jit(solution)/shard_map/ppermute | solution.py:387

commit v5 on v4

--- a/solution.py
+++ b/solution.py
@@ -147,13 +147,6 @@
     return (((row // 2) ^ (t % upper * 2 + t // upper)) * 2 + ((row % 2) ^ far)) * q + p % q
 
 
-def held_row(j, q, upper, rows):
-    row = lax.axis_index("row")
-    apart = (row // 2) ^ (j // q // 2)
-    t = apart % 2 * upper + apart // 2
-    return ((row % 2) ^ (j // q % 2)) * (rows // 2) + t * q + j % q
-
-
 def pack_kernel(we, wg, wo, gain, mine):
     s = wg.shape[0]
     for e in range(4):
@@ -195,11 +188,15 @@
     gain_out[:, s:] = other[6 * s : 6 * s + 1, :s]
 
 
-def project_kernel(blk, x_ref, wdh, wtl, z, left, s1, right, s3, gate, zown, rown, proj):
+def project_kernel(blk, whole, wdh, wtl, z, left, s1, right, s3, gate, zown, rown, ct, proj):
     c = LANES
+    x_ref = whole.at[0]
     upper = x_ref.shape[0] // (2 * blk)
     chan = lax.axis_index("chan")
     half = blk // 2
+    if ct is not None:
+        for k, cells in enumerate(cells_from(whole.at[1], blk, upper, chan)):
+            ct[k * half : (k + 1) * half, :] = cells
     for k, cells in enumerate(cells_from(x_ref, blk, upper, chan)):
         at = slice(k * half, (k + 1) * half)
         zhat, rstd = norm_lanes(cells)
@@ -238,10 +235,12 @@
     lax.fori_loop(0, n // ROWS, some, 0)
 
 
-def triangle_kernel(n, q, upper, left, right, gain_ref, woh, wol, xhat, rstds, xs, mixed, right_t, tri):
+def triangle_kernel(n, q, upper, left, sides, gain_ref, woh, wol, xhat, rstds, xs, mixed, right, right_t, tri):
     c = LANES
     for p in range(n):
-        right_t[pl.ds(true_row(p, q, upper, n), n, stride=n), :] = right[p * n : (p + 1) * n, :]
+        ref, at = sides[p // (n // 2)], p % (n // 2) * n
+        right[pl.ds(pl.multiple_of(true_row(p, q, upper, n) * n, n), n), :] = ref[at : at + n, :]
+    right_t[...] = jnp.swapaxes(right[...].reshape(n, n, c), 0, 1).reshape(n * n, c)
 
     def body(first):
         return products(
@@ -259,21 +258,23 @@
 
 
 def gradient_kernel(
-    n, x_ref, y_ref, left, right, z_n, s1_n, s3_n, gate_n, z_f, s1_f, s3_f, gate_f, zown, rown,
+    n, ct_n, y_ref, left, right, z_n, s1_n, right_n, s3_n, gate_n, z_f, s1_f, right_f, s3_f, gate_f, zown, rown,
     xhat, rstds, xs, mixed, gain_ref, out_gain_ref, own, other, wnh, wnl, wqh, wql,
     up_ref, dp_ref, dig_ref, dog_ref, de_ref, dg_ref, do_ref, ms, dh, dl, upd, hidden, dtri, d_left, d_right, grads,
 ):
     c, s = LANES, LANES // 2
     blk = up_ref.shape[0]
     q = blk // n
-    upper = x_ref.shape[0] // (2 * blk)
+    y_ref = y_ref.at[1]
+    upper = y_ref.shape[0] // (2 * blk)
     chan = lax.axis_index("chan")
     half = blk // 2
     part = n * n // 2
-    sides = ((x_ref, gate_n), (y_ref, gate_f))
-
-    for k, (ref, gate) in enumerate(sides):
-        for b, ct in enumerate(cells_from(ref, blk, upper, chan)):
+    near = (ct_n[at, :] for at in chunks(part, half))
+    sides = ((near, gate_n), (cells_from(y_ref, blk, upper, chan), gate_f))
+
+    for k, (cells, gate) in enumerate(sides):
+        for b, ct in enumerate(cells):
             here, there = slice(b * half, (b + 1) * half), slice(k * part + b * half, k * part + (b + 1) * half)
             a, mix = gate[here, :], mixed[there, :]
             dm = ct * a
@@ -290,10 +291,8 @@
         total = total + jnp.sum((found * hidden[at, :]).reshape(-1, 8, c), axis=0)
     dog_ref[...] = jnp.sum(total, axis=0, keepdims=True)[:, :s]
 
-    held = [pl.multiple_of(held_row(m, q, upper, n) * n, n) for m in range(n)]
-
     def of_left(first):
-        return products(n, lambda a, m: row_of(dtri, (first + a) * n + m), lambda m: right[pl.ds(held[m], n), :])
+        return products(n, lambda a, m: row_of(dtri, (first + a) * n + m), lambda m: right[m * n : (m + 1) * n, :])
 
     def of_right(first):
         mine = [true_row(first + a, q, upper, n) for a in range(ROWS)]
@@ -301,7 +300,7 @@
 
     over_rows(n, d_left, of_left)
     over_rows(n, d_right, of_right)
-    for k, (s1, s3) in enumerate(((s1_n, s3_n), (s1_f, s3_f))):
+    for k, (s1, edge, s3) in enumerate(((s1_n, right_n, s3_n), (s1_f, right_f, s3_f))):
         for here in chunks(part):
             at = slice(k * part + here.start, k * part + here.stop)
             d, a = d_left[at, :], s1[here, :]
@@ -309,7 +308,7 @@
             dh[at, c : 2 * c], dl[at, c : 2 * c] = split(d * left[at, :] * (1.0 - a))
             d, a = d_right[at, :], s3[here, :]
             dh[at, 2 * c : 3 * c], dl[at, 2 * c : 3 * c] = split(d * a)
-            dh[at, 3 * c : 4 * c], dl[at, 3 * c : 4 * c] = split(d * right[at, :] * (1.0 - a))
+            dh[at, 3 * c : 4 * c], dl[at, 3 * c : 4 * c] = split(d * edge[here, :] * (1.0 - a))
 
     def turned(at, z):
         zt = z[...].T
@@ -346,17 +345,18 @@
 
 
 def rest_kernel(
-    n, blk, x_ref, y_ref, pair_ref, z_n, left_n, s1_n, right_n, s3_n, gate_n, zown, rown, gain_ref, out_gain_ref, own,
+    n, blk, y_ref, z_n, left_n, s1_n, right_n, s3_n, gate_n, zown, rown, ct_n, gain_ref, out_gain_ref, own,
     other, wnh, wnl, wdh, wtl, woh, wol, wqh, wql, up_ref, dp_ref, dig_ref, dog_ref, de_ref, dg_ref, do_ref,
-    left, right, z_f, s1_f, s3_f, gate_f, xhat, rstds, xs, mixed, right_t, tri, proj, *scratch,
+    left, right, z_f, s1_f, right_f, s3_f, gate_f, xhat, rstds, xs, mixed, right_t, tri, proj, *scratch,
 ):
-    q, upper, part = blk // n, x_ref.shape[0] // (2 * blk), n * n // 2
-    left[:part, :], right[:part, :] = left_n[...], right_n[...]
-    left_f, right_f = left.at[pl.ds(part, part)], right.at[pl.ds(part, part)]
-    project_kernel(blk, pair_ref, wdh, wtl, z_f, left_f, s1_f, right_f, s3_f, gate_f, None, None, proj)
-    triangle_kernel(n, q, upper, left, right, out_gain_ref, woh, wol, xhat, rstds, xs, mixed, right_t, tri)
+    q, upper, part = blk // n, y_ref.shape[1] // (2 * blk), n * n // 2
+    left[:part, :] = left_n[...]
+    left_f = left.at[pl.ds(part, part)]
+    project_kernel(blk, y_ref, wdh, wtl, z_f, left_f, s1_f, right_f, s3_f, gate_f, None, None, None, proj)
+    sides = (right_n, right_f)
+    triangle_kernel(n, q, upper, left, sides, out_gain_ref, woh, wol, xhat, rstds, xs, mixed, right, right_t, tri)
     gradient_kernel(
-        n, x_ref, y_ref, left, right, z_n, s1_n, s3_n, gate_n, z_f, s1_f, s3_f, gate_f, zown, rown,
+        n, ct_n, y_ref, left, right, z_n, s1_n, right_n, s3_n, gate_n, z_f, s1_f, right_f, s3_f, gate_f, zown, rown,
         xhat, rstds, xs, mixed, gain_ref, out_gain_ref, own, other, wnh, wnl, wqh, wql,
         up_ref, dp_ref, dig_ref, dog_ref, de_ref, dg_ref, do_ref, *scratch,
     )
@@ -415,25 +415,23 @@
     )
     parts, wdh = lax.optimization_barrier((parts, wdh))
     held = jnp.concatenate([held, *parts[::-1]], axis=1)
-    pairs, cots = held[0], held[1]
-    pairs_far = swap(pairs, 2)
-    cots_far = swap(cots, 2)
+    far = swap(held, 2)
 
     full, both, wide = ((cells, c), F32), ((cells, 2 * c), BF16), ((cells, 5 * c), BF16)
     part, own = ((cells // 2, c), F32), ((blk, c), F32)
     half, many = [((cells // 2, 2 * c), BF16)] + [part] * 5, ((cells // 2, 5 * c), F32)
     near = call(
-        functools.partial(project_kernel, blk), "project", half + [own] * 2, [many], 16, 1 << 30, pairs, wdh, wtl
+        functools.partial(project_kernel, blk), "project", half + [own] * 2 + [part], [many], 16, 1 << 30, held, wdh, wtl
     )
     up, dp, dig, dog, de, dg, do = call(
         functools.partial(rest_kernel, n, blk),
         "rest",
         [(x, F32) for x in [(blk, s), (blk, s), (1, s), (1, s), (4, s, c), (s, c), (s, c)]],
-        [full, full] + half[:1] + [part] * 3 + [full, full, both, full, full, full, many]
+        [full, full] + half[:1] + [part] * 4 + [full, full, both, full, full, full, many]
         + [both, wide, wide, own] + [full] * 4 + [((5 * c, c), F32)],
         32,
         1 << 33,
-        cots, cots_far, pairs_far, *near, gain, out_gain, mine, other, wnh, wnl, wdh, wtl, woh, wol, wqh, wql,
+        far, *near, gain, out_gain, mine, other, wnh, wnl, wdh, wtl, woh, wol, wqh, wql,
     )
 
     def pair_of(x):

time: 30.3 us -> 29.9 us (0.987)
  starting transfers between devices: 11.6 us -> 11.1 us
  waiting for transfers between devices: 6.76 us -> 7.26 us
  Pallas kernels: 9.19 us -> 8.87 us
    ppermute x9 -> x8, starting transfers between devices: 11.6 us -> 11.1 us  [swap(): lax.ppermute(x, ('row', 'chan'), [(i, i ^ bits) for i in range(devices)])]
    ppermute x9 -> x8, waiting for transfers between devices: 6.76 us -> 7.26 us  [swap(): lax.ppermute(x, ('row', 'chan'), [(i, i ^ bits) for i in range(devices)])]
    pallas_call x4, Pallas kernels: 9.19 us -> 8.87 us  [call(): pl.pallas_call(kernel, out_shape=[jax.ShapeDtypeStruct(shape, dtype) for...]
  transfers between devices with their start and end apart: 9 -> 8, of which waited for: 5 -> 4; matrix products, arithmetic and copies ran while one was open for 0% -> 0% of each run, Pallas kernels for 4% -> 4%
where the time goes in v5:
time: 29.9 us; the launch traced here: 29.7 us
  starting transfers between devices  11.1 us (37%)
  Pallas kernels  8.87 us (30%)
  waiting for transfers between devices  7.26 us (24%)
  local copies, waits for them, and re-layouts  1.53 us (5%)
  between operations  0.76 us (3%)
    ppermute x8, starting transfers between devices, swap(): lax.ppermute(x, ('row', 'chan'), [(i, i ^ bits) for i in range(devices)])  11.1 us
    pallas_call x4, Pallas kernels, call(): pl.pallas_call(kernel, out_shape=[jax.ShapeDtypeStruct(shape, dtype) for...  8.87 us
    ppermute x8, waiting for transfers between devices, swap(): lax.ppermute(x, ('row', 'chan'), [(i, i ^ bits) for i in range(devices)])  7.26 us
    squeeze x2, local copies, waits for them, and re-layouts, packed(): return jnp.concatenate([x[0], x[1]], axis=1)[None]  0.75 us
    unnamed x15, local copies, waits for them, and re-layouts  0.7 us
  transfers between devices with their start and end apart: 8, of which 4 were waited for; matrix products, arithmetic and copies ran while one was open for 0% of the time, Pallas kernels for 4%

profile of v5, /device:TPU:0, one launch (start us, length us, event | category | flops | bytes accessed | tf_op | source)
XLA Modules:
  0.0 29.7 jit_solution(1355234165785121894)
XLA Ops:
  0.6 0.0 copy-start.4
  0.6 0.7 %slice_bitcast_fusion.3 = (f32[32,64]{1,0:T(8,128)S(1)}, f32[32,64]{1,0:T(8,128)S(1)}) fusion(f32[2,32,64]{2,1,0:T(8,128)} %bitcast.32), kind=kLoop, calls=%fused_computation.6 | loop fusion | bytes 32768 | tf_op jit(solution)/shard_map/squeeze | solution.py:391
  1.4 0.0 copy-done.4
  1.4 0.1 maximum_bitcast_fusion
  1.5 0.0 copy-start
  1.5 0.1 fusion
  1.6 0.1 maximum_select_fusion
  1.7 5.1 %collective-permute-start.2 = (f32[2,32,128]{2,1,0:T(8,128)S(1)}, f32[2,32,128]{2,1,0:T(8,128)S(1)}, u32[]{:S(2)}, u32[]{:S(2)}) collective-permute-start(f32[2,32,128]{2,1,0:T(8,128)S(1)} %maximum_select_fusion), channel_id=1, source_target_pairs={{0,24},{1,25},{2,26},{3,27},{4,28},{5,29},{6,30},{7,31},{8,16},{9,... | collective-permute-start | bytes 98312 | tf_op jit(solution)/shard_map/ppermute | solution.py:387
  6.8 0.0 collective-permute-start.1
  6.8 0.6 %collective-permute-start = (f32[2,32,128]{2,1,0:T(8,128)S(1)}, f32[2,32,128]{2,1,0:T(8,128)S(1)}, u32[]{:S(2)}, u32[]{:S(2)}) collective-permute-start(f32[2,32,128]{2,1,0:T(8,128)S(1)} %maximum_select_fusion), channel_id=1, source_target_pairs={{0,8},{1,9},{2,10},{3,11},{4,12},{5,13},{6,14},{7,15},{8,0},{9,1},... | collective-permute-start | bytes 98312 | tf_op jit(solution)/shard_map/ppermute | solution.py:387
  7.4 0.0 copy-done.5
  7.4 0.0 copy-done
  7.4 0.0 copy-done.1
  7.4 0.0 copy-done.2
  7.5 1.7 %collective-permute-start.6 = (f32[392,128]{1,0:T(8,128)S(1)}, f32[392,128]{1,0:T(8,128)S(1)}, u32[]{:S(2)}, u32[]{:S(2)}) collective-permute-start(f32[392,128]{1,0:T(8,128)S(1)} %pack.1.mine.own), channel_id=1, source_target_pairs={{0,1},{1,0},{2,3},{3,2},{4,5},{5,4},{6,7},{7,6},{8,9},{9,8},{10,11... | collective-permute-start | bytes 602120 | tf_op jit(solution)/shard_map/ppermute | solution.py:387
  9.2 0.0 collective-permute-done.2
  9.2 2.4 %collective-permute-done.1 = f32[2,32,128]{2,1,0:T(8,128)S(1)} collective-permute-done((f32[2,32,128]{2,1,0:T(8,128)S(1)}, f32[2,32,128]{2,1,0:T(8,128)S(1)}, u32[]{:S(2)}, u32[]{:S(2)}) %collective-permute-start.1) | collective-permute-done | bytes 32800 | tf_op jit(solution)/shard_map/ppermute | solution.py:387
  11.6 0.0 collective-permute-done
  11.6 2.5 %collective-permute-start.5 = (f32[2,128,128]{2,1,0:T(8,128)S(1)}, f32[2,128,128]{2,1,0:T(8,128)S(1)}, u32[]{:S(2)}, u32[]{:S(2)}) collective-permute-start(f32[2,128,128]{2,1,0:T(8,128)S(1)} %pad_maximum_fusion), channel_id=1, source_target_pairs={{0,5},{1,4},{2,7},{3,6},{4,1},{5,0},{6,3},{7,2},{8,13},{9,12},{10,... | collective-permute-start | bytes 393224 | tf_op jit(solution)/shard_map/ppermute | solution.py:387
  14.1 0.5 %collective-permute-start.4 = (f32[2,128,128]{2,1,0:T(8,128)S(1)}, f32[2,128,128]{2,1,0:T(8,128)S(1)}, u32[]{:S(2)}, u32[]{:S(2)}) collective-permute-start(f32[2,128,128]{2,1,0:T(8,128)S(1)} %pad_maximum_fusion), channel_id=1, source_target_pairs={{0,4},{1,5},{2,6},{3,7},{4,0},{5,1},{6,2},{7,3},{8,12},{9,13},{10,... | collective-permute-start | bytes 393224 | tf_op jit(solution)/shard_map/ppermute | solution.py:387
  14.6 0.5 %collective-permute-start.3 = (f32[2,128,128]{2,1,0:T(8,128)S(1)}, f32[2,128,128]{2,1,0:T(8,128)S(1)}, u32[]{:S(2)}, u32[]{:S(2)}) collective-permute-start(f32[2,128,128]{2,1,0:T(8,128)S(1)} %pad_maximum_fusion), channel_id=1, source_target_pairs={{0,1},{1,0},{2,3},{3,2},{4,5},{5,4},{6,7},{7,6},{8,9},{9,8},{10,11... | collective-permute-start | bytes 393224 | tf_op jit(solution)/shard_map/ppermute | solution.py:387
  15.2 0.0 copy-start.3
  15.2 0.0 collective-permute-done.6.other
  15.2 0.6 %copy-done.3 = f32[128]{0:T(128)S(1)} copy-done((f32[128]{0:T(128)S(1)}, f32[128]{0:T(128)}, u32[]{:S(2)}) %copy-start.3) | copy-done | bytes 536
  15.8 0.2 prepare.1
  16.0 2.9 %collective-permute-done.5 = f32[2,128,128]{2,1,0:T(8,128)S(1)} collective-permute-done((f32[2,128,128]{2,1,0:T(8,128)S(1)}, f32[2,128,128]{2,1,0:T(8,128)S(1)}, u32[]{:S(2)}, u32[]{:S(2)}) %collective-permute-start.5) | collective-permute-done | bytes 131104 | tf_op jit(solution)/shard_map/ppermute | solution.py:387
  18.9 1.0 %collective-permute-done.4 = f32[2,128,128]{2,1,0:T(8,128)S(1)} collective-permute-done((f32[2,128,128]{2,1,0:T(8,128)S(1)}, f32[2,128,128]{2,1,0:T(8,128)S(1)}, u32[]{:S(2)}, u32[]{:S(2)}) %collective-permute-start.4) | collective-permute-done | bytes 131104 | tf_op jit(solution)/shard_map/ppermute | solution.py:387
  19.8 0.0 collective-permute-done.3
  19.9 0.1 collective-permute-start.7
  20.0 0.9 %project.1 = (bf16[512,256]{1,0:T(8,128)(2,1)S(1)}, f32[512,128]{1,0:T(8,128)S(1)}, f32[512,128]{1,0:T(8,128)S(1)}, f32[512,128]{1,0:T(8,128)S(1)}, f32[512,128]...) custom-call(f32[2,512,128]{2,1,0:T(8,128)S(1)} %constant_dynamic-upd, ...), custom_call_target="tpu_custom_call" | custom-call | flops 1073741824 | bytes 1024 | tf_op jit(solution)/shard_map/project/pallas_call | solution.py:367
  20.9 1.0 %collective-permute-done.7.y_ref = f32[2,512,128]{2,1,0:T(8,128)S(1)} collective-permute-done((f32[2,512,128]{2,1,0:T(8,128)S(1)}, f32[2,512,128]{2,1,0:T(8,128)S(1)}, u32[]{:S(2)}, u32[]{:S(2)}) %collective-permute-start.7) | collective-permute-done | bytes 524320 | tf_op jit(solution)/shard_map/ppermute | solution.py:387
  21.9 7.8 %rest.1 = (f32[64,64]{1,0:T(8,128)}, f32[64,64]{1,0:T(8,128)}, f32[1,64]{1,0:T(1,128)}, f32[1,64]{1,0:T(1,128)}, f32[4,64,128]{2,1,0:T(8,128)}, /*index=5*/f32[64,128]{1,0:T(8,128)}, f32[64,128]{1,0:T(8,128)}) custom-call(f32[2,512,128]{2,1,0:T(8,128)S(1)} %collective-permute-done.7.y_ref, bf16[512,256]{1,0:T(8,128)(2,1)S(1)} %get-tuple-element.46.z_n, ...), custom_call_target="tpu_custom_call" | custom-call | flops 8589934592 | bytes 1024 | tf_op jit(solution)/shard_map/rest/pallas_call | solution.py:367
  (12 shorter events, 0.1 us)
Async XLA Ops:
  0.6 0.8 %copy-start.4 = (f32[64,2,32]{0,2,1:T(8,128)S(1)}, f32[64,2,32]{0,2,1:T(8,128)}, u32[]{:S(2)}) copy-start(f32[64,2,32]{0,2,1:T(8,128)} %param.13) | copy-start | bytes 49156
  1.5 5.9 %copy-start = (f32[4,128,64]{1,2,0:T(8,128)S(1)}, f32[4,128,64]{1,2,0:T(8,128)}, u32[]{:S(2)}) copy-start(f32[4,128,64]{1,2,0:T(8,128)} %param.10) | copy-start | bytes 393220
  1.6 5.8 %copy-start.1 = (f32[128,64]{0,1:T(8,128)S(1)}, f32[128,64]{0,1:T(8,128)}, u32[]{:S(2)}) copy-start(f32[128,64]{0,1:T(8,128)} %param.11) | copy-start | bytes 98308
  1.6 5.9 %copy-start.2 = (f32[64,128]{1,0:T(8,128)S(1)}, f32[64,128]{1,0:T(8,128)}, u32[]{:S(2)}) copy-start(f32[64,128]{1,0:T(8,128)} %wo.1) | copy-start | bytes 98308
  1.7 5.8 %copy-start.5 = (f32[64]{0:T(128)S(1)}, f32[64]{0:T(128)}, u32[]{:S(2)}) copy-start(f32[64]{0:T(128)} %param.9) | copy-start | bytes 772
  1.7 7.5 %collective-permute-start.2 = (f32[2,32,128]{2,1,0:T(8,128)S(1)}, f32[2,32,128]{2,1,0:T(8,128)S(1)}, u32[]{:S(2)}, u32[]{:S(2)}) collective-permute-start(f32[2,32,128]{2,1,0:T(8,128)S(1)} %maximum_select_fusion), channel_id=1, source_target_pairs={{0,24},{1,25},{2,26},{3,27},{4,28},{5,29},{6,30},{7,31},{8,16},{9,... | collective-permute-start | bytes 98312 | tf_op jit(solution)/shard_map/ppermute | solution.py:387
  6.8 4.8 %collective-permute-start.1 = (f32[2,32,128]{2,1,0:T(8,128)S(1)}, f32[2,32,128]{2,1,0:T(8,128)S(1)}, u32[]{:S(2)}, u32[]{:S(2)}) collective-permute-start(f32[2,32,128]{2,1,0:T(8,128)S(1)} %maximum_select_fusion), channel_id=1, source_target_pairs={{0,16},{1,17},{2,18},{3,19},{4,20},{5,21},{6,22},{7,23},{8,24},{9,... | collective-permute-start | bytes 98312 | tf_op jit(solution)/shard_map/ppermute | solution.py:387
  6.8 4.8 %collective-permute-start = (f32[2,32,128]{2,1,0:T(8,128)S(1)}, f32[2,32,128]{2,1,0:T(8,128)S(1)}, u32[]{:S(2)}, u32[]{:S(2)}) collective-permute-start(f32[2,32,128]{2,1,0:T(8,128)S(1)} %maximum_select_fusion), channel_id=1, source_target_pairs={{0,8},{1,9},{2,10},{3,11},{4,12},{5,13},{6,14},{7,15},{8,0},{9,1},... | collective-permute-start | bytes 98312 | tf_op jit(solution)/shard_map/ppermute | solution.py:387
  7.5 7.7 %collective-permute-start.6 = (f32[392,128]{1,0:T(8,128)S(1)}, f32[392,128]{1,0:T(8,128)S(1)}, u32[]{:S(2)}, u32[]{:S(2)}) collective-permute-start(f32[392,128]{1,0:T(8,128)S(1)} %pack.1.mine.own), channel_id=1, source_target_pairs={{0,1},{1,0},{2,3},{3,2},{4,5},{5,4},{6,7},{7,6},{8,9},{9,8},{10,11... | collective-permute-start | bytes 602120 | tf_op jit(solution)/shard_map/ppermute | solution.py:387
  11.6 7.3 %collective-permute-start.5 = (f32[2,128,128]{2,1,0:T(8,128)S(1)}, f32[2,128,128]{2,1,0:T(8,128)S(1)}, u32[]{:S(2)}, u32[]{:S(2)}) collective-permute-start(f32[2,128,128]{2,1,0:T(8,128)S(1)} %pad_maximum_fusion), channel_id=1, source_target_pairs={{0,5},{1,4},{2,7},{3,6},{4,1},{5,0},{6,3},{7,2},{8,13},{9,12},{10,... | collective-permute-start | bytes 393224 | tf_op jit(solution)/shard_map/ppermute | solution.py:387
  14.1 5.7 %collective-permute-start.4 = (f32[2,128,128]{2,1,0:T(8,128)S(1)}, f32[2,128,128]{2,1,0:T(8,128)S(1)}, u32[]{:S(2)}, u32[]{:S(2)}) collective-permute-start(f32[2,128,128]{2,1,0:T(8,128)S(1)} %pad_maximum_fusion), channel_id=1, source_target_pairs={{0,4},{1,5},{2,6},{3,7},{4,0},{5,1},{6,2},{7,3},{8,12},{9,13},{10,... | collective-permute-start | bytes 393224 | tf_op jit(solution)/shard_map/ppermute | solution.py:387
  14.6 5.2 %collective-permute-start.3 = (f32[2,128,128]{2,1,0:T(8,128)S(1)}, f32[2,128,128]{2,1,0:T(8,128)S(1)}, u32[]{:S(2)}, u32[]{:S(2)}) collective-permute-start(f32[2,128,128]{2,1,0:T(8,128)S(1)} %pad_maximum_fusion), channel_id=1, source_target_pairs={{0,1},{1,0},{2,3},{3,2},{4,5},{5,4},{6,7},{7,6},{8,9},{9,8},{10,11... | collective-permute-start | bytes 393224 | tf_op jit(solution)/shard_map/ppermute | solution.py:387
  15.2 0.7 %copy-start.3 = (f32[128]{0:T(128)S(1)}, f32[128]{0:T(128)}, u32[]{:S(2)}) copy-start(f32[128]{0:T(128)} %param.8) | copy-start | bytes 1540
  19.9 2.0 %collective-permute-start.7 = (f32[2,512,128]{2,1,0:T(8,128)S(1)}, f32[2,512,128]{2,1,0:T(8,128)S(1)}, u32[]{:S(2)}, u32[]{:S(2)}) collective-permute-start(f32[2,512,128]{2,1,0:T(8,128)S(1)} %constant_dynamic-update-slice_fusion.whole), channel_id=1, source_target_pairs={{0,2},{1,3},{2,0},{3,1},{4,6},{5,7},{6,4},{7,5},{8,10},{9,11},{10,... | collective-permute-start | bytes 1572872 | tf_op jit(solution)/shard_map/ppermute | solution.py:387

commit v6 on v5

--- a/solution.py
+++ b/solution.py
@@ -126,25 +126,28 @@
     return centred * rstd, rstd
 
 
-def cells_from(ref, blk, upper, chan):
+def cells_from(k, own_ref, rest_ref, blk):
     half = blk // 2
-    low = lax.broadcasted_iota(jnp.int32, (half, LANES), 1) < LANES // 2
-    for t in range(2 * upper):
-        own, other = ((0, 3), (2, 1))[t // upper]
-
-        def block(side):
-            at = (t % upper + upper * (own + (other - own) * side)) * half
-            return ref[pl.ds(pl.multiple_of(at, half), half), :]
-
-        first, second = block(chan), block(1 - chan)
-        yield jnp.where(low, first, second)
-        yield pltpu.roll(jnp.where(low, second, first), LANES // 2, 1)
+    across = own_ref.shape[1]
+    low = (lax.broadcasted_iota(jnp.int32, (half, LANES), 1) < LANES // 2) == (lax.axis_index("chan") == 0)
+    for t in range(2 * across // half):
+        at = t * half % across
+
+        def rest(line, at=at):
+            return rest_ref[k, line * across + at : line * across + at + half, :]
+
+        if t * half < across:
+            own, other = own_ref[k, at : at + half, :], rest(2)
+        else:
+            own, other = rest(1), rest(0)
+        yield jnp.where(low, own, other)
+        yield pltpu.roll(jnp.where(low, other, own), LANES // 2, 1)
 
 
 def true_row(p, q, upper, rows):
     row = lax.axis_index("row")
     far, t = p // (rows // 2), p % (rows // 2) // q
-    return (((row // 2) ^ (t % upper * 2 + t // upper)) * 2 + ((row % 2) ^ far)) * q + p % q
+    return (((row // 2) ^ ((upper - t % upper) % upper * 2 + t // upper)) * 2 + ((row % 2) ^ far)) * q + p % q
 
 
 def pack_kernel(we, wg, wo, gain, mine):
@@ -188,16 +191,13 @@
     gain_out[:, s:] = other[6 * s : 6 * s + 1, :s]
 
 
-def project_kernel(blk, whole, wdh, wtl, z, left, s1, right, s3, gate, zown, rown, ct, proj):
+def project_kernel(blk, own_ref, rest_ref, wdh, wtl, z, left, s1, right, s3, gate, zown, rown, ct, proj):
     c = LANES
-    x_ref = whole.at[0]
-    upper = x_ref.shape[0] // (2 * blk)
-    chan = lax.axis_index("chan")
     half = blk // 2
     if ct is not None:
-        for k, cells in enumerate(cells_from(whole.at[1], blk, upper, chan)):
+        for k, cells in enumerate(cells_from(1, own_ref, rest_ref, blk)):
             ct[k * half : (k + 1) * half, :] = cells
-    for k, cells in enumerate(cells_from(x_ref, blk, upper, chan)):
+    for k, cells in enumerate(cells_from(0, own_ref, rest_ref, blk)):
         at = slice(k * half, (k + 1) * half)
         zhat, rstd = norm_lanes(cells)
         z[at, :c], z[at, c:] = split(zhat)
@@ -227,9 +227,11 @@
     return ref[pl.ds(at, 8, stride=0), :]
 
 
-def over_rows(n, out, body):
+def over_rows(n, outs, bodies):
     def some(b, carry):
-        out[pl.ds(pl.multiple_of(b * ROWS * n, ROWS * n), ROWS * n), :] = body(b * ROWS)
+        here = pl.ds(pl.multiple_of(b * ROWS * n, ROWS * n), ROWS * n)
+        for out, body in zip(outs, bodies, strict=True):
+            out[here, :] = body(b * ROWS)
         return carry
 
     lax.fori_loop(0, n // ROWS, some, 0)
@@ -247,7 +249,7 @@
             n, lambda a, m: row_of(left, (first + a) * n + m), lambda m: right_t[m * n : (m + 1) * n, :]
         )
 
-    over_rows(n, tri, body)
+    over_rows(n, (tri,), (body,))
     for at in chunks(n * n):
         found, rstd = norm_lanes(tri[at, :])
         xhat[at, :] = found
@@ -258,20 +260,19 @@
 
 
 def gradient_kernel(
-    n, ct_n, y_ref, left, right, z_n, s1_n, right_n, s3_n, gate_n, z_f, s1_f, right_f, s3_f, gate_f, zown, rown,
+    n, ct_n, far_a, far_b, left, right, z_n, s1_n, right_n, s3_n, gate_n, z_f, s1_f, right_f, s3_f, gate_f, zown, rown,
     xhat, rstds, xs, mixed, gain_ref, out_gain_ref, own, other, wnh, wnl, wqh, wql,
     up_ref, dp_ref, dig_ref, dog_ref, de_ref, dg_ref, do_ref, ms, dh, dl, upd, hidden, dtri, d_left, d_right, grads,
 ):
     c, s = LANES, LANES // 2
     blk = up_ref.shape[0]
     q = blk // n
-    y_ref = y_ref.at[1]
-    upper = y_ref.shape[0] // (2 * blk)
+    upper = 2 * far_a.shape[1] // blk
     chan = lax.axis_index("chan")
     half = blk // 2
     part = n * n // 2
     near = (ct_n[at, :] for at in chunks(part, half))
-    sides = ((near, gate_n), (cells_from(y_ref, blk, upper, chan), gate_f))
+    sides = ((near, gate_n), (cells_from(1, far_a, far_b, blk), gate_f))
 
     for k, (cells, gate) in enumerate(sides):
         for b, ct in enumerate(cells):
@@ -298,8 +299,7 @@
         mine = [true_row(first + a, q, upper, n) for a in range(ROWS)]
         return products(n, lambda a, m: row_of(dtri, m * n + mine[a]), lambda m: left[m * n : (m + 1) * n, :])
 
-    over_rows(n, d_left, of_left)
-    over_rows(n, d_right, of_right)
+    over_rows(n, (d_left, d_right), (of_left, of_right))
     for k, (s1, edge, s3) in enumerate(((s1_n, right_n, s3_n), (s1_f, right_f, s3_f))):
         for here in chunks(part):
             at = slice(k * part + here.start, k * part + here.stop)
@@ -345,18 +345,18 @@
 
 
 def rest_kernel(
-    n, blk, y_ref, z_n, left_n, s1_n, right_n, s3_n, gate_n, zown, rown, ct_n, gain_ref, out_gain_ref, own,
+    n, blk, far_a, far_b, z_n, left_n, s1_n, right_n, s3_n, gate_n, zown, rown, ct_n, gain_ref, out_gain_ref, own,
     other, wnh, wnl, wdh, wtl, woh, wol, wqh, wql, up_ref, dp_ref, dig_ref, dog_ref, de_ref, dg_ref, do_ref,
     left, right, z_f, s1_f, right_f, s3_f, gate_f, xhat, rstds, xs, mixed, right_t, tri, proj, *scratch,
 ):
-    q, upper, part = blk // n, y_ref.shape[1] // (2 * blk), n * n // 2
+    q, upper, part = blk // n, 2 * far_a.shape[1] // blk, n * n // 2
     left[:part, :] = left_n[...]
     left_f = left.at[pl.ds(part, part)]
-    project_kernel(blk, y_ref, wdh, wtl, z_f, left_f, s1_f, right_f, s3_f, gate_f, None, None, None, proj)
+    project_kernel(blk, far_a, far_b, wdh, wtl, z_f, left_f, s1_f, right_f, s3_f, gate_f, None, None, None, proj)
     sides = (right_n, right_f)
     triangle_kernel(n, q, upper, left, sides, out_gain_ref, woh, wol, xhat, rstds, xs, mixed, right, right_t, tri)
     gradient_kernel(
-        n, ct_n, y_ref, left, right, z_n, s1_n, right_n, s3_n, gate_n, z_f, s1_f, right_f, s3_f, gate_f, zown, rown,
+        n, ct_n, far_a, far_b, left, right, z_n, s1_n, right_n, s3_n, gate_n, z_f, s1_f, right_f, s3_f, gate_f, zown, rown,
         xhat, rstds, xs, mixed, gain_ref, out_gain_ref, own, other, wnh, wnl, wqh, wql,
         up_ref, dp_ref, dig_ref, dog_ref, de_ref, dg_ref, do_ref, *scratch,
     )
@@ -397,10 +397,10 @@
     held = lax.optimization_barrier(held)
     held = jnp.where(lax.axis_index("chan") == 0, held, jnp.concatenate([held[..., s:], held[..., :s]], axis=-1))
     (mine,) = call(pack_kernel, "pack", [((6 * s + 8, c), F32)], [], 8, 1 << 20, w_e, w_g, w_out, gain_row)
-    held = jnp.concatenate([held] + [swap(held, 8 * apart) for apart in range(1, upper)], axis=1)
+    held = jnp.concatenate([held] + [swap(held, 8 * apart) for apart in range(upper - 1, 0, -1)], axis=1)
     other = swap(mine, 1)
     held, mine = lax.optimization_barrier((held, mine))
-    parts = [swap(held, bits) for bits in (1, 4, 5)]
+    parts = [swap(held, bits) for bits in (5, 4, 1)]
 
     gain = in_gain[None]
     wnh, wnl, wdh, wtl, woh, wol, wqh, wql, out_gain = call(
@@ -413,15 +413,16 @@
         1 << 20,
         gain, mine, other,
     )
-    parts, wdh = lax.optimization_barrier((parts, wdh))
-    held = jnp.concatenate([held, *parts[::-1]], axis=1)
-    far = swap(held, 2)
+    far_a = swap(held, 2)
+    parts, wdh, far_a = lax.optimization_barrier((parts, wdh, far_a))
+    others = jnp.concatenate(parts, axis=1)
+    far_b = swap(others, 2)
 
     full, both, wide = ((cells, c), F32), ((cells, 2 * c), BF16), ((cells, 5 * c), BF16)
     part, own = ((cells // 2, c), F32), ((blk, c), F32)
     half, many = [((cells // 2, 2 * c), BF16)] + [part] * 5, ((cells // 2, 5 * c), F32)
     near = call(
-        functools.partial(project_kernel, blk), "project", half + [own] * 2 + [part], [many], 16, 1 << 30, held, wdh, wtl
+        functools.partial(project_kernel, blk), "project", half + [own] * 2 + [part], [many], 16, 1 << 30, held, others, wdh, wtl
     )
     up, dp, dig, dog, de, dg, do = call(
         functools.partial(rest_kernel, n, blk),
@@ -431,7 +432,7 @@
         + [both, wide, wide, own] + [full] * 4 + [((5 * c, c), F32)],
         32,
         1 << 33,
-        far, *near, gain, out_gain, mine, other, wnh, wnl, wdh, wtl, woh, wol, wqh, wql,
+        far_a, far_b, *near, gain, out_gain, mine, other, wnh, wnl, wdh, wtl, woh, wol, wqh, wql,
     )
 
     def pair_of(x):
@@ -446,7 +447,7 @@
     def shards(pair, in_gain, output_gain, w_edges, *rest):
         n, c = pair.shape[2], w_edges.shape[1]
         fits = (
-            chans == 2 and devices >= 8 and devices & (devices - 1) == 0 and n <= 32 and n % 16 == 0
+            chans == 2 and devices >= 8 and devices & (devices - 1) == 0 and n <= 32 and n * n % (2 * DEEP) == 0 and n % ROWS == 0
             and c == LANES and w_edges.shape[2] * chans == LANES and (pair.shape[1] * n) % 32 == 0
         )
         step = functools.partial(gathered, devices) if fits else spread

time: 29.9 us -> 29.6 us (0.990)
  local copies, waits for them, and re-layouts: 1.53 us -> 0.89 us
  waiting for transfers between devices: 7.26 us -> 7.74 us
    unnamed x15 -> x14, local copies, waits for them, and re-layouts: 0.7 us -> 0.05 us
    ppermute x8 -> x9, waiting for transfers between devices: 7.26 us -> 7.74 us  [swap(): lax.ppermute(x, ('row', 'chan'), [(i, i ^ bits) for i in range(devices)])]
    ppermute x8 -> x9, starting transfers between devices: 11.1 us -> 11.1 us  [swap(): lax.ppermute(x, ('row', 'chan'), [(i, i ^ bits) for i in range(devices)])]
  transfers between devices with their start and end apart: 8 -> 9, of which waited for: 4 -> 4; matrix products, arithmetic and copies ran while one was open for 0% -> 0% of each run, Pallas kernels for 4% -> 4%
where the time goes in v6:
time: 29.6 us; the launch traced here: 29.4 us
  starting transfers between devices  11.1 us (38%)
  Pallas kernels  8.76 us (30%)
  waiting for transfers between devices  7.74 us (26%)
  local copies, waits for them, and re-layouts  0.89 us (3%)
  between operations  0.75 us (3%)
    ppermute x9, starting transfers between devices, swap(): lax.ppermute(x, ('row', 'chan'), [(i, i ^ bits) for i in range(devices)])  11.1 us
    pallas_call x4, Pallas kernels, call(): pl.pallas_call(kernel, out_shape=[jax.ShapeDtypeStruct(shape, dtype) for...  8.76 us
    ppermute x9, waiting for transfers between devices, swap(): lax.ppermute(x, ('row', 'chan'), [(i, i ^ bits) for i in range(devices)])  7.74 us
    squeeze x2, local copies, waits for them, and re-layouts, packed(): return jnp.concatenate([x[0], x[1]], axis=1)[None]  0.75 us
  transfers between devices with their start and end apart: 9, of which 4 were waited for; matrix products, arithmetic and copies ran while one was open for 0% of the time, Pallas kernels for 4%

profile of v6, /device:TPU:0, one launch (start us, length us, event | category | flops | bytes accessed | tf_op | source)
XLA Modules:
  0.0 29.4 jit_solution(2098764798206587809)
XLA Ops:
  0.6 0.0 copy-start.4
  0.6 0.7 %slice_bitcast_fusion.3 = (f32[32,64]{1,0:T(8,128)S(1)}, f32[32,64]{1,0:T(8,128)S(1)}) fusion(f32[2,32,64]{2,1,0:T(8,128)} %bitcast.32), kind=kLoop, calls=%fused_computation.6 | loop fusion | bytes 32768 | tf_op jit(solution)/shard_map/squeeze | solution.py:391
  1.4 0.0 copy-done.4
  1.4 0.1 maximum_bitcast_fusion
  1.5 0.0 copy-start
  1.5 0.1 fusion
  1.6 0.1 maximum_select_fusion
  1.7 5.1 %collective-permute-start = (f32[2,32,128]{2,1,0:T(8,128)S(1)}, f32[2,32,128]{2,1,0:T(8,128)S(1)}, u32[]{:S(2)}, u32[]{:S(2)}) collective-permute-start(f32[2,32,128]{2,1,0:T(8,128)S(1)} %maximum_select_fusion), channel_id=1, source_target_pairs={{0,24},{1,25},{2,26},{3,27},{4,28},{5,29},{6,30},{7,31},{8,16},{9,... | collective-permute-start | bytes 98312 | tf_op jit(solution)/shard_map/ppermute | solution.py:387
  6.8 0.0 collective-permute-start.1
  6.8 0.6 %collective-permute-start.2 = (f32[2,32,128]{2,1,0:T(8,128)S(1)}, f32[2,32,128]{2,1,0:T(8,128)S(1)}, u32[]{:S(2)}, u32[]{:S(2)}) collective-permute-start(f32[2,32,128]{2,1,0:T(8,128)S(1)} %maximum_select_fusion), channel_id=1, source_target_pairs={{0,8},{1,9},{2,10},{3,11},{4,12},{5,13},{6,14},{7,15},{8,0},{9,1},... | collective-permute-start | bytes 98312 | tf_op jit(solution)/shard_map/ppermute | solution.py:387
  7.4 0.0 copy-done.5
  7.4 0.0 copy-done
  7.4 0.0 copy-done.1
  7.5 1.7 %collective-permute-start.6 = (f32[392,128]{1,0:T(8,128)S(1)}, f32[392,128]{1,0:T(8,128)S(1)}, u32[]{:S(2)}, u32[]{:S(2)}) collective-permute-start(f32[392,128]{1,0:T(8,128)S(1)} %pack.1.mine.own), channel_id=1, source_target_pairs={{0,1},{1,0},{2,3},{3,2},{4,5},{5,4},{6,7},{7,6},{8,9},{9,8},{10,11... | collective-permute-start | bytes 602120 | tf_op jit(solution)/shard_map/ppermute | solution.py:387
  9.2 0.0 collective-permute-done
  9.2 2.4 %collective-permute-done.1 = f32[2,32,128]{2,1,0:T(8,128)S(1)} collective-permute-done((f32[2,32,128]{2,1,0:T(8,128)S(1)}, f32[2,32,128]{2,1,0:T(8,128)S(1)}, u32[]{:S(2)}, u32[]{:S(2)}) %collective-permute-start.1) | collective-permute-done | bytes 32800 | tf_op jit(solution)/shard_map/ppermute | solution.py:387
  11.6 0.0 collective-permute-done.2
  11.6 0.0 copy-start.3
  11.6 2.5 %collective-permute-start.3 = (f32[2,128,128]{2,1,0:T(8,128)S(1)}, f32[2,128,128]{2,1,0:T(8,128)S(1)}, u32[]{:S(2)}, u32[]{:S(2)}) collective-permute-start(f32[2,128,128]{2,1,0:T(8,128)S(1)} %pad_maximum_fusion.own_ref), channel_id=1, source_target_pairs={{0,5},{1,4},{2,7},{3,6},{4,1},{5,0},{6,3},{7,2},{8,13},{9,12},{10,... | collective-permute-start | bytes 393224 | tf_op jit(solution)/shard_map/ppermute | solution.py:387
  14.1 0.5 %collective-permute-start.4 = (f32[2,128,128]{2,1,0:T(8,128)S(1)}, f32[2,128,128]{2,1,0:T(8,128)S(1)}, u32[]{:S(2)}, u32[]{:S(2)}) collective-permute-start(f32[2,128,128]{2,1,0:T(8,128)S(1)} %pad_maximum_fusion.own_ref), channel_id=1, source_target_pairs={{0,4},{1,5},{2,6},{3,7},{4,0},{5,1},{6,2},{7,3},{8,12},{9,13},{10,... | collective-permute-start | bytes 393224 | tf_op jit(solution)/shard_map/ppermute | solution.py:387
  14.6 0.5 %collective-permute-start.5 = (f32[2,128,128]{2,1,0:T(8,128)S(1)}, f32[2,128,128]{2,1,0:T(8,128)S(1)}, u32[]{:S(2)}, u32[]{:S(2)}) collective-permute-start(f32[2,128,128]{2,1,0:T(8,128)S(1)} %pad_maximum_fusion.own_ref), channel_id=1, source_target_pairs={{0,1},{1,0},{2,3},{3,2},{4,5},{5,4},{6,7},{7,6},{8,9},{9,8},{10,11... | collective-permute-start | bytes 393224 | tf_op jit(solution)/shard_map/ppermute | solution.py:387
  15.2 0.0 collective-permute-start.7
  15.2 0.0 collective-permute-done.6.other
  15.2 0.2 prepare.1
  15.4 3.5 %collective-permute-done.3 = f32[2,128,128]{2,1,0:T(8,128)S(1)} collective-permute-done((f32[2,128,128]{2,1,0:T(8,128)S(1)}, f32[2,128,128]{2,1,0:T(8,128)S(1)}, u32[]{:S(2)}, u32[]{:S(2)}) %collective-permute-start.3) | collective-permute-done | bytes 131104 | tf_op jit(solution)/shard_map/ppermute | solution.py:387
  18.9 1.0 %collective-permute-done.4 = f32[2,128,128]{2,1,0:T(8,128)S(1)} collective-permute-done((f32[2,128,128]{2,1,0:T(8,128)S(1)}, f32[2,128,128]{2,1,0:T(8,128)S(1)}, u32[]{:S(2)}, u32[]{:S(2)}) %collective-permute-start.4) | collective-permute-done | bytes 131104 | tf_op jit(solution)/shard_map/ppermute | solution.py:387
  19.8 0.0 collective-permute-done.5
  19.8 0.0 collective-permute-done.7.far_a
  19.9 0.1 collective-permute-start.8
  20.0 0.9 %project.1 = (bf16[512,256]{1,0:T(8,128)(2,1)S(1)}, f32[512,128]{1,0:T(8,128)S(1)}, f32[512,128]{1,0:T(8,128)S(1)}, f32[512,128]{1,0:T(8,128)S(1)}, f32[512,128]...) custom-call(f32[2,128,128]{2,1,0:T(8,128)S(1)} %pad_maximum_fusion.o, ...), custom_call_target="tpu_custom_call" | custom-call | flops 1073741824 | bytes 1024 | tf_op jit(solution)/shard_map/project/pallas_call | solution.py:367
  20.9 0.8 %collective-permute-done.8.far_b = f32[2,384,128]{2,1,0:T(8,128)S(1)} collective-permute-done((f32[2,384,128]{2,1,0:T(8,128)S(1)}, f32[2,384,128]{2,1,0:T(8,128)S(1)}, u32[]{:S(2)}, u32[]{:S(2)}) %collective-permute-start.8) | collective-permute-done | bytes 393248 | tf_op jit(solution)/shard_map/ppermute | solution.py:387
  21.7 7.7 %rest.1 = (f32[64,64]{1,0:T(8,128)}, f32[64,64]{1,0:T(8,128)}, f32[1,64]{1,0:T(1,128)}, f32[1,64]{1,0:T(1,128)}, f32[4,64,128]{2,1,0:T(8,128)}, /*index=5*/f32[64,128]{1,0:T(8,128)}, f32[64,128]{1,0:T(8,128)}) custom-call(f32[2,128,128]{2,1,0:T(8,128)S(1)} %collective-permute-done.7.far_a, f32[2,384,128]{2,1,0:T(8,128)S(1)} %collective-permute-done.8.far_b, ...), custom_call_target="tpu_custom_call" | custom-call | flops 8589934592 | bytes 1024 | tf_op jit(solution)/shard_map/rest/pallas_call | solution.py:367
  (13 shorter events, 0.1 us)
Async XLA Ops:
  0.6 0.8 %copy-start.4 = (f32[64,2,32]{0,2,1:T(8,128)S(1)}, f32[64,2,32]{0,2,1:T(8,128)}, u32[]{:S(2)}) copy-start(f32[64,2,32]{0,2,1:T(8,128)} %param.13) | copy-start | bytes 49156
  1.5 5.9 %copy-start = (f32[4,128,64]{1,2,0:T(8,128)S(1)}, f32[4,128,64]{1,2,0:T(8,128)}, u32[]{:S(2)}) copy-start(f32[4,128,64]{1,2,0:T(8,128)} %param.10) | copy-start | bytes 393220
  1.6 5.8 %copy-start.1 = (f32[128,64]{0,1:T(8,128)S(1)}, f32[128,64]{0,1:T(8,128)}, u32[]{:S(2)}) copy-start(f32[128,64]{0,1:T(8,128)} %param.11) | copy-start | bytes 98308
  1.6 5.9 %copy-start.2 = (f32[64,128]{1,0:T(8,128)S(1)}, f32[64,128]{1,0:T(8,128)}, u32[]{:S(2)}) copy-start(f32[64,128]{1,0:T(8,128)} %wo.1) | copy-start | bytes 98308
  1.7 5.8 %copy-start.5 = (f32[64]{0:T(128)S(1)}, f32[64]{0:T(128)}, u32[]{:S(2)}) copy-start(f32[64]{0:T(128)} %param.9) | copy-start | bytes 772
  1.7 7.5 %collective-permute-start = (f32[2,32,128]{2,1,0:T(8,128)S(1)}, f32[2,32,128]{2,1,0:T(8,128)S(1)}, u32[]{:S(2)}, u32[]{:S(2)}) collective-permute-start(f32[2,32,128]{2,1,0:T(8,128)S(1)} %maximum_select_fusion), channel_id=1, source_target_pairs={{0,24},{1,25},{2,26},{3,27},{4,28},{5,29},{6,30},{7,31},{8,16},{9,... | collective-permute-start | bytes 98312 | tf_op jit(solution)/shard_map/ppermute | solution.py:387
  6.8 4.8 %collective-permute-start.1 = (f32[2,32,128]{2,1,0:T(8,128)S(1)}, f32[2,32,128]{2,1,0:T(8,128)S(1)}, u32[]{:S(2)}, u32[]{:S(2)}) collective-permute-start(f32[2,32,128]{2,1,0:T(8,128)S(1)} %maximum_select_fusion), channel_id=1, source_target_pairs={{0,16},{1,17},{2,18},{3,19},{4,20},{5,21},{6,22},{7,23},{8,24},{9,... | collective-permute-start | bytes 98312 | tf_op jit(solution)/shard_map/ppermute | solution.py:387
  6.8 4.8 %collective-permute-start.2 = (f32[2,32,128]{2,1,0:T(8,128)S(1)}, f32[2,32,128]{2,1,0:T(8,128)S(1)}, u32[]{:S(2)}, u32[]{:S(2)}) collective-permute-start(f32[2,32,128]{2,1,0:T(8,128)S(1)} %maximum_select_fusion), channel_id=1, source_target_pairs={{0,8},{1,9},{2,10},{3,11},{4,12},{5,13},{6,14},{7,15},{8,0},{9,1},... | collective-permute-start | bytes 98312 | tf_op jit(solution)/shard_map/ppermute | solution.py:387
  7.5 7.7 %collective-permute-start.6 = (f32[392,128]{1,0:T(8,128)S(1)}, f32[392,128]{1,0:T(8,128)S(1)}, u32[]{:S(2)}, u32[]{:S(2)}) collective-permute-start(f32[392,128]{1,0:T(8,128)S(1)} %pack.1.mine.own), channel_id=1, source_target_pairs={{0,1},{1,0},{2,3},{3,2},{4,5},{5,4},{6,7},{7,6},{8,9},{9,8},{10,11... | collective-permute-start | bytes 602120 | tf_op jit(solution)/shard_map/ppermute | solution.py:387
  11.6 3.6 %copy-start.3 = (f32[128]{0:T(128)S(1)}, f32[128]{0:T(128)}, u32[]{:S(2)}) copy-start(f32[128]{0:T(128)} %param.8) | copy-start | bytes 1540
  11.6 7.3 %collective-permute-start.3 = (f32[2,128,128]{2,1,0:T(8,128)S(1)}, f32[2,128,128]{2,1,0:T(8,128)S(1)}, u32[]{:S(2)}, u32[]{:S(2)}) collective-permute-start(f32[2,128,128]{2,1,0:T(8,128)S(1)} %pad_maximum_fusion.own_ref), channel_id=1, source_target_pairs={{0,5},{1,4},{2,7},{3,6},{4,1},{5,0},{6,3},{7,2},{8,13},{9,12},{10,... | collective-permute-start | bytes 393224 | tf_op jit(solution)/shard_map/ppermute | solution.py:387
  14.1 5.7 %collective-permute-start.4 = (f32[2,128,128]{2,1,0:T(8,128)S(1)}, f32[2,128,128]{2,1,0:T(8,128)S(1)}, u32[]{:S(2)}, u32[]{:S(2)}) collective-permute-start(f32[2,128,128]{2,1,0:T(8,128)S(1)} %pad_maximum_fusion.own_ref), channel_id=1, source_target_pairs={{0,4},{1,5},{2,6},{3,7},{4,0},{5,1},{6,2},{7,3},{8,12},{9,13},{10,... | collective-permute-start | bytes 393224 | tf_op jit(solution)/shard_map/ppermute | solution.py:387
  14.6 5.2 %collective-permute-start.5 = (f32[2,128,128]{2,1,0:T(8,128)S(1)}, f32[2,128,128]{2,1,0:T(8,128)S(1)}, u32[]{:S(2)}, u32[]{:S(2)}) collective-permute-start(f32[2,128,128]{2,1,0:T(8,128)S(1)} %pad_maximum_fusion.own_ref), channel_id=1, source_target_pairs={{0,1},{1,0},{2,3},{3,2},{4,5},{5,4},{6,7},{7,6},{8,9},{9,8},{10,11... | collective-permute-start | bytes 393224 | tf_op jit(solution)/shard_map/ppermute | solution.py:387
  15.2 4.7 %collective-permute-start.7 = (f32[2,128,128]{2,1,0:T(8,128)S(1)}, f32[2,128,128]{2,1,0:T(8,128)S(1)}, u32[]{:S(2)}, u32[]{:S(2)}) collective-permute-start(f32[2,128,128]{2,1,0:T(8,128)S(1)} %pad_maximum_fusion.own_ref), channel_id=1, source_target_pairs={{0,2},{1,3},{2,0},{3,1},{4,6},{5,7},{6,4},{7,5},{8,10},{9,11},{10,... | collective-permute-start | bytes 393224 | tf_op jit(solution)/shard_map/ppermute | solution.py:387
  19.9 1.8 %collective-permute-start.8 = (f32[2,384,128]{2,1,0:T(8,128)S(1)}, f32[2,384,128]{2,1,0:T(8,128)S(1)}, u32[]{:S(2)}, u32[]{:S(2)}) collective-permute-start(f32[2,384,128]{2,1,0:T(8,128)S(1)} %constant_dynamic-update-slice_fusion.rest_ref), channel_id=1, source_target_pairs={{0,2},{1,3},{2,0},{3,1},{4,6},{5,7},{6,4},{7,5},{8,10},{9,11},{10,... | collective-permute-start | bytes 1179656 | tf_op jit(solution)/shard_map/ppermute | solution.py:387

commit v7 on v6

--- a/solution.py
+++ b/solution.py
@@ -104,8 +104,9 @@
     return jnp.dot(a, b, preferred_element_type=F32)
 
 
-def matmul(a, twice_high, low):
-    return dot(a, twice_high) + dot(a[:, :LANES], low)
+def put_split(ref, at, x):
+    high, low = split(x)
+    ref[at, :LANES], ref[at, LANES : 2 * LANES], ref[at, 2 * LANES :] = high, low, high
 
 
 def down(a, b):
@@ -159,7 +160,7 @@
     mine[6 * s :, :] = gain[...]
 
 
-def prepare_kernel(gain_ref, mine, other, wnh, wnl, wdh, wtl, woh, wol, wqh, wql, gain_out):
+def prepare_kernel(gain_ref, mine, other, wnh, wnl, wdh, woh, wqh, gain_out):
     c = LANES
     s = c // 2
     chan = lax.axis_index("chan")
@@ -172,26 +173,23 @@
     def put(k, whole):
         at = slice(k * c, (k + 1) * c)
         wnh[at, :], wnl[at, :] = split(whole)
-        high, wtl[:, at] = split(whole.T)
-        wdh[:c, at] = high
-        wdh[c:, at] = high
+        high, low = split(whole.T)
+        wdh[:c, at], wdh[c : 2 * c, at], wdh[2 * c :, at] = high, high, low
 
     for e in range(4):
         put(e, jnp.concatenate(both(e), axis=0) * gain)
     a, b = both(4)
     put(4, jnp.concatenate([jnp.where(chan == 0, a, b), jnp.where(chan == 0, b, a)], axis=0) * gain)
     whole = jnp.concatenate(both(5), axis=0)
-    high, wol[...] = split(whole)
-    woh[:c, :] = high
-    woh[c:, :] = high
-    high, wql[...] = split(whole.T)
-    wqh[:c, :] = high
-    wqh[c:, :] = high
+    high, low = split(whole)
+    woh[:c, :], woh[c : 2 * c, :], woh[2 * c :, :] = high, high, low
+    high, low = split(whole.T)
+    wqh[:c, :], wqh[c : 2 * c, :], wqh[2 * c :, :] = high, high, low
     gain_out[:, :s] = mine[6 * s : 6 * s + 1, :s]
     gain_out[:, s:] = other[6 * s : 6 * s + 1, :s]
 
 
-def project_kernel(blk, own_ref, rest_ref, wdh, wtl, z, left, s1, right, s3, gate, zown, rown, ct, proj):
+def project_kernel(blk, own_ref, rest_ref, wdh, z, left, s1, right, s3, gate, zown, rown, ct, proj):
     c = LANES
     half = blk // 2
     if ct is not None:
@@ -200,12 +198,12 @@
     for k, cells in enumerate(cells_from(0, own_ref, rest_ref, blk)):
         at = slice(k * half, (k + 1) * half)
         zhat, rstd = norm_lanes(cells)
-        z[at, :c], z[at, c:] = split(zhat)
+        put_split(z, at, zhat)
         if k < 2 and zown is not None:
             zown[at, :] = zhat
             rown[at, :] = jnp.broadcast_to(rstd, zhat.shape)
     for at in chunks(z.shape[0], DEEP):
-        proj[at, :] = matmul(z[at, :], wdh[...], wtl[...])
+        proj[at, :] = dot(z[at, :], wdh[...])
     for at in chunks(z.shape[0]):
         a = jax.nn.sigmoid(proj[at, c : 2 * c])
         left[at, :], s1[at, :] = a * proj[at, :c], a
@@ -237,7 +235,7 @@
     lax.fori_loop(0, n // ROWS, some, 0)
 
 
-def triangle_kernel(n, q, upper, left, sides, gain_ref, woh, wol, xhat, rstds, xs, mixed, right, right_t, tri):
+def triangle_kernel(n, q, upper, left, sides, gain_ref, woh, xhat, rstds, xs, mixed, right, right_t, tri):
     c = LANES
     for p in range(n):
         ref, at = sides[p // (n // 2)], p % (n // 2) * n
@@ -254,14 +252,14 @@
         found, rstd = norm_lanes(tri[at, :])
         xhat[at, :] = found
         rstds[at, :] = jnp.broadcast_to(rstd, found.shape)
-        xs[at, :c], xs[at, c:] = split(found * gain_ref[...])
+        put_split(xs, at, found * gain_ref[...])
     for at in chunks(n * n, DEEP):
-        mixed[at, :] = matmul(xs[at, :], woh[...], wol[...])
+        mixed[at, :] = dot(xs[at, :], woh[...])
 
 
 def gradient_kernel(
     n, ct_n, far_a, far_b, left, right, z_n, s1_n, right_n, s3_n, gate_n, z_f, s1_f, right_f, s3_f, gate_f, zown, rown,
-    xhat, rstds, xs, mixed, gain_ref, out_gain_ref, own, other, wnh, wnl, wqh, wql,
+    xhat, rstds, xs, mixed, gain_ref, out_gain_ref, own, other, wnh, wnl, wqh,
     up_ref, dp_ref, dig_ref, dog_ref, de_ref, dg_ref, do_ref, ms, dh, dl, upd, hidden, dtri, d_left, d_right, grads,
 ):
     c, s = LANES, LANES // 2
@@ -279,12 +277,12 @@
             here, there = slice(b * half, (b + 1) * half), slice(k * part + b * half, k * part + (b + 1) * half)
             a, mix = gate[here, :], mixed[there, :]
             dm = ct * a
-            ms[there, :c], ms[there, c:] = split(dm)
+            put_split(ms, there, dm)
             dh[there, 4 * c :], dl[there, 4 * c :] = split(dm * mix * (1.0 - a))
             if k == 0 and b < 2:
                 upd[here, :] = a * mix
     for at in chunks(n * n, DEEP):
-        hidden[at, :] = matmul(ms[at, :], wqh[...], wql[...])
+        hidden[at, :] = dot(ms[at, :], wqh[...])
     total = jnp.zeros((8, c), F32)
     for at in chunks(n * n):
         found, ng = xhat[at, :], hidden[at, :] * out_gain_ref[...]
@@ -311,7 +309,7 @@
             dh[at, 3 * c : 4 * c], dl[at, 3 * c : 4 * c] = split(d * edge[here, :] * (1.0 - a))
 
     def turned(at, z):
-        zt = z[...].T
+        zt = z[:, : 2 * c].T
         wide = dot(zt, dh[at, :])
         return wide[:c] + (wide[c:] + dot(zt[:c], dl[at, :]))
 
@@ -320,7 +318,7 @@
         return wide[:, :c] + (wide[:, c:] + down(low, b[:, :c]))
 
     grads[...] = (turned(slice(0, part), z_n) + turned(slice(part, 2 * part), z_f)).T
-    do_ref[...] = joined(xs[:, :s], xs[:, c : c + s], ms[...])
+    do_ref[...] = joined(xs[:, :s], xs[:, c : c + s], ms[:, : 2 * c])
 
     gain = gain_ref[...]
     mine = pl.ds(pl.multiple_of(4 * c + s * chan, s), s)
@@ -346,18 +344,18 @@
 
 def rest_kernel(
     n, blk, far_a, far_b, z_n, left_n, s1_n, right_n, s3_n, gate_n, zown, rown, ct_n, gain_ref, out_gain_ref, own,
-    other, wnh, wnl, wdh, wtl, woh, wol, wqh, wql, up_ref, dp_ref, dig_ref, dog_ref, de_ref, dg_ref, do_ref,
+    other, wnh, wnl, wdh, woh, wqh, up_ref, dp_ref, dig_ref, dog_ref, de_ref, dg_ref, do_ref,
     left, right, z_f, s1_f, right_f, s3_f, gate_f, xhat, rstds, xs, mixed, right_t, tri, proj, *scratch,
 ):
     q, upper, part = blk // n, 2 * far_a.shape[1] // blk, n * n // 2
     left[:part, :] = left_n[...]
     left_f = left.at[pl.ds(part, part)]
-    project_kernel(blk, far_a, far_b, wdh, wtl, z_f, left_f, s1_f, right_f, s3_f, gate_f, None, None, None, proj)
+    project_kernel(blk, far_a, far_b, wdh, z_f, left_f, s1_f, right_f, s3_f, gate_f, None, None, None, proj)
     sides = (right_n, right_f)
-    triangle_kernel(n, q, upper, left, sides, out_gain_ref, woh, wol, xhat, rstds, xs, mixed, right, right_t, tri)
+    triangle_kernel(n, q, upper, left, sides, out_gain_ref, woh, xhat, rstds, xs, mixed, right, right_t, tri)
     gradient_kernel(
         n, ct_n, far_a, far_b, left, right, z_n, s1_n, right_n, s3_n, gate_n, z_f, s1_f, right_f, s3_f, gate_f, zown, rown,
-        xhat, rstds, xs, mixed, gain_ref, out_gain_ref, own, other, wnh, wnl, wqh, wql,
+        xhat, rstds, xs, mixed, gain_ref, out_gain_ref, own, other, wnh, wnl, wqh,
         up_ref, dp_ref, dig_ref, dog_ref, de_ref, dg_ref, do_ref, *scratch,
     )
 
@@ -403,10 +401,10 @@
     parts = [swap(held, bits) for bits in (5, 4, 1)]
 
     gain = in_gain[None]
-    wnh, wnl, wdh, wtl, woh, wol, wqh, wql, out_gain = call(
+    wnh, wnl, wdh, woh, wqh, out_gain = call(
         prepare_kernel,
         "prepare",
-        [(x, BF16) for x in [(5 * c, c), (5 * c, c), (2 * c, 5 * c), (c, 5 * c), (2 * c, c), (c, c), (2 * c, c), (c, c)]]
+        [(x, BF16) for x in [(5 * c, c), (5 * c, c), (3 * c, 5 * c), (3 * c, c), (3 * c, c)]]
         + [((1, c), F32)],
         [],
         8,
@@ -418,11 +416,11 @@
     others = jnp.concatenate(parts, axis=1)
     far_b = swap(others, 2)
 
-    full, both, wide = ((cells, c), F32), ((cells, 2 * c), BF16), ((cells, 5 * c), BF16)
+    full, both, wide = ((cells, c), F32), ((cells, 3 * c), BF16), ((cells, 5 * c), BF16)
     part, own = ((cells // 2, c), F32), ((blk, c), F32)
-    half, many = [((cells // 2, 2 * c), BF16)] + [part] * 5, ((cells // 2, 5 * c), F32)
+    half, many = [((cells // 2, 3 * c), BF16)] + [part] * 5, ((cells // 2, 5 * c), F32)
     near = call(
-        functools.partial(project_kernel, blk), "project", half + [own] * 2 + [part], [many], 16, 1 << 30, held, others, wdh, wtl
+        functools.partial(project_kernel, blk), "project", half + [own] * 2 + [part], [many], 16, 1 << 30, held, others, wdh
     )
     up, dp, dig, dog, de, dg, do = call(
         functools.partial(rest_kernel, n, blk),
@@ -432,7 +430,7 @@
         + [both, wide, wide, own] + [full] * 4 + [((5 * c, c), F32)],
         32,
         1 << 33,
-        far_a, far_b, *near, gain, out_gain, mine, other, wnh, wnl, wdh, wtl, woh, wol, wqh, wql,
+        far_a, far_b, *near, gain, out_gain, mine, other, wnh, wnl, wdh, woh, wqh,
     )
 
     def pair_of(x):

time: 29.6 us -> 29.7 us (level)
  no operation moved by 1% of the time
where the time goes in v7:
time: 29.7 us; the launch traced here: 29.4 us
  starting transfers between devices  11.1 us (37%)
  Pallas kernels  8.99 us (30%)
  waiting for transfers between devices  7.57 us (25%)
  local copies, waits for them, and re-layouts  0.89 us (3%)
  between operations  0.75 us (3%)
    ppermute x9, starting transfers between devices, swap(): lax.ppermute(x, ('row', 'chan'), [(i, i ^ bits) for i in range(devices)])  11.1 us
    pallas_call x4, Pallas kernels, call(): pl.pallas_call(kernel, out_shape=[jax.ShapeDtypeStruct(shape, dtype) for...  8.99 us
    ppermute x9, waiting for transfers between devices, swap(): lax.ppermute(x, ('row', 'chan'), [(i, i ^ bits) for i in range(devices)])  7.57 us
    squeeze x2, local copies, waits for them, and re-layouts, packed(): return jnp.concatenate([x[0], x[1]], axis=1)[None]  0.75 us
  transfers between devices with their start and end apart: 9, of which 4 were waited for; matrix products, arithmetic and copies ran while one was open for 0% of the time, Pallas kernels for 4%

profile of v7, /device:TPU:0, one launch (start us, length us, event | category | flops | bytes accessed | tf_op | source)
XLA Modules:
  0.0 29.4 jit_solution(8452705790897616939)
XLA Ops:
  0.6 0.0 copy-start.4
  0.6 0.7 %slice_bitcast_fusion.3 = (f32[32,64]{1,0:T(8,128)S(1)}, f32[32,64]{1,0:T(8,128)S(1)}) fusion(f32[2,32,64]{2,1,0:T(8,128)} %bitcast.32), kind=kLoop, calls=%fused_computation.6 | loop fusion | bytes 32768 | tf_op jit(solution)/shard_map/squeeze | solution.py:389
  1.4 0.0 copy-done.4
  1.4 0.1 maximum_bitcast_fusion
  1.5 0.0 copy-start
  1.5 0.1 fusion
  1.6 0.1 maximum_select_fusion
  1.7 5.1 %collective-permute-start = (f32[2,32,128]{2,1,0:T(8,128)S(1)}, f32[2,32,128]{2,1,0:T(8,128)S(1)}, u32[]{:S(2)}, u32[]{:S(2)}) collective-permute-start(f32[2,32,128]{2,1,0:T(8,128)S(1)} %maximum_select_fusion), channel_id=1, source_target_pairs={{0,24},{1,25},{2,26},{3,27},{4,28},{5,29},{6,30},{7,31},{8,16},{9,... | collective-permute-start | bytes 98312 | tf_op jit(solution)/shard_map/ppermute | solution.py:385
  6.8 0.0 collective-permute-start.1
  6.8 0.6 %collective-permute-start.2 = (f32[2,32,128]{2,1,0:T(8,128)S(1)}, f32[2,32,128]{2,1,0:T(8,128)S(1)}, u32[]{:S(2)}, u32[]{:S(2)}) collective-permute-start(f32[2,32,128]{2,1,0:T(8,128)S(1)} %maximum_select_fusion), channel_id=1, source_target_pairs={{0,8},{1,9},{2,10},{3,11},{4,12},{5,13},{6,14},{7,15},{8,0},{9,1},... | collective-permute-start | bytes 98312 | tf_op jit(solution)/shard_map/ppermute | solution.py:385
  7.4 0.0 copy-done.5
  7.4 0.0 copy-done
  7.4 0.0 copy-done.1
  7.5 1.7 %collective-permute-start.6 = (f32[392,128]{1,0:T(8,128)S(1)}, f32[392,128]{1,0:T(8,128)S(1)}, u32[]{:S(2)}, u32[]{:S(2)}) collective-permute-start(f32[392,128]{1,0:T(8,128)S(1)} %pack.1.mine.own), channel_id=1, source_target_pairs={{0,1},{1,0},{2,3},{3,2},{4,5},{5,4},{6,7},{7,6},{8,9},{9,8},{10,11... | collective-permute-start | bytes 602120 | tf_op jit(solution)/shard_map/ppermute | solution.py:385
  9.2 0.0 collective-permute-done
  9.2 2.4 %collective-permute-done.1 = f32[2,32,128]{2,1,0:T(8,128)S(1)} collective-permute-done((f32[2,32,128]{2,1,0:T(8,128)S(1)}, f32[2,32,128]{2,1,0:T(8,128)S(1)}, u32[]{:S(2)}, u32[]{:S(2)}) %collective-permute-start.1) | collective-permute-done | bytes 32800 | tf_op jit(solution)/shard_map/ppermute | solution.py:385
  11.6 0.0 collective-permute-done.2
  11.6 0.0 copy-start.3
  11.6 2.5 %collective-permute-start.3 = (f32[2,128,128]{2,1,0:T(8,128)S(1)}, f32[2,128,128]{2,1,0:T(8,128)S(1)}, u32[]{:S(2)}, u32[]{:S(2)}) collective-permute-start(f32[2,128,128]{2,1,0:T(8,128)S(1)} %pad_maximum_fusion.own_ref), channel_id=1, source_target_pairs={{0,5},{1,4},{2,7},{3,6},{4,1},{5,0},{6,3},{7,2},{8,13},{9,12},{10,... | collective-permute-start | bytes 393224 | tf_op jit(solution)/shard_map/ppermute | solution.py:385
  14.1 0.5 %collective-permute-start.4 = (f32[2,128,128]{2,1,0:T(8,128)S(1)}, f32[2,128,128]{2,1,0:T(8,128)S(1)}, u32[]{:S(2)}, u32[]{:S(2)}) collective-permute-start(f32[2,128,128]{2,1,0:T(8,128)S(1)} %pad_maximum_fusion.own_ref), channel_id=1, source_target_pairs={{0,4},{1,5},{2,6},{3,7},{4,0},{5,1},{6,2},{7,3},{8,12},{9,13},{10,... | collective-permute-start | bytes 393224 | tf_op jit(solution)/shard_map/ppermute | solution.py:385
  14.6 0.5 %collective-permute-start.5 = (f32[2,128,128]{2,1,0:T(8,128)S(1)}, f32[2,128,128]{2,1,0:T(8,128)S(1)}, u32[]{:S(2)}, u32[]{:S(2)}) collective-permute-start(f32[2,128,128]{2,1,0:T(8,128)S(1)} %pad_maximum_fusion.own_ref), channel_id=1, source_target_pairs={{0,1},{1,0},{2,3},{3,2},{4,5},{5,4},{6,7},{7,6},{8,9},{9,8},{10,11... | collective-permute-start | bytes 393224 | tf_op jit(solution)/shard_map/ppermute | solution.py:385
  15.2 0.0 collective-permute-start.7
  15.2 0.0 collective-permute-done.6.other
  15.2 0.2 prepare.1
  15.4 3.5 %collective-permute-done.3 = f32[2,128,128]{2,1,0:T(8,128)S(1)} collective-permute-done((f32[2,128,128]{2,1,0:T(8,128)S(1)}, f32[2,128,128]{2,1,0:T(8,128)S(1)}, u32[]{:S(2)}, u32[]{:S(2)}) %collective-permute-start.3) | collective-permute-done | bytes 131104 | tf_op jit(solution)/shard_map/ppermute | solution.py:385
  18.9 1.0 %collective-permute-done.4 = f32[2,128,128]{2,1,0:T(8,128)S(1)} collective-permute-done((f32[2,128,128]{2,1,0:T(8,128)S(1)}, f32[2,128,128]{2,1,0:T(8,128)S(1)}, u32[]{:S(2)}, u32[]{:S(2)}) %collective-permute-start.4) | collective-permute-done | bytes 131104 | tf_op jit(solution)/shard_map/ppermute | solution.py:385
  19.8 0.0 collective-permute-done.5
  19.8 0.0 collective-permute-done.7.far_a
  19.9 0.1 collective-permute-start.8
  20.0 1.0 %project.1 = (bf16[512,384]{1,0:T(8,128)(2,1)S(1)}, f32[512,128]{1,0:T(8,128)S(1)}, f32[512,128]{1,0:T(8,128)S(1)}, f32[512,128]{1,0:T(8,128)S(1)}, f32[512,128]...) custom-call(f32[2,128,128]{2,1,0:T(8,128)S(1)} %pad_maximum_fusion.o, ...), custom_call_target="tpu_custom_call" | custom-call | flops 1073741824 | bytes 1024 | tf_op jit(solution)/shard_map/project/pallas_call | solution.py:365
  21.0 0.7 %collective-permute-done.8.far_b = f32[2,384,128]{2,1,0:T(8,128)S(1)} collective-permute-done((f32[2,384,128]{2,1,0:T(8,128)S(1)}, f32[2,384,128]{2,1,0:T(8,128)S(1)}, u32[]{:S(2)}, u32[]{:S(2)}) %collective-permute-start.8) | collective-permute-done | bytes 393248 | tf_op jit(solution)/shard_map/ppermute | solution.py:385
  21.7 7.7 %rest.1 = (f32[64,64]{1,0:T(8,128)}, f32[64,64]{1,0:T(8,128)}, f32[1,64]{1,0:T(1,128)}, f32[1,64]{1,0:T(1,128)}, f32[4,64,128]{2,1,0:T(8,128)}, /*index=5*/f32[64,128]{1,0:T(8,128)}, f32[64,128]{1,0:T(8,128)}) custom-call(f32[2,128,128]{2,1,0:T(8,128)S(1)} %collective-permute-done.7.far_a, f32[2,384,128]{2,1,0:T(8,128)S(1)} %collective-permute-done.8.far_b, ...), custom_call_target="tpu_custom_call" | custom-call | flops 8589934592 | bytes 1024 | tf_op jit(solution)/shard_map/rest/pallas_call | solution.py:365
  (13 shorter events, 0.1 us)
Async XLA Ops:
  0.6 0.8 %copy-start.4 = (f32[64,2,32]{0,2,1:T(8,128)S(1)}, f32[64,2,32]{0,2,1:T(8,128)}, u32[]{:S(2)}) copy-start(f32[64,2,32]{0,2,1:T(8,128)} %param.13) | copy-start | bytes 49156
  1.5 5.9 %copy-start = (f32[4,128,64]{1,2,0:T(8,128)S(1)}, f32[4,128,64]{1,2,0:T(8,128)}, u32[]{:S(2)}) copy-start(f32[4,128,64]{1,2,0:T(8,128)} %param.10) | copy-start | bytes 393220
  1.6 5.8 %copy-start.1 = (f32[128,64]{0,1:T(8,128)S(1)}, f32[128,64]{0,1:T(8,128)}, u32[]{:S(2)}) copy-start(f32[128,64]{0,1:T(8,128)} %param.11) | copy-start | bytes 98308
  1.6 5.9 %copy-start.2 = (f32[64,128]{1,0:T(8,128)S(1)}, f32[64,128]{1,0:T(8,128)}, u32[]{:S(2)}) copy-start(f32[64,128]{1,0:T(8,128)} %wo.1) | copy-start | bytes 98308
  1.7 5.8 %copy-start.5 = (f32[64]{0:T(128)S(1)}, f32[64]{0:T(128)}, u32[]{:S(2)}) copy-start(f32[64]{0:T(128)} %param.9) | copy-start | bytes 772
  1.7 7.5 %collective-permute-start = (f32[2,32,128]{2,1,0:T(8,128)S(1)}, f32[2,32,128]{2,1,0:T(8,128)S(1)}, u32[]{:S(2)}, u32[]{:S(2)}) collective-permute-start(f32[2,32,128]{2,1,0:T(8,128)S(1)} %maximum_select_fusion), channel_id=1, source_target_pairs={{0,24},{1,25},{2,26},{3,27},{4,28},{5,29},{6,30},{7,31},{8,16},{9,... | collective-permute-start | bytes 98312 | tf_op jit(solution)/shard_map/ppermute | solution.py:385
  6.8 4.8 %collective-permute-start.1 = (f32[2,32,128]{2,1,0:T(8,128)S(1)}, f32[2,32,128]{2,1,0:T(8,128)S(1)}, u32[]{:S(2)}, u32[]{:S(2)}) collective-permute-start(f32[2,32,128]{2,1,0:T(8,128)S(1)} %maximum_select_fusion), channel_id=1, source_target_pairs={{0,16},{1,17},{2,18},{3,19},{4,20},{5,21},{6,22},{7,23},{8,24},{9,... | collective-permute-start | bytes 98312 | tf_op jit(solution)/shard_map/ppermute | solution.py:385
  6.8 4.8 %collective-permute-start.2 = (f32[2,32,128]{2,1,0:T(8,128)S(1)}, f32[2,32,128]{2,1,0:T(8,128)S(1)}, u32[]{:S(2)}, u32[]{:S(2)}) collective-permute-start(f32[2,32,128]{2,1,0:T(8,128)S(1)} %maximum_select_fusion), channel_id=1, source_target_pairs={{0,8},{1,9},{2,10},{3,11},{4,12},{5,13},{6,14},{7,15},{8,0},{9,1},... | collective-permute-start | bytes 98312 | tf_op jit(solution)/shard_map/ppermute | solution.py:385
  7.5 7.7 %collective-permute-start.6 = (f32[392,128]{1,0:T(8,128)S(1)}, f32[392,128]{1,0:T(8,128)S(1)}, u32[]{:S(2)}, u32[]{:S(2)}) collective-permute-start(f32[392,128]{1,0:T(8,128)S(1)} %pack.1.mine.own), channel_id=1, source_target_pairs={{0,1},{1,0},{2,3},{3,2},{4,5},{5,4},{6,7},{7,6},{8,9},{9,8},{10,11... | collective-permute-start | bytes 602120 | tf_op jit(solution)/shard_map/ppermute | solution.py:385
  11.6 3.6 %copy-start.3 = (f32[128]{0:T(128)S(1)}, f32[128]{0:T(128)}, u32[]{:S(2)}) copy-start(f32[128]{0:T(128)} %param.8) | copy-start | bytes 1540
  11.6 7.3 %collective-permute-start.3 = (f32[2,128,128]{2,1,0:T(8,128)S(1)}, f32[2,128,128]{2,1,0:T(8,128)S(1)}, u32[]{:S(2)}, u32[]{:S(2)}) collective-permute-start(f32[2,128,128]{2,1,0:T(8,128)S(1)} %pad_maximum_fusion.own_ref), channel_id=1, source_target_pairs={{0,5},{1,4},{2,7},{3,6},{4,1},{5,0},{6,3},{7,2},{8,13},{9,12},{10,... | collective-permute-start | bytes 393224 | tf_op jit(solution)/shard_map/ppermute | solution.py:385
  14.1 5.7 %collective-permute-start.4 = (f32[2,128,128]{2,1,0:T(8,128)S(1)}, f32[2,128,128]{2,1,0:T(8,128)S(1)}, u32[]{:S(2)}, u32[]{:S(2)}) collective-permute-start(f32[2,128,128]{2,1,0:T(8,128)S(1)} %pad_maximum_fusion.own_ref), channel_id=1, source_target_pairs={{0,4},{1,5},{2,6},{3,7},{4,0},{5,1},{6,2},{7,3},{8,12},{9,13},{10,... | collective-permute-start | bytes 393224 | tf_op jit(solution)/shard_map/ppermute | solution.py:385
  14.6 5.2 %collective-permute-start.5 = (f32[2,128,128]{2,1,0:T(8,128)S(1)}, f32[2,128,128]{2,1,0:T(8,128)S(1)}, u32[]{:S(2)}, u32[]{:S(2)}) collective-permute-start(f32[2,128,128]{2,1,0:T(8,128)S(1)} %pad_maximum_fusion.own_ref), channel_id=1, source_target_pairs={{0,1},{1,0},{2,3},{3,2},{4,5},{5,4},{6,7},{7,6},{8,9},{9,8},{10,11... | collective-permute-start | bytes 393224 | tf_op jit(solution)/shard_map/ppermute | solution.py:385
  15.2 4.7 %collective-permute-start.7 = (f32[2,128,128]{2,1,0:T(8,128)S(1)}, f32[2,128,128]{2,1,0:T(8,128)S(1)}, u32[]{:S(2)}, u32[]{:S(2)}) collective-permute-start(f32[2,128,128]{2,1,0:T(8,128)S(1)} %pad_maximum_fusion.own_ref), channel_id=1, source_target_pairs={{0,2},{1,3},{2,0},{3,1},{4,6},{5,7},{6,4},{7,5},{8,10},{9,11},{10,... | collective-permute-start | bytes 393224 | tf_op jit(solution)/shard_map/ppermute | solution.py:385
  19.9 1.8 %collective-permute-start.8 = (f32[2,384,128]{2,1,0:T(8,128)S(1)}, f32[2,384,128]{2,1,0:T(8,128)S(1)}, u32[]{:S(2)}, u32[]{:S(2)}) collective-permute-start(f32[2,384,128]{2,1,0:T(8,128)S(1)} %constant_dynamic-update-slice_fusion.rest_ref), channel_id=1, source_target_pairs={{0,2},{1,3},{2,0},{3,1},{4,6},{5,7},{6,4},{7,5},{8,10},{9,11},{10,... | collective-permute-start | bytes 1179656 | tf_op jit(solution)/shard_map/ppermute | solution.py:385

commit v8 on v7

--- a/solution.py
+++ b/solution.py
@@ -127,7 +127,7 @@
     return centred * rstd, rstd
 
 
-def cells_from(k, own_ref, rest_ref, blk):
+def cells_from(k, own_ref, cross_ref, rest_ref, blk):
     half = blk // 2
     across = own_ref.shape[1]
     low = (lax.broadcasted_iota(jnp.int32, (half, LANES), 1) < LANES // 2) == (lax.axis_index("chan") == 0)
@@ -138,9 +138,9 @@
             return rest_ref[k, line * across + at : line * across + at + half, :]
 
         if t * half < across:
-            own, other = own_ref[k, at : at + half, :], rest(2)
+            own, other = own_ref[k, at : at + half, :], rest(1)
         else:
-            own, other = rest(1), rest(0)
+            own, other = rest(0), cross_ref[k, at : at + half, :]
         yield jnp.where(low, own, other)
         yield pltpu.roll(jnp.where(low, other, own), LANES // 2, 1)
 
@@ -189,13 +189,13 @@
     gain_out[:, s:] = other[6 * s : 6 * s + 1, :s]
 
 
-def project_kernel(blk, own_ref, rest_ref, wdh, z, left, s1, right, s3, gate, zown, rown, ct, proj):
+def project_kernel(blk, own_ref, cross_ref, rest_ref, wdh, z, left, s1, right, s3, gate, zown, rown, ct, proj):
     c = LANES
     half = blk // 2
     if ct is not None:
-        for k, cells in enumerate(cells_from(1, own_ref, rest_ref, blk)):
+        for k, cells in enumerate(cells_from(1, own_ref, cross_ref, rest_ref, blk)):
             ct[k * half : (k + 1) * half, :] = cells
-    for k, cells in enumerate(cells_from(0, own_ref, rest_ref, blk)):
+    for k, cells in enumerate(cells_from(0, own_ref, cross_ref, rest_ref, blk)):
         at = slice(k * half, (k + 1) * half)
         zhat, rstd = norm_lanes(cells)
         put_split(z, at, zhat)
@@ -258,7 +258,7 @@
 
 
 def gradient_kernel(
-    n, ct_n, far_a, far_b, left, right, z_n, s1_n, right_n, s3_n, gate_n, z_f, s1_f, right_f, s3_f, gate_f, zown, rown,
+    n, ct_n, far_a, far_c, far_b, left, right, z_n, s1_n, right_n, s3_n, gate_n, z_f, s1_f, right_f, s3_f, gate_f, zown, rown,
     xhat, rstds, xs, mixed, gain_ref, out_gain_ref, own, other, wnh, wnl, wqh,
     up_ref, dp_ref, dig_ref, dog_ref, de_ref, dg_ref, do_ref, ms, dh, dl, upd, hidden, dtri, d_left, d_right, grads,
 ):
@@ -270,7 +270,7 @@
     half = blk // 2
     part = n * n // 2
     near = (ct_n[at, :] for at in chunks(part, half))
-    sides = ((near, gate_n), (cells_from(1, far_a, far_b, blk), gate_f))
+    sides = ((near, gate_n), (cells_from(1, far_a, far_c, far_b, blk), gate_f))
 
     for k, (cells, gate) in enumerate(sides):
         for b, ct in enumerate(cells):
@@ -343,18 +343,18 @@
 
 
 def rest_kernel(
-    n, blk, far_a, far_b, z_n, left_n, s1_n, right_n, s3_n, gate_n, zown, rown, ct_n, gain_ref, out_gain_ref, own,
+    n, blk, far_a, far_c, far_b, z_n, left_n, s1_n, right_n, s3_n, gate_n, zown, rown, ct_n, gain_ref, out_gain_ref, own,
     other, wnh, wnl, wdh, woh, wqh, up_ref, dp_ref, dig_ref, dog_ref, de_ref, dg_ref, do_ref,
     left, right, z_f, s1_f, right_f, s3_f, gate_f, xhat, rstds, xs, mixed, right_t, tri, proj, *scratch,
 ):
     q, upper, part = blk // n, 2 * far_a.shape[1] // blk, n * n // 2
     left[:part, :] = left_n[...]
     left_f = left.at[pl.ds(part, part)]
-    project_kernel(blk, far_a, far_b, wdh, z_f, left_f, s1_f, right_f, s3_f, gate_f, None, None, None, proj)
+    project_kernel(blk, far_a, far_c, far_b, wdh, z_f, left_f, s1_f, right_f, s3_f, gate_f, None, None, None, proj)
     sides = (right_n, right_f)
     triangle_kernel(n, q, upper, left, sides, out_gain_ref, woh, xhat, rstds, xs, mixed, right, right_t, tri)
     gradient_kernel(
-        n, ct_n, far_a, far_b, left, right, z_n, s1_n, right_n, s3_n, gate_n, z_f, s1_f, right_f, s3_f, gate_f, zown, rown,
+        n, ct_n, far_a, far_c, far_b, left, right, z_n, s1_n, right_n, s3_n, gate_n, z_f, s1_f, right_f, s3_f, gate_f, zown, rown,
         xhat, rstds, xs, mixed, gain_ref, out_gain_ref, own, other, wnh, wnl, wqh,
         up_ref, dp_ref, dig_ref, dog_ref, de_ref, dg_ref, do_ref, *scratch,
     )
@@ -412,7 +412,9 @@
         gain, mine, other,
     )
     far_a = swap(held, 2)
-    parts, wdh, far_a = lax.optimization_barrier((parts, wdh, far_a))
+    cross, *parts = parts
+    far_c = swap(cross, 2)
+    cross, parts, wdh, far_a = lax.optimization_barrier((cross, parts, wdh, far_a))
     others = jnp.concatenate(parts, axis=1)
     far_b = swap(others, 2)
 
@@ -420,7 +422,7 @@
     part, own = ((cells // 2, c), F32), ((blk, c), F32)
     half, many = [((cells // 2, 3 * c), BF16)] + [part] * 5, ((cells // 2, 5 * c), F32)
     near = call(
-        functools.partial(project_kernel, blk), "project", half + [own] * 2 + [part], [many], 16, 1 << 30, held, others, wdh
+        functools.partial(project_kernel, blk), "project", half + [own] * 2 + [part], [many], 16, 1 << 30, held, cross, others, wdh
     )
     up, dp, dig, dog, de, dg, do = call(
         functools.partial(rest_kernel, n, blk),
@@ -430,7 +432,7 @@
         + [both, wide, wide, own] + [full] * 4 + [((5 * c, c), F32)],
         32,
         1 << 33,
-        far_a, far_b, *near, gain, out_gain, mine, other, wnh, wnl, wdh, woh, wqh,
+        far_a, far_c, far_b, *near, gain, out_gain, mine, other, wnh, wnl, wdh, woh, wqh,
     )
 
     def pair_of(x):

time: 29.7 us -> 29.7 us (level)
  starting transfers between devices: 11.1 us -> 11.6 us
  waiting for transfers between devices: 7.57 us -> 7.07 us
    ppermute x9 -> x10, starting transfers between devices: 11.1 us -> 11.6 us  [swap(): lax.ppermute(x, ('row', 'chan'), [(i, i ^ bits) for i in range(devices)])]
    ppermute x9 -> x10, waiting for transfers between devices: 7.57 us -> 7.07 us  [swap(): lax.ppermute(x, ('row', 'chan'), [(i, i ^ bits) for i in range(devices)])]
  transfers between devices with their start and end apart: 9 -> 10, of which waited for: 4 -> 4; matrix products, arithmetic and copies ran while one was open for 0% -> 0% of each run, Pallas kernels for 4% -> 4%
where the time goes in v8:
time: 29.7 us; the launch traced here: 29.4 us
  starting transfers between devices  11.6 us (39%)
  Pallas kernels  8.99 us (30%)
  waiting for transfers between devices  7.07 us (24%)
  local copies, waits for them, and re-layouts  0.88 us (3%)
  between operations  0.74 us (2%)
    ppermute x10, starting transfers between devices, swap(): lax.ppermute(x, ('row', 'chan'), [(i, i ^ bits) for i in range(devices)])  11.6 us
    pallas_call x4, Pallas kernels, call(): pl.pallas_call(kernel, out_shape=[jax.ShapeDtypeStruct(shape, dtype) for...  8.99 us
    ppermute x10, waiting for transfers between devices, swap(): lax.ppermute(x, ('row', 'chan'), [(i, i ^ bits) for i in range(devices)])  7.07 us
    squeeze x2, local copies, waits for them, and re-layouts, packed(): return jnp.concatenate([x[0], x[1]], axis=1)[None]  0.75 us
  transfers between devices with their start and end apart: 10, of which 4 were waited for; matrix products, arithmetic and copies ran while one was open for 0% of the time, Pallas kernels for 4%

profile of v8, /device:TPU:0, one launch (start us, length us, event | category | flops | bytes accessed | tf_op | source)
XLA Modules:
  0.0 29.4 jit_solution(5667791041330231367)
XLA Ops:
  0.6 0.0 copy-start.4
  0.6 0.7 %slice_bitcast_fusion.3 = (f32[32,64]{1,0:T(8,128)S(1)}, f32[32,64]{1,0:T(8,128)S(1)}) fusion(f32[2,32,64]{2,1,0:T(8,128)} %bitcast.32), kind=kLoop, calls=%fused_computation.6 | loop fusion | bytes 32768 | tf_op jit(solution)/shard_map/squeeze | solution.py:389
  1.4 0.0 copy-done.4
  1.4 0.1 maximum_bitcast_fusion
  1.5 0.0 copy-start
  1.5 0.1 fusion
  1.6 0.1 maximum_select_fusion
  1.7 5.1 %collective-permute-start = (f32[2,32,128]{2,1,0:T(8,128)S(1)}, f32[2,32,128]{2,1,0:T(8,128)S(1)}, u32[]{:S(2)}, u32[]{:S(2)}) collective-permute-start(f32[2,32,128]{2,1,0:T(8,128)S(1)} %maximum_select_fusion), channel_id=1, source_target_pairs={{0,24},{1,25},{2,26},{3,27},{4,28},{5,29},{6,30},{7,31},{8,16},{9,... | collective-permute-start | bytes 98312 | tf_op jit(solution)/shard_map/ppermute | solution.py:385
  6.8 0.0 collective-permute-start.1
  6.8 0.6 %collective-permute-start.2 = (f32[2,32,128]{2,1,0:T(8,128)S(1)}, f32[2,32,128]{2,1,0:T(8,128)S(1)}, u32[]{:S(2)}, u32[]{:S(2)}) collective-permute-start(f32[2,32,128]{2,1,0:T(8,128)S(1)} %maximum_select_fusion), channel_id=1, source_target_pairs={{0,8},{1,9},{2,10},{3,11},{4,12},{5,13},{6,14},{7,15},{8,0},{9,1},... | collective-permute-start | bytes 98312 | tf_op jit(solution)/shard_map/ppermute | solution.py:385
  7.5 1.7 %collective-permute-start.6 = (f32[392,128]{1,0:T(8,128)S(1)}, f32[392,128]{1,0:T(8,128)S(1)}, u32[]{:S(2)}, u32[]{:S(2)}) collective-permute-start(f32[392,128]{1,0:T(8,128)S(1)} %pack.1.mine.own), channel_id=1, source_target_pairs={{0,1},{1,0},{2,3},{3,2},{4,5},{5,4},{6,7},{7,6},{8,9},{9,8},{10,11... | collective-permute-start | bytes 602120 | tf_op jit(solution)/shard_map/ppermute | solution.py:385
  9.2 0.0 collective-permute-done
  9.2 2.4 %collective-permute-done.1 = f32[2,32,128]{2,1,0:T(8,128)S(1)} collective-permute-done((f32[2,32,128]{2,1,0:T(8,128)S(1)}, f32[2,32,128]{2,1,0:T(8,128)S(1)}, u32[]{:S(2)}, u32[]{:S(2)}) %collective-permute-start.1) | collective-permute-done | bytes 32800 | tf_op jit(solution)/shard_map/ppermute | solution.py:385
  11.6 0.0 collective-permute-done.2
  11.6 0.0 copy-start.3
  11.6 2.5 %collective-permute-start.3 = (f32[2,128,128]{2,1,0:T(8,128)S(1)}, f32[2,128,128]{2,1,0:T(8,128)S(1)}, u32[]{:S(2)}, u32[]{:S(2)}) collective-permute-start(f32[2,128,128]{2,1,0:T(8,128)S(1)} %pad_maximum_fusion.own_ref), channel_id=1, source_target_pairs={{0,5},{1,4},{2,7},{3,6},{4,1},{5,0},{6,3},{7,2},{8,13},{9,12},{10,... | collective-permute-start | bytes 393224 | tf_op jit(solution)/shard_map/ppermute | solution.py:385
  14.1 0.5 %collective-permute-start.4 = (f32[2,128,128]{2,1,0:T(8,128)S(1)}, f32[2,128,128]{2,1,0:T(8,128)S(1)}, u32[]{:S(2)}, u32[]{:S(2)}) collective-permute-start(f32[2,128,128]{2,1,0:T(8,128)S(1)} %pad_maximum_fusion.own_ref), channel_id=1, source_target_pairs={{0,4},{1,5},{2,6},{3,7},{4,0},{5,1},{6,2},{7,3},{8,12},{9,13},{10,... | collective-permute-start | bytes 393224 | tf_op jit(solution)/shard_map/ppermute | solution.py:385
  14.6 0.5 %collective-permute-start.5 = (f32[2,128,128]{2,1,0:T(8,128)S(1)}, f32[2,128,128]{2,1,0:T(8,128)S(1)}, u32[]{:S(2)}, u32[]{:S(2)}) collective-permute-start(f32[2,128,128]{2,1,0:T(8,128)S(1)} %pad_maximum_fusion.own_ref), channel_id=1, source_target_pairs={{0,1},{1,0},{2,3},{3,2},{4,5},{5,4},{6,7},{7,6},{8,9},{9,8},{10,11... | collective-permute-start | bytes 393224 | tf_op jit(solution)/shard_map/ppermute | solution.py:385
  15.2 0.0 collective-permute-start.7
  15.2 0.0 collective-permute-done.6.other
  15.2 0.0 copy-done.3
  15.2 0.2 prepare.1
  15.4 3.5 %collective-permute-done.3.cross_ref = f32[2,128,128]{2,1,0:T(8,128)S(1)} collective-permute-done((f32[2,128,128]{2,1,0:T(8,128)S(1)}, f32[2,128,128]{2,1,0:T(8,128)S(1)}, u32[]{:S(2)}, u32[]{:S(2)}) %collective-permute-start.3) | collective-permute-done | bytes 131104 | tf_op jit(solution)/shard_map/ppermute | solution.py:385
  18.9 1.0 %collective-permute-done.4 = f32[2,128,128]{2,1,0:T(8,128)S(1)} collective-permute-done((f32[2,128,128]{2,1,0:T(8,128)S(1)}, f32[2,128,128]{2,1,0:T(8,128)S(1)}, u32[]{:S(2)}, u32[]{:S(2)}) %collective-permute-start.4) | collective-permute-done | bytes 131104 | tf_op jit(solution)/shard_map/ppermute | solution.py:385
  19.8 0.0 collective-permute-done.5
  19.9 0.0 collective-permute-done.7.far_a
  19.9 0.1 collective-permute-start.9
  20.0 0.5 %collective-permute-start.8 = (f32[2,128,128]{2,1,0:T(8,128)S(1)}, f32[2,128,128]{2,1,0:T(8,128)S(1)}, u32[]{:S(2)}, u32[]{:S(2)}) collective-permute-start(f32[2,128,128]{2,1,0:T(8,128)S(1)} %collective-permute-done.3.cross_ref), channel_id=1, source_target_pairs={{0,2},{1,3},{2,0},{3,1},{4,6},{5,7},{6,4},{7,5},{8,10},{9,11},{10,... | collective-permute-start | bytes 393224 | tf_op jit(solution)/shard_map/ppermute | solution.py:385
  20.5 1.0 %project.1 = (bf16[512,384]{1,0:T(8,128)(2,1)S(1)}, f32[512,128]{1,0:T(8,128)S(1)}, f32[512,128]{1,0:T(8,128)S(1)}, f32[512,128]{1,0:T(8,128)S(1)}, f32[512,128]...) custom-call(f32[2,128,128]{2,1,0:T(8,128)S(1)} %pad_maximum_fusion.o, ...), custom_call_target="tpu_custom_call" | custom-call | flops 1073741824 | bytes 1024 | tf_op jit(solution)/shard_map/project/pallas_call | solution.py:365
  21.5 0.2 collective-permute-done.8.far_c
  21.7 0.0 collective-permute-done.9.far_b
  21.7 7.7 %rest.1 = (f32[64,64]{1,0:T(8,128)}, f32[64,64]{1,0:T(8,128)}, f32[1,64]{1,0:T(1,128)}, f32[1,64]{1,0:T(1,128)}, f32[4,64,128]{2,1,0:T(8,128)}, /*index=5*/f32[64,128]{1,0:T(8,128)}, f32[64,128]{1,0:T(8,128)}) custom-call(f32[2,128,128]{2,1,0:T(8,128)S(1)} %collective-permute-done.7.far_a, f32[2,128,128]{2,1,0:T(8,128)S(1)} %collective-permute-done.8.far_c, ...), custom_call_target="tpu_custom_call" | custom-call | flops 8589934592 | bytes 1024 | tf_op jit(solution)/shard_map/rest/pallas_call | solution.py:365
  (14 shorter events, 0.1 us)
Async XLA Ops:
  0.6 0.8 %copy-start.4 = (f32[64,2,32]{0,2,1:T(8,128)S(1)}, f32[64,2,32]{0,2,1:T(8,128)}, u32[]{:S(2)}) copy-start(f32[64,2,32]{0,2,1:T(8,128)} %param.13) | copy-start | bytes 49156
  1.5 5.9 %copy-start = (f32[4,128,64]{1,2,0:T(8,128)S(1)}, f32[4,128,64]{1,2,0:T(8,128)}, u32[]{:S(2)}) copy-start(f32[4,128,64]{1,2,0:T(8,128)} %param.10) | copy-start | bytes 393220
  1.6 5.8 %copy-start.1 = (f32[128,64]{0,1:T(8,128)S(1)}, f32[128,64]{0,1:T(8,128)}, u32[]{:S(2)}) copy-start(f32[128,64]{0,1:T(8,128)} %param.11) | copy-start | bytes 98308
  1.6 5.9 %copy-start.2 = (f32[64,128]{1,0:T(8,128)S(1)}, f32[64,128]{1,0:T(8,128)}, u32[]{:S(2)}) copy-start(f32[64,128]{1,0:T(8,128)} %wo.1) | copy-start | bytes 98308
  1.7 5.8 %copy-start.5 = (f32[64]{0:T(128)S(1)}, f32[64]{0:T(128)}, u32[]{:S(2)}) copy-start(f32[64]{0:T(128)} %param.9) | copy-start | bytes 772
  1.7 7.5 %collective-permute-start = (f32[2,32,128]{2,1,0:T(8,128)S(1)}, f32[2,32,128]{2,1,0:T(8,128)S(1)}, u32[]{:S(2)}, u32[]{:S(2)}) collective-permute-start(f32[2,32,128]{2,1,0:T(8,128)S(1)} %maximum_select_fusion), channel_id=1, source_target_pairs={{0,24},{1,25},{2,26},{3,27},{4,28},{5,29},{6,30},{7,31},{8,16},{9,... | collective-permute-start | bytes 98312 | tf_op jit(solution)/shard_map/ppermute | solution.py:385
  6.8 4.8 %collective-permute-start.1 = (f32[2,32,128]{2,1,0:T(8,128)S(1)}, f32[2,32,128]{2,1,0:T(8,128)S(1)}, u32[]{:S(2)}, u32[]{:S(2)}) collective-permute-start(f32[2,32,128]{2,1,0:T(8,128)S(1)} %maximum_select_fusion), channel_id=1, source_target_pairs={{0,16},{1,17},{2,18},{3,19},{4,20},{5,21},{6,22},{7,23},{8,24},{9,... | collective-permute-start | bytes 98312 | tf_op jit(solution)/shard_map/ppermute | solution.py:385
  6.8 4.8 %collective-permute-start.2 = (f32[2,32,128]{2,1,0:T(8,128)S(1)}, f32[2,32,128]{2,1,0:T(8,128)S(1)}, u32[]{:S(2)}, u32[]{:S(2)}) collective-permute-start(f32[2,32,128]{2,1,0:T(8,128)S(1)} %maximum_select_fusion), channel_id=1, source_target_pairs={{0,8},{1,9},{2,10},{3,11},{4,12},{5,13},{6,14},{7,15},{8,0},{9,1},... | collective-permute-start | bytes 98312 | tf_op jit(solution)/shard_map/ppermute | solution.py:385
  7.5 7.7 %collective-permute-start.6 = (f32[392,128]{1,0:T(8,128)S(1)}, f32[392,128]{1,0:T(8,128)S(1)}, u32[]{:S(2)}, u32[]{:S(2)}) collective-permute-start(f32[392,128]{1,0:T(8,128)S(1)} %pack.1.mine.own), channel_id=1, source_target_pairs={{0,1},{1,0},{2,3},{3,2},{4,5},{5,4},{6,7},{7,6},{8,9},{9,8},{10,11... | collective-permute-start | bytes 602120 | tf_op jit(solution)/shard_map/ppermute | solution.py:385
  11.6 3.6 %copy-start.3 = (f32[128]{0:T(128)S(1)}, f32[128]{0:T(128)}, u32[]{:S(2)}) copy-start(f32[128]{0:T(128)} %param.8) | copy-start | bytes 1540
  11.6 7.3 %collective-permute-start.3 = (f32[2,128,128]{2,1,0:T(8,128)S(1)}, f32[2,128,128]{2,1,0:T(8,128)S(1)}, u32[]{:S(2)}, u32[]{:S(2)}) collective-permute-start(f32[2,128,128]{2,1,0:T(8,128)S(1)} %pad_maximum_fusion.own_ref), channel_id=1, source_target_pairs={{0,5},{1,4},{2,7},{3,6},{4,1},{5,0},{6,3},{7,2},{8,13},{9,12},{10,... | collective-permute-start | bytes 393224 | tf_op jit(solution)/shard_map/ppermute | solution.py:385
  14.1 5.7 %collective-permute-start.4 = (f32[2,128,128]{2,1,0:T(8,128)S(1)}, f32[2,128,128]{2,1,0:T(8,128)S(1)}, u32[]{:S(2)}, u32[]{:S(2)}) collective-permute-start(f32[2,128,128]{2,1,0:T(8,128)S(1)} %pad_maximum_fusion.own_ref), channel_id=1, source_target_pairs={{0,4},{1,5},{2,6},{3,7},{4,0},{5,1},{6,2},{7,3},{8,12},{9,13},{10,... | collective-permute-start | bytes 393224 | tf_op jit(solution)/shard_map/ppermute | solution.py:385
  14.6 5.2 %collective-permute-start.5 = (f32[2,128,128]{2,1,0:T(8,128)S(1)}, f32[2,128,128]{2,1,0:T(8,128)S(1)}, u32[]{:S(2)}, u32[]{:S(2)}) collective-permute-start(f32[2,128,128]{2,1,0:T(8,128)S(1)} %pad_maximum_fusion.own_ref), channel_id=1, source_target_pairs={{0,1},{1,0},{2,3},{3,2},{4,5},{5,4},{6,7},{7,6},{8,9},{9,8},{10,11... | collective-permute-start | bytes 393224 | tf_op jit(solution)/shard_map/ppermute | solution.py:385
  15.2 4.7 %collective-permute-start.7 = (f32[2,128,128]{2,1,0:T(8,128)S(1)}, f32[2,128,128]{2,1,0:T(8,128)S(1)}, u32[]{:S(2)}, u32[]{:S(2)}) collective-permute-start(f32[2,128,128]{2,1,0:T(8,128)S(1)} %pad_maximum_fusion.own_ref), channel_id=1, source_target_pairs={{0,2},{1,3},{2,0},{3,1},{4,6},{5,7},{6,4},{7,5},{8,10},{9,11},{10,... | collective-permute-start | bytes 393224 | tf_op jit(solution)/shard_map/ppermute | solution.py:385
  19.9 1.8 %collective-permute-start.9 = (f32[2,256,128]{2,1,0:T(8,128)S(1)}, f32[2,256,128]{2,1,0:T(8,128)S(1)}, u32[]{:S(2)}, u32[]{:S(2)}) collective-permute-start(f32[2,256,128]{2,1,0:T(8,128)S(1)} %constant_dynamic-update-slice_fusion.rest_ref), channel_id=1, source_target_pairs={{0,2},{1,3},{2,0},{3,1},{4,6},{5,7},{6,4},{7,5},{8,10},{9,11},{10,... | collective-permute-start | bytes 786440 | tf_op jit(solution)/shard_map/ppermute | solution.py:385
  20.0 1.7 %collective-permute-start.8 = (f32[2,128,128]{2,1,0:T(8,128)S(1)}, f32[2,128,128]{2,1,0:T(8,128)S(1)}, u32[]{:S(2)}, u32[]{:S(2)}) collective-permute-start(f32[2,128,128]{2,1,0:T(8,128)S(1)} %collective-permute-done.3.cross_ref), channel_id=1, source_target_pairs={{0,2},{1,3},{2,0},{3,1},{4,6},{5,7},{6,4},{7,5},{8,10},{9,11},{10,... | collective-permute-start | bytes 393224 | tf_op jit(solution)/shard_map/ppermute | solution.py:385
